TPU v7x, 32 devices: a whole 2x2x4 slice. The times are simulated.
32 devices in a mesh: rep: 8 (over y, x, core), seq: 4 (over z).
Axes of the slice: x: 2, y: 2, z: 4, core: 2. Of those that a mesh axis runs over, the one named last changes fastest.
Arguments:
- block_input: bfloat16 [8192, 1536], P(('rep', 'seq')), may hold values from -6 to 6
- cotangent: bfloat16 [8192, 1536], P(('rep', 'seq')), may hold values from -6 to 6
- lengths: int32 [8], P('rep'), may hold values from 256 to 1024, as said below
- offsets: int32 [8], P('rep'), may hold values from 0 to 768, as said below
- norm_gains: bfloat16 [2, 2, 1536], P(None, None, 'seq'), may hold values from 0.5 to 1.5
- branch_proj: bfloat16 [2, 1536, 2048], P(None, 'seq'), may hold values from -0.15625 to 0.15625
- stream_proj: bfloat16 [2, 1536, 2048], P(None, 'seq'), may hold values from -0.15625 to 0.15625
- conv_kernel: bfloat16 [2, 4, 2048], P(None, None, 'seq'), may hold values from -3 to 3
- conv_bias: bfloat16 [2, 2048], P(None, 'seq'), may hold values from -2 to 2
- rate_proj: bfloat16 [2, 2048, 256], P(None, 'seq'), may hold values from -0.375 to 0.375
- admit_proj: bfloat16 [2, 2048, 256], P(None, 'seq'), may hold values from -0.375 to 0.375
- gate_bias: bfloat16 [2, 2, 2048], P(None, None, 'seq'), may hold values from -3 to 3
- decay_logit: bfloat16 [2, 2048], P(None, 'seq'), may hold values from 2.1875 to 9.1875
- out_proj: bfloat16 [2, 2048, 1536], P(None, 'seq'), may hold values from -0.25 to 0.25
- mlp_gate: bfloat16 [2, 1536, 4608], P(None, 'seq'), may hold values from -0.15625 to 0.15625
- mlp_up: bfloat16 [2, 1536, 4608], P(None, 'seq'), may hold values from -0.15625 to 0.15625
- mlp_down: bfloat16 [2, 4608, 1536], P(None, 'seq'), may hold values from -0.125 to 0.125
Outputs:
- block_output: bfloat16 [8192, 1536], P(('rep', 'seq'))
- input_grad: float32 [8192, 1536], P(('rep', 'seq'))
- grad_norm_gains: float32 [2, 2, 1536], P(None, None, ('rep', 'seq'))
- grad_branch_proj: float32 [2, 1536, 2048], P(None, ('rep', 'seq'))
- grad_stream_proj: float32 [2, 1536, 2048], P(None, ('rep', 'seq'))
- grad_conv_kernel: float32 [2, 4, 2048], P(None, None, ('rep', 'seq'))
- grad_conv_bias: float32 [2, 2048], P(None, ('rep', 'seq'))
- grad_rate_proj: float32 [2, 2048, 256], P(None, ('rep', 'seq'))
- grad_admit_proj: float32 [2, 2048, 256], P(None, ('rep', 'seq'))
- grad_gate_bias: float32 [2, 2, 2048], P(None, None, ('rep', 'seq'))
- grad_decay_logit: float32 [2, 2048], P(None, ('rep', 'seq'))
- grad_out_proj: float32 [2, 2048, 1536], P(None, ('rep', 'seq'))
- grad_mlp_gate: float32 [2, 1536, 4608], P(None, ('rep', 'seq'))
- grad_mlp_up: float32 [2, 1536, 4608], P(None, ('rep', 'seq'))
- grad_mlp_down: float32 [2, 4608, 1536], P(None, ('rep', 'seq'))
Inputs may be any that keep to these rules, and one draw needn't show every extreme that they name: `lengths`: some group's sequence fills its whole slot of 1024 positions and some group's has 256 positions. offsets[g] + lengths[g] <= 1024; some group's sequence ends at the slot's last position.
All inputs are finite; a program needn't handle non-finite values.
Results may differ from a plain program's by a relative error of at most 0.015.
Values may be sent and summed in bfloat16 or wider, within the bound.
A program may use at most 512 MiB of HBM per device.

v0:
```python
from functools import partial

import jax
import jax.numpy as jnp
from jax import lax
from jax.sharding import PartitionSpec as P

CONV = 4
LAYERS = 2


EPSILON = 1e-06


def passed_along(value, axis, steps):
    count = lax.axis_size(axis)
    first, last = (max(0, -steps), min(count, count - steps))
    return lax.ppermute(value, axis, [(source, source + steps) for source in range(first, last)])


def prefix(part, axis, combine, identity, reverse):
    count = lax.axis_size(axis)
    place = lax.axis_index(axis)
    ahead = count - 1 - place if reverse else place
    gathered = jax.tree.map(lambda a: lax.all_gather(a, axis), part)
    state = jax.tree.map(lambda a, e: jnp.zeros_like(a) + jnp.asarray(e, a.dtype), part, identity)

    def one(step, state):
        source = count - 1 - step if reverse else step
        return combine(
            state, jax.tree.map(lambda a: lax.dynamic_index_in_dim(a, source, 0, False), gathered)
        )

    return lax.fori_loop(0, ahead, one, state)


def rms_scale(values, scale_vec):
    return (
        values * lax.rsqrt(jnp.mean(values * values, axis=-1, keepdims=True) + EPSILON) * scale_vec
    )


def gate_terms(pre_rate, pre_admit, conv_value, decay_logit, gate_bias, restart):
    rate_gate = jax.nn.sigmoid(pre_rate + gate_bias[0])
    admit_gate = jax.nn.sigmoid(pre_admit + gate_bias[1])
    log_retain = -8.0 * rate_gate * jax.nn.softplus(-decay_logit)
    retain = jnp.where(restart, 0.0, jnp.exp(log_retain))
    input_scale = jnp.where(restart, 1.0, jnp.sqrt(-jnp.expm1(2.0 * log_retain)))
    return (retain, input_scale * admit_gate * conv_value)


def glu_product(gate_in, value_in):
    return jax.nn.gelu(gate_in, approximate=True) * value_in


def chain(earlier, later):
    return (earlier[0] * later[0], later[0] * earlier[1] + later[1])


def blockwise(values, weight):
    head_width = weight.shape[1]
    head_count = weight.shape[0] // head_width
    result = jnp.einsum(
        "thi,hij->thj",
        values.reshape(values.shape[0], head_count, head_width),
        weight.reshape(head_count, head_width, head_width),
        preferred_element_type=jnp.float32,
    )
    return result.reshape(values.shape[0], head_count * head_width)


def block_input_grad(grads, weight):
    head_width = weight.shape[1]
    head_count = weight.shape[0] // head_width
    result = jnp.einsum(
        "thj,hij->thi",
        grads.reshape(grads.shape[0], head_count, head_width),
        weight.reshape(head_count, head_width, head_width),
        preferred_element_type=jnp.float32,
    )
    return result.reshape(grads.shape[0], head_count * head_width)


def block_weight_grad(values, grads, head_width):
    head_count = values.shape[1] // head_width
    result = jnp.einsum(
        "thi,thj->hij",
        values.reshape(values.shape[0], head_count, head_width),
        grads.reshape(grads.shape[0], head_count, head_width),
        preferred_element_type=jnp.float32,
    )
    return result.reshape(head_count * head_width, head_width)


def slot_masks(length, offset, row_count):
    start = lax.axis_index("seq") * row_count
    positions = start + jnp.arange(row_count + 2 * (CONV - 1), dtype=jnp.int32) - (CONV - 1)
    inside = (positions >= offset) & (positions < offset + length)
    core = inside[CONV - 1 : CONV - 1 + row_count]
    restart = (
        (positions[CONV - 1 : CONV - 1 + row_count] == 0)
        | (core != inside[CONV - 2 : CONV - 2 + row_count])
    )[:, None]
    same_fwd = [
        (core == inside[CONV - 1 - back_steps : CONV - 1 - back_steps + row_count]).astype(
            jnp.float32
        )[:, None]
        for back_steps in range(1, CONV)
    ]
    same_back = [
        (inside[CONV - 1 + back_steps : CONV - 1 + back_steps + row_count] == core).astype(
            jnp.float32
        )[:, None]
        for back_steps in range(1, CONV)
    ]
    return (core.astype(jnp.float32)[:, None], restart, same_fwd, same_back)


def fetch(weights, layer_idx):
    return (
        lax.all_gather(weights[0][layer_idx], "seq", axis=1, tiled=True),
        lax.all_gather(weights[1][layer_idx], "seq", axis=0, tiled=True),
        lax.all_gather(weights[2][layer_idx], "seq", axis=0, tiled=True),
        lax.all_gather(weights[3][layer_idx], "seq", axis=1, tiled=True),
        lax.all_gather(weights[4][layer_idx], "seq", axis=0, tiled=True),
        lax.all_gather(weights[5][layer_idx], "seq", axis=0, tiled=True),
        lax.all_gather(weights[6][layer_idx], "seq", axis=0, tiled=True),
        lax.all_gather(weights[7][layer_idx], "seq", axis=1, tiled=True),
        lax.all_gather(weights[8][layer_idx], "seq", axis=0, tiled=True),
        lax.all_gather(weights[9][layer_idx], "seq", axis=0, tiled=True),
        lax.all_gather(weights[10][layer_idx], "seq", axis=0, tiled=True),
        lax.all_gather(weights[11][layer_idx], "seq", axis=0, tiled=True),
        lax.all_gather(weights[12][layer_idx], "seq", axis=0, tiled=True),
    )


def owner_share(summed):
    device_count = lax.axis_size(("rep", "seq"))
    owner = lax.axis_index(("rep", "seq"))
    width = summed.shape[-1] // device_count
    return lax.dynamic_slice_in_dim(summed, owner * width, width, summed.ndim - 1)


def reduce_grads(grads):
    small = lax.psum((grads[0], grads[3], grads[4], grads[7], grads[8]), ("rep", "seq"))
    small = tuple((owner_share(member) for member in small))
    large = (
        lax.psum_scatter(grads[1], ("rep", "seq"), scatter_dimension=0, tiled=True),
        lax.psum_scatter(grads[2], ("rep", "seq"), scatter_dimension=0, tiled=True),
        lax.psum_scatter(grads[5], ("rep", "seq"), scatter_dimension=0, tiled=True),
        lax.psum_scatter(grads[6], ("rep", "seq"), scatter_dimension=0, tiled=True),
        lax.psum_scatter(grads[9], ("rep", "seq"), scatter_dimension=0, tiled=True),
        lax.psum_scatter(grads[10], ("rep", "seq"), scatter_dimension=0, tiled=True),
        lax.psum_scatter(grads[11], ("rep", "seq"), scatter_dimension=0, tiled=True),
        lax.psum_scatter(grads[12], ("rep", "seq"), scatter_dimension=0, tiled=True),
    )
    return (
        small[0],
        large[0],
        large[1],
        small[1],
        small[2],
        large[2],
        large[3],
        small[3],
        small[4],
        large[4],
        large[5],
        large[6],
        large[7],
    )


def layer_forward(residual, params, masks):
    (
        norm_gain,
        branch_proj,
        stream_proj,
        conv_kernel,
        conv_bias,
        rate_proj,
        admit_proj,
        gate_bias,
        decay_logit,
        out_proj,
        mlp_gate,
        mlp_up,
        mlp_down,
    ) = params
    inside, restart, same_fwd, same_back = masks
    row_count = residual.shape[0]
    normed = rms_scale(residual, norm_gain[0].astype(jnp.float32)).astype(jnp.bfloat16)
    branch = jnp.dot(normed, branch_proj, preferred_element_type=jnp.float32)
    stream = jnp.dot(normed, stream_proj, preferred_element_type=jnp.float32)
    before = passed_along(stream[row_count - (CONV - 1) :], "seq", 1)
    widened = jnp.concatenate([before, stream], 0)
    kernel = conv_kernel.astype(jnp.float32)
    mixed = conv_bias.astype(jnp.float32) + kernel[0] * stream
    for back_steps in range(1, CONV):
        lower = CONV - 1 - back_steps
        mixed = (
            mixed
            + kernel[back_steps] * widened[lower : lower + row_count] * same_fwd[back_steps - 1]
        )
    conv_low = mixed.astype(jnp.bfloat16)
    pre_rate = blockwise(conv_low, rate_proj)
    pre_admit = blockwise(conv_low, admit_proj)
    retain, inflow = gate_terms(
        pre_rate,
        pre_admit,
        conv_low.astype(jnp.float32),
        decay_logit.astype(jnp.float32),
        gate_bias.astype(jnp.float32),
        restart,
    )
    running, local_states = lax.associative_scan(chain, (retain, inflow), axis=0)
    carried = prefix(
        (running[row_count - 1], local_states[row_count - 1]),
        "seq",
        chain,
        (jnp.ones_like(inflow[0]), jnp.zeros_like(inflow[0])),
        False,
    )
    carry_in = carried[1]
    states = local_states + running * carry_in
    joined = glu_product(branch, states).astype(jnp.bfloat16)
    middle = residual + jnp.dot(joined, out_proj, preferred_element_type=jnp.float32)
    normed_two = rms_scale(middle, norm_gain[1].astype(jnp.float32)).astype(jnp.bfloat16)
    up_gate = jnp.dot(normed_two, mlp_gate, preferred_element_type=jnp.float32)
    up_value = jnp.dot(normed_two, mlp_up, preferred_element_type=jnp.float32)
    hidden = glu_product(up_gate, up_value).astype(jnp.bfloat16)
    output = middle + jnp.dot(hidden, mlp_down, preferred_element_type=jnp.float32)
    saved = (
        residual,
        normed,
        branch,
        widened,
        conv_low,
        pre_rate,
        pre_admit,
        retain,
        states,
        carry_in,
        joined,
        middle,
        normed_two,
        up_gate,
        up_value,
        hidden,
    )
    return (output, saved)


def layer_backward(upstream, params, saved, masks):
    (
        norm_gain,
        branch_proj,
        stream_proj,
        conv_kernel,
        conv_bias,
        rate_proj,
        admit_proj,
        gate_bias,
        decay_logit,
        out_proj,
        mlp_gate,
        mlp_up,
        mlp_down,
    ) = params
    (
        residual,
        normed,
        branch,
        widened,
        conv_low,
        pre_rate,
        pre_admit,
        retain,
        states,
        carry_in,
        joined,
        middle,
        normed_two,
        up_gate,
        up_value,
        hidden,
    ) = saved
    inside, restart, same_fwd, same_back = masks
    row_count = upstream.shape[0]
    down_low = upstream.astype(jnp.bfloat16)
    grad_mlp_down = jnp.dot(hidden.T, down_low, preferred_element_type=jnp.float32)
    grad_hidden = jnp.dot(down_low, mlp_down.T, preferred_element_type=jnp.float32)
    _, glu_pull = jax.vjp(glu_product, up_gate, up_value)
    grad_gate_part, grad_value_part = glu_pull(grad_hidden)
    grad_up_gate = grad_gate_part.astype(jnp.bfloat16)
    grad_up_value = grad_value_part.astype(jnp.bfloat16)
    grad_mlp_gate = jnp.dot(normed_two.T, grad_up_gate, preferred_element_type=jnp.float32)
    grad_mlp_up = jnp.dot(normed_two.T, grad_up_value, preferred_element_type=jnp.float32)
    grad_normed_two = jnp.dot(
        grad_up_gate, mlp_gate.T, preferred_element_type=jnp.float32
    ) + jnp.dot(grad_up_value, mlp_up.T, preferred_element_type=jnp.float32)
    _, norm_pull_two = jax.vjp(rms_scale, middle, norm_gain[1].astype(jnp.float32))
    middle_part, grad_gain_two = norm_pull_two(grad_normed_two)
    grad_middle = upstream + middle_part
    mid_low = grad_middle.astype(jnp.bfloat16)
    grad_out_proj = jnp.dot(joined.T, mid_low, preferred_element_type=jnp.float32)
    grad_joined = jnp.dot(mid_low, out_proj.T, preferred_element_type=jnp.float32)
    _, mix_pull = jax.vjp(glu_product, branch, states)
    branch_part, grad_direct = mix_pull(grad_joined)
    grad_branch = branch_part.astype(jnp.bfloat16)
    retain_next = jnp.concatenate([retain[1:], jnp.ones_like(retain[:1])], 0)
    suffix, local_grad = lax.associative_scan(
        chain, (retain_next, grad_direct), reverse=True, axis=0
    )
    outgoing = (retain[0] * suffix[0], retain[0] * local_grad[0])
    incoming = prefix(
        outgoing, "seq", chain, (jnp.ones_like(retain[0]), jnp.zeros_like(retain[0])), True
    )[1]
    grad_states = local_grad + suffix * incoming
    previous = jnp.concatenate([carry_in[None], states[: row_count - 1]], 0)
    grad_retain = grad_states * previous
    _, gate_pull = jax.vjp(
        partial(gate_terms, restart=restart),
        pre_rate,
        pre_admit,
        conv_low.astype(jnp.float32),
        decay_logit.astype(jnp.float32),
        gate_bias.astype(jnp.float32),
    )
    rate_part, admit_part, grad_conv_direct, grad_decay_logit, grad_gate_bias = gate_pull(
        (grad_retain, grad_states)
    )
    grad_pre_rate = rate_part.astype(jnp.bfloat16)
    grad_pre_admit = admit_part.astype(jnp.bfloat16)
    head_width = rate_proj.shape[1]
    grad_rate_proj = block_weight_grad(conv_low, grad_pre_rate, head_width)
    grad_admit_proj = block_weight_grad(conv_low, grad_pre_admit, head_width)
    grad_mixed = (
        grad_conv_direct
        + block_input_grad(grad_pre_rate, rate_proj)
        + block_input_grad(grad_pre_admit, admit_proj)
    )
    after = passed_along(grad_mixed[: CONV - 1], "seq", -1)
    widened_grad = jnp.concatenate([grad_mixed, after], 0)
    kernel = conv_kernel.astype(jnp.float32)
    stream = widened[CONV - 1 :]
    kernel_rows = [jnp.sum(grad_mixed * stream, axis=0)]
    grad_stream_full = kernel[0] * grad_mixed
    for back_steps in range(1, CONV):
        lower = CONV - 1 - back_steps
        kernel_rows.append(
            jnp.sum(
                grad_mixed * widened[lower : lower + row_count] * same_fwd[back_steps - 1], axis=0
            )
        )
        grad_stream_full = (
            grad_stream_full
            + kernel[back_steps]
            * widened_grad[back_steps : back_steps + row_count]
            * same_back[back_steps - 1]
        )
    grad_conv_kernel = jnp.stack(kernel_rows, 0)
    grad_conv_bias = jnp.sum(grad_mixed, axis=0)
    grad_stream = grad_stream_full.astype(jnp.bfloat16)
    grad_branch_proj = jnp.dot(normed.T, grad_branch, preferred_element_type=jnp.float32)
    grad_stream_proj = jnp.dot(normed.T, grad_stream, preferred_element_type=jnp.float32)
    grad_normed = jnp.dot(grad_branch, branch_proj.T, preferred_element_type=jnp.float32) + jnp.dot(
        grad_stream, stream_proj.T, preferred_element_type=jnp.float32
    )
    _, norm_pull_one = jax.vjp(rms_scale, residual, norm_gain[0].astype(jnp.float32))
    residual_part, grad_gain_one = norm_pull_one(grad_normed)
    grad_in = grad_middle + residual_part
    grads = (
        jnp.stack([grad_gain_one, grad_gain_two], 0),
        grad_branch_proj,
        grad_stream_proj,
        grad_conv_kernel,
        grad_conv_bias,
        grad_rate_proj,
        grad_admit_proj,
        grad_gate_bias,
        grad_decay_logit,
        grad_out_proj,
        grad_mlp_gate,
        grad_mlp_up,
        grad_mlp_down,
    )
    return (grad_in, grads)


def local(
    block_input,
    cotangent,
    lengths,
    offsets,
    norm_gains,
    branch_proj,
    stream_proj,
    conv_kernel,
    conv_bias,
    rate_proj,
    admit_proj,
    gate_bias,
    decay_logit,
    out_proj,
    mlp_gate,
    mlp_up,
    mlp_down,
):
    weights = (
        norm_gains,
        branch_proj,
        stream_proj,
        conv_kernel,
        conv_bias,
        rate_proj,
        admit_proj,
        gate_bias,
        decay_logit,
        out_proj,
        mlp_gate,
        mlp_up,
        mlp_down,
    )
    row_count = block_input.shape[0]
    masks = slot_masks(lengths[0], offsets[0], row_count)
    residual = block_input.astype(jnp.float32)
    saved_all = []
    for layer_idx in range(LAYERS):
        params = fetch(weights, layer_idx)
        residual, saved = layer_forward(residual, params, masks)
        saved_all.append(saved)
    gradient = cotangent.astype(jnp.float32) * masks[0]
    per_layer = [None] * LAYERS
    for layer_idx in reversed(range(LAYERS)):
        params = fetch(weights, layer_idx)
        gradient, grads = layer_backward(gradient, params, saved_all[layer_idx], masks)
        per_layer[layer_idx] = reduce_grads(grads)
    stacked = tuple(
        (
            jnp.stack([per_layer[layer_idx][member_idx] for layer_idx in range(LAYERS)], 0)
            for member_idx in range(13)
        )
    )
    return (residual.astype(jnp.bfloat16), gradient) + stacked


def solution(mesh):
    placed = (
        P(("rep", "seq"), None),
        P(("rep", "seq"), None),
        P("rep"),
        P("rep"),
        P(None, None, "seq"),
        P(None, "seq", None),
        P(None, "seq", None),
        P(None, None, "seq"),
        P(None, "seq"),
        P(None, "seq", None),
        P(None, "seq", None),
        P(None, None, "seq"),
        P(None, "seq"),
        P(None, "seq", None),
        P(None, "seq", None),
        P(None, "seq", None),
        P(None, "seq", None),
    )
    return jax.shard_map(
        local,
        mesh=mesh,
        in_specs=placed,
        out_specs=(
            P(("rep", "seq"), None),
            P(("rep", "seq"), None),
            P(None, None, ("rep", "seq")),
            P(None, ("rep", "seq"), None),
            P(None, ("rep", "seq"), None),
            P(None, None, ("rep", "seq")),
            P(None, ("rep", "seq")),
            P(None, ("rep", "seq"), None),
            P(None, ("rep", "seq"), None),
            P(None, None, ("rep", "seq")),
            P(None, ("rep", "seq")),
            P(None, ("rep", "seq"), None),
            P(None, ("rep", "seq"), None),
            P(None, ("rep", "seq"), None),
            P(None, ("rep", "seq"), None),
        ),
        check_vma=False,
    )
```

profile of v0, /device:TPU:0, one launch (start us, length us, event | category | flops | bytes accessed | tf_op | source)
XLA Modules:
  0.0 6317.6 jit_solution(8932036363639834888)
XLA Ops:
  63.3 17.5 all-gather.3
  80.9 16.2 all-gather.7
  380.3 15.7 all-gather.27
  470.2 195.2 %all-gather.61.cloned.1.call-done = bf16[1,1536,4608]{2,1,0:T(8,128)(2,1)} async-done(((bf16[1,384,4608]{2,1,0:T(8,128)(2,1)}), bf16[1,1536,4608]{2,1,0:T(8,128)(2,1)}) %all-gather.61.cloned.1.call-update) | async-done | bytes 14155792 | tf_op jit(solution)/shard_map/all_gather | solution.py:131
  675.9 233.3 %all-gather.63.cloned.1.call-done = bf16[1,1536,4608]{2,1,0:T(8,128)(2,1)} async-done(((bf16[1,384,4608]{2,1,0:T(8,128)(2,1)}), bf16[1,1536,4608]{2,1,0:T(8,128)(2,1)}) %all-gather.63.cloned.1.call-update) | async-done | bytes 14155792 | tf_op jit(solution)/shard_map/all_gather | solution.py:132
  922.1 230.8 %all-gather.65.cloned.1.call-done = bf16[1,4608,1536]{2,1,0:T(8,128)(2,1)} async-done(((bf16[1,1152,1536]{2,1,0:T(8,128)(2,1)}), bf16[1,4608,1536]{2,1,0:T(8,128)(2,1)}) %all-gather.65.cloned.1.call-update) | async-done | bytes 14155792 | tf_op jit(solution)/shard_map/all_gather | solution.py:133
  1162.1 106.5 %all-gather.69.cloned.1.call-done = bf16[1,1536,2048]{2,1,0:T(8,128)(2,1)} async-done(((bf16[1,384,2048]{2,1,0:T(8,128)(2,1)}), bf16[1,1536,2048]{2,1,0:T(8,128)(2,1)}) %all-gather.69.cloned.1.call-update) | async-done | bytes 6291472 | tf_op jit(solution)/shard_map/all_gather | solution.py:123
  1274.5 237.7 %all-gather.81.cloned.1.call-done = bf16[1,4608,1536]{2,1,0:T(8,128)(2,1)} async-done(((bf16[1,1152,1536]{2,1,0:T(8,128)(2,1)}), bf16[1,4608,1536]{2,1,0:T(8,128)(2,1)}) %all-gather.81.cloned.1.call-update) | async-done | bytes 14155792 | tf_op jit(solution)/shard_map/all_gather | solution.py:133
  1544.9 23.9 all-gather.73.cloned.1.call-done
  1826.3 16.2 all-gather.28
  1860.4 184.8 %all-gather.79.cloned.1.call-done = bf16[1,1536,4608]{2,1,0:T(8,128)(2,1)} async-done(((bf16[1,384,4608]{2,1,0:T(8,128)(2,1)}), bf16[1,1536,4608]{2,1,0:T(8,128)(2,1)}) %all-gather.79.cloned.1.call-update) | async-done | bytes 14155792 | tf_op jit(solution)/shard_map/all_gather | solution.py:132
  2056.7 232.1 %all-gather.77.cloned.1.call-done = bf16[1,1536,4608]{2,1,0:T(8,128)(2,1)} async-done(((bf16[1,384,4608]{2,1,0:T(8,128)(2,1)}), bf16[1,1536,4608]{2,1,0:T(8,128)(2,1)}) %all-gather.77.cloned.1.call-update) | async-done | bytes 14155792 | tf_op jit(solution)/shard_map/all_gather | solution.py:131
  2655.0 16.9 rev.17
  2671.9 16.7 rev.16
  2947.0 16.7 rev.19
  2963.8 16.9 rev.18
  3201.5 100.6 %reduce-scatter.31.cloned.1.call-done = f32[64,256]{1,0:T(8,128)} async-done(((f32[2048,256]{1,0:T(8,128)}), f32[64,256]{1,0:T(8,128)}) %reduce-scatter.31.cloned.1.call-update) | async-done | bytes 65552 | tf_op jit(solution)/shard_map/reduce_scatter | solution.py:151
  3302.2 138.3 %reduce-scatter.29.cloned.1.call-done = f32[64,256]{1,0:T(8,128)} async-done(((f32[2048,256]{1,0:T(8,128)}), f32[64,256]{1,0:T(8,128)}) %reduce-scatter.29.cloned.1.call-update) | async-done | bytes 65552 | tf_op jit(solution)/shard_map/reduce_scatter | solution.py:151
  3442.0 136.2 %reduce-scatter.27.cloned.1.call-done = f32[64,256]{1,0:T(8,128)} async-done(((f32[2048,256]{1,0:T(8,128)}), f32[64,256]{1,0:T(8,128)}) %reduce-scatter.27.cloned.1.call-update) | async-done | bytes 65552 | tf_op jit(solution)/shard_map/reduce_scatter | solution.py:150
  3578.2 138.3 %reduce-scatter.25.cloned.1.call-done = f32[64,256]{1,0:T(8,128)} async-done(((f32[2048,256]{1,0:T(8,128)}), f32[64,256]{1,0:T(8,128)}) %reduce-scatter.25.cloned.1.call-update) | async-done | bytes 65552 | tf_op jit(solution)/shard_map/reduce_scatter | solution.py:150
  3718.1 159.4 %reduce-scatter.19.cloned.1.call-done = f32[48,2048]{1,0:T(8,128)} async-done(((f32[1536,2048]{1,0:T(8,128)}), f32[48,2048]{1,0:T(8,128)}) %reduce-scatter.19.cloned.1.call-update) | async-done | bytes 393232 | tf_op jit(solution)/shard_map/reduce_scatter | solution.py:148
  3877.4 160.9 %reduce-scatter.17.cloned.1.call-done = f32[48,2048]{1,0:T(8,128)} async-done(((f32[1536,2048]{1,0:T(8,128)}), f32[48,2048]{1,0:T(8,128)}) %reduce-scatter.17.cloned.1.call-update) | async-done | bytes 393232 | tf_op jit(solution)/shard_map/reduce_scatter | solution.py:148
  4040.3 159.7 %reduce-scatter.35.cloned.1.call-done = f32[64,1536]{1,0:T(8,128)} async-done(((f32[2048,1536]{1,0:T(8,128)}), f32[64,1536]{1,0:T(8,128)}) %reduce-scatter.35.cloned.1.call-update) | async-done | bytes 393232 | tf_op jit(solution)/shard_map/reduce_scatter | solution.py:152
  4200.1 160.5 %reduce-scatter.33.cloned.1.call-done = f32[64,1536]{1,0:T(8,128)} async-done(((f32[2048,1536]{1,0:T(8,128)}), f32[64,1536]{1,0:T(8,128)}) %reduce-scatter.33.cloned.1.call-update) | async-done | bytes 393232 | tf_op jit(solution)/shard_map/reduce_scatter | solution.py:152
  4362.6 159.3 %reduce-scatter.23.cloned.1.call-done = f32[48,2048]{1,0:T(8,128)} async-done(((f32[1536,2048]{1,0:T(8,128)}), f32[48,2048]{1,0:T(8,128)}) %reduce-scatter.23.cloned.1.call-update) | async-done | bytes 393232 | tf_op jit(solution)/shard_map/reduce_scatter | solution.py:149
  4522.0 160.6 %reduce-scatter.21.cloned.1.call-done = f32[48,2048]{1,0:T(8,128)} async-done(((f32[1536,2048]{1,0:T(8,128)}), f32[48,2048]{1,0:T(8,128)}) %reduce-scatter.21.cloned.1.call-update) | async-done | bytes 393232 | tf_op jit(solution)/shard_map/reduce_scatter | solution.py:149
  4684.6 268.3 %reduce-scatter.47.cloned.1.call-done = f32[144,1536]{1,0:T(8,128)} async-done(((f32[4608,1536]{1,0:T(8,128)}), f32[144,1536]{1,0:T(8,128)}) %reduce-scatter.47.cloned.1.call-update) | async-done | bytes 884752 | tf_op jit(solution)/shard_map/reduce_scatter | solution.py:155
  4952.9 270.9 %reduce-scatter.45.cloned.1.call-done = f32[144,1536]{1,0:T(8,128)} async-done(((f32[4608,1536]{1,0:T(8,128)}), f32[144,1536]{1,0:T(8,128)}) %reduce-scatter.45.cloned.1.call-update) | async-done | bytes 884752 | tf_op jit(solution)/shard_map/reduce_scatter | solution.py:155
  5226.6 268.2 %reduce-scatter.43.cloned.1.call-done = f32[48,4608]{1,0:T(8,128)} async-done(((f32[1536,4608]{1,0:T(8,128)}), f32[48,4608]{1,0:T(8,128)}) %reduce-scatter.43.cloned.1.call-update) | async-done | bytes 884752 | tf_op jit(solution)/shard_map/reduce_scatter | solution.py:154
  5494.8 271.1 %reduce-scatter.41.cloned.1.call-done = f32[48,4608]{1,0:T(8,128)} async-done(((f32[1536,4608]{1,0:T(8,128)}), f32[48,4608]{1,0:T(8,128)}) %reduce-scatter.41.cloned.1.call-update) | async-done | bytes 884752 | tf_op jit(solution)/shard_map/reduce_scatter | solution.py:154
  5768.6 268.3 %reduce-scatter.39.cloned.1.call-done = f32[48,4608]{1,0:T(8,128)} async-done(((f32[1536,4608]{1,0:T(8,128)}), f32[48,4608]{1,0:T(8,128)}) %reduce-scatter.39.cloned.1.call-update) | async-done | bytes 884752 | tf_op jit(solution)/shard_map/reduce_scatter | solution.py:153
  6037.0 270.8 %reduce-scatter.37.cloned.1.call-done = f32[48,4608]{1,0:T(8,128)} async-done(((f32[1536,4608]{1,0:T(8,128)}), f32[48,4608]{1,0:T(8,128)}) %reduce-scatter.37.cloned.1.call-update) | async-done | bytes 884752 | tf_op jit(solution)/shard_map/reduce_scatter | solution.py:153
  (1358 shorter events, 1629.1 us)
Async XLA Ops:
  13.3 194.0 %all-gather.57.cloned.1.call-start = ((), (), s32[]{:S(2)}) async-start(), calls=%async_computation.35 | async-start | bytes 1310720 | tf_op jit(solution)/shard_map/all_gather | solution.py:127
  15.2 414.6 %all-gather.51.cloned.1.call-start = ((), (), s32[]{:S(2)}) async-start(), calls=%async_computation.32 | async-start | bytes 7864320 | tf_op jit(solution)/shard_map/all_gather | solution.py:122
  17.2 423.7 %all-gather.59.cloned.1.call-start = ((), (), s32[]{:S(2)}) async-start(), calls=%async_computation.36 | async-start | bytes 7864320 | tf_op jit(solution)/shard_map/all_gather | solution.py:130
  21.1 644.3 %all-gather.61.cloned.1.call-start = ((), (), s32[]{:S(2)}) async-start(), calls=%async_computation.37 | async-start | bytes 17694720 | tf_op jit(solution)/shard_map/all_gather | solution.py:131
  28.3 880.8 %all-gather.63.cloned.1.call-start = ((), (), s32[]{:S(2)}) async-start(), calls=%async_computation.38 | async-start | bytes 17694720 | tf_op jit(solution)/shard_map/all_gather | solution.py:132
  34.8 1118.1 %all-gather.65.cloned.1.call-start = ((), (), s32[]{:S(2)}) async-start(), calls=%async_computation.39 | async-start | bytes 17694720 | tf_op jit(solution)/shard_map/all_gather | solution.py:133
  41.4 1227.2 %all-gather.69.cloned.1.call-start = ((), (), s32[]{:S(2)}) async-start(), calls=%async_computation.41 | async-start | bytes 7864320 | tf_op jit(solution)/shard_map/all_gather | solution.py:123
  42.2 1470.0 %all-gather.81.cloned.1.call-start = ((), (), s32[]{:S(2)}) async-start(), calls=%async_computation.47 | async-start | bytes 17694720 | tf_op jit(solution)/shard_map/all_gather | solution.py:133
  42.8 1497.2 %all-gather.71.cloned.1.call-start = ((), (), s32[]{:S(2)}) async-start(), calls=%async_computation.42 | async-start | bytes 1310720 | tf_op jit(solution)/shard_map/all_gather | solution.py:126
  43.5 1525.3 %all-gather.73.cloned.1.call-start = ((), (), s32[]{:S(2)}) async-start(), calls=%async_computation.43 | async-start | bytes 1310720 | tf_op jit(solution)/shard_map/all_gather | solution.py:127
  44.1 1798.5 %all-gather.67.cloned.1.call-start = ((), (), s32[]{:S(2)}) async-start(), calls=%async_computation.40 | async-start | bytes 7864320 | tf_op jit(solution)/shard_map/all_gather | solution.py:122
  44.8 1808.0 %all-gather.75.cloned.1.call-start = ((), (), s32[]{:S(2)}) async-start(), calls=%async_computation.44 | async-start | bytes 7864320 | tf_op jit(solution)/shard_map/all_gather | solution.py:130
  45.4 1999.8 %all-gather.79.cloned.1.call-start = ((), (), s32[]{:S(2)}) async-start(), calls=%async_computation.46 | async-start | bytes 17694720 | tf_op jit(solution)/shard_map/all_gather | solution.py:132
  46.0 2242.8 %all-gather.77.cloned.1.call-start = ((), (), s32[]{:S(2)}) async-start(), calls=%async_computation.45 | async-start | bytes 17694720 | tf_op jit(solution)/shard_map/all_gather | solution.py:131
  46.6 3144.6 %all-reduce.139.cloned.1.call-start = ((), (), s32[]{:S(2)}) async-start(), calls=%async_computation.48 | async-start | bytes 311296 | tf_op jit(solution)/shard_map/psum | solution.py:145
  1273.2 250.4 %collective-permute-start.1 = (f32[3,2048]{1,0:T(4,128)S(1)}, f32[3,2048]{1,0:T(4,128)S(1)}, u32[]{:S(2)}, u32[]{:S(2)}) collective-permute-start(f32[3,2048]{1,0:T(4,128)S(1)} %slice.1713), channel_id=1, source_target_pairs={{0,1},{1,2},{2,3},{4,5},{5,6},{6,7},{8,9},{9,10},{10,11},{12,13},{... | collective-permute-start | bytes 73736 | tf_op jit(solution)/shard_map/ppermute | solution.py:18
  3033.6 268.5 %reduce-scatter.31.cloned.1.call-start = ((), (), s32[]{:S(2)}) async-start(), calls=%async_computation.23 | async-start | bytes 2162688 | tf_op jit(solution)/shard_map/reduce_scatter | solution.py:151
  3035.5 405.0 %reduce-scatter.29.cloned.1.call-start = ((), (), s32[]{:S(2)}) async-start(), calls=%async_computation.22 | async-start | bytes 2162688 | tf_op jit(solution)/shard_map/reduce_scatter | solution.py:151
  3039.7 538.5 %reduce-scatter.27.cloned.1.call-start = ((), (), s32[]{:S(2)}) async-start(), calls=%async_computation.21 | async-start | bytes 2162688 | tf_op jit(solution)/shard_map/reduce_scatter | solution.py:150
  3042.8 673.7 %reduce-scatter.25.cloned.1.call-start = ((), (), s32[]{:S(2)}) async-start(), calls=%async_computation.20 | async-start | bytes 2162688 | tf_op jit(solution)/shard_map/reduce_scatter | solution.py:150
  3045.9 831.5 %reduce-scatter.19.cloned.1.call-start = ((), (), s32[]{:S(2)}) async-start(), calls=%async_computation.17 | async-start | bytes 12976128 | tf_op jit(solution)/shard_map/reduce_scatter | solution.py:148
  3053.6 984.7 %reduce-scatter.17.cloned.1.call-start = ((), (), s32[]{:S(2)}) async-start(), calls=%async_computation.16 | async-start | bytes 12976128 | tf_op jit(solution)/shard_map/reduce_scatter | solution.py:148
  3061.4 1138.7 %reduce-scatter.35.cloned.1.call-start = ((), (), s32[]{:S(2)}) async-start(), calls=%async_computation.25 | async-start | bytes 12976128 | tf_op jit(solution)/shard_map/reduce_scatter | solution.py:152
  3070.5 1290.1 %reduce-scatter.33.cloned.1.call-start = ((), (), s32[]{:S(2)}) async-start(), calls=%async_computation.24 | async-start | bytes 12976128 | tf_op jit(solution)/shard_map/reduce_scatter | solution.py:152
  3079.5 1442.5 %reduce-scatter.23.cloned.1.call-start = ((), (), s32[]{:S(2)}) async-start(), calls=%async_computation.19 | async-start | bytes 12976128 | tf_op jit(solution)/shard_map/reduce_scatter | solution.py:149
  3087.0 1595.5 %reduce-scatter.21.cloned.1.call-start = ((), (), s32[]{:S(2)}) async-start(), calls=%async_computation.18 | async-start | bytes 12976128 | tf_op jit(solution)/shard_map/reduce_scatter | solution.py:149
  3094.7 1858.2 %reduce-scatter.47.cloned.1.call-start = ((), (), s32[]{:S(2)}) async-start(), calls=%async_computation.31 | async-start | bytes 29196288 | tf_op jit(solution)/shard_map/reduce_scatter | solution.py:155
  3108.8 2115.0 %reduce-scatter.45.cloned.1.call-start = ((), (), s32[]{:S(2)}) async-start(), calls=%async_computation.30 | async-start | bytes 29196288 | tf_op jit(solution)/shard_map/reduce_scatter | solution.py:155
  3123.4 2371.4 %reduce-scatter.43.cloned.1.call-start = ((), (), s32[]{:S(2)}) async-start(), calls=%async_computation.29 | async-start | bytes 29196288 | tf_op jit(solution)/shard_map/reduce_scatter | solution.py:154
  3137.5 2628.4 %reduce-scatter.41.cloned.1.call-start = ((), (), s32[]{:S(2)}) async-start(), calls=%async_computation.28 | async-start | bytes 29196288 | tf_op jit(solution)/shard_map/reduce_scatter | solution.py:154
  3151.6 2885.4 %reduce-scatter.39.cloned.1.call-start = ((), (), s32[]{:S(2)}) async-start(), calls=%async_computation.27 | async-start | bytes 29196288 | tf_op jit(solution)/shard_map/reduce_scatter | solution.py:153
  3164.6 3143.2 %reduce-scatter.37.cloned.1.call-start = ((), (), s32[]{:S(2)}) async-start(), calls=%async_computation.26 | async-start | bytes 29196288 | tf_op jit(solution)/shard_map/reduce_scatter | solution.py:153
  (287 other events, 5747.7 us)
Sparse Core Ops, SparseCore 0:
  11.3 118.9 all-gather.52
  132.5 26.3 all-gather.54
  161.0 27.8 all-gather.56
  190.9 115.1 all-gather.50
  307.5 114.2 all-gather.58
  423.2 242.1 all-gather.60
  667.0 242.1 all-gather.62
  910.7 242.1 all-gather.64
  1155.0 113.5 all-gather.68
  1270.0 242.1 all-gather.80
  1541.3 27.4 all-gather.72
  1570.9 114.8 all-gather.66
  1687.3 113.8 all-gather.74
  1802.6 242.5 all-gather.78
  2046.6 242.1 all-gather.76
  3033.8 125.2 all-reduce.138
  3161.3 140.8 reduce-scatter.30
  3304.4 136.0 reduce-scatter.28
  3442.7 135.5 reduce-scatter.26
  3580.5 135.9 reduce-scatter.24
  3723.6 153.7 reduce-scatter.18
  3883.4 154.8 reduce-scatter.16
  4045.2 154.8 reduce-scatter.34
  4206.1 154.4 reduce-scatter.32
  4367.5 154.4 reduce-scatter.22
  4527.8 154.7 reduce-scatter.20
  4690.1 262.7 reduce-scatter.46
  4960.5 263.2 reduce-scatter.44
  5231.3 263.4 reduce-scatter.42
  5502.4 263.4 reduce-scatter.40
  5773.4 263.4 reduce-scatter.38
  6044.4 263.3 reduce-scatter.36
  (1 shorter events, 26.1 us)
where the time goes:
time: 6350 us; the launch traced here: 6320 us
  waiting for transfers between devices  4560 us (72%)
  local copies, waits for them, and re-layouts  851 us (13%)
  matrix products  361 us (6%)
  other arithmetic  274 us (4%)
  blocking collectives  245 us (4%)
    reduce_scatter x2, waiting for transfers between devices, reduce_grads(): lax.psum_scatter(grads[11], ('rep', 'seq'), scatter_dimension=0, tiled=True)  539 us
    reduce_scatter x2, waiting for transfers between devices, reduce_grads(): lax.psum_scatter(grads[12], ('rep', 'seq'), scatter_dimension=0, tiled=True)  539 us
    reduce_scatter x2, waiting for transfers between devices, reduce_grads(): lax.psum_scatter(grads[10], ('rep', 'seq'), scatter_dimension=0, tiled=True)  539 us
    all_gather x2, waiting for transfers between devices, fetch(): lax.all_gather(weights[12][layer_idx], 'seq', axis=0, tiled=True)  468 us
    all_gather x2, waiting for transfers between devices, fetch(): lax.all_gather(weights[10][layer_idx], 'seq', axis=0, tiled=True)  427 us
    all_gather x2, waiting for transfers between devices, fetch(): lax.all_gather(weights[11][layer_idx], 'seq', axis=0, tiled=True)  418 us
    reduce_scatter x2, waiting for transfers between devices, reduce_grads(): lax.psum_scatter(grads[1], ('rep', 'seq'), scatter_dimension=0, tiled=True)  320 us
    reduce_scatter x2, waiting for transfers between devices, reduce_grads(): lax.psum_scatter(grads[9], ('rep', 'seq'), scatter_dimension=0, tiled=True)  320 us
  transfers between devices with their start and end apart: 37, of which 27 were waited for; matrix products, arithmetic and copies ran while one was open for 12% of the time, Pallas kernels for 0%

commit v1 on v0

v1 whole, which is shorter than its diff:
```python
from functools import partial

import jax
import jax.numpy as jnp
from jax import lax
from jax.experimental import pallas as pl
from jax.experimental.pallas import tpu as pltpu
from jax.sharding import PartitionSpec as P

CONV = 4
LAYERS = 2
EPSILON = 1e-06
BF = jnp.bfloat16
F32 = jnp.float32


def dot(a, b):
    return jnp.dot(a, b, preferred_element_type=F32)


def dot_tn(a, b):
    return lax.dot_general(a, b, (((0,), (0,)), ((), ())), preferred_element_type=F32)


def dot_nt(a, b):
    return lax.dot_general(a, b, (((1,), (1,)), ((), ())), preferred_element_type=F32)


def rms_scale(values, scale_vec):
    return (
        values * lax.rsqrt(jnp.mean(values * values, axis=-1, keepdims=True) + EPSILON) * scale_vec
    )


def gate_terms(pre_rate, pre_admit, conv_value, decay_logit, gate_bias, restart):
    rate_gate = jax.nn.sigmoid(pre_rate + gate_bias[0])
    admit_gate = jax.nn.sigmoid(pre_admit + gate_bias[1])
    log_retain = -8.0 * rate_gate * jax.nn.softplus(-decay_logit)
    retain = jnp.where(restart, 0.0, jnp.exp(log_retain))
    input_scale = jnp.where(restart, 1.0, jnp.sqrt(-jnp.expm1(2.0 * log_retain)))
    return (retain, input_scale * admit_gate * conv_value)


def glu_product(gate_in, value_in):
    return jax.nn.gelu(gate_in, approximate=True) * value_in


class Plan:
    def __init__(self, mesh, heads):
        self.rep = mesh.shape["rep"]
        self.seq = mesh.shape["seq"]
        self.tp = min(heads, self.rep)
        self.dp = self.rep // self.tp
        tp, dp = self.tp, self.dp
        self.tp_groups = None if dp == 1 else [[d * tp + t for t in range(tp)] for d in range(dp)]
        self.dp_groups = [[d * tp + t for d in range(dp)] for t in range(tp)]


def gather_plane(plan, value):
    return lax.all_gather(value, "rep", axis=0, tiled=True, axis_index_groups=plan.tp_groups)


def scatter_plane(plan, value):
    return lax.psum_scatter(
        value, "rep", scatter_dimension=0, tiled=True, axis_index_groups=plan.tp_groups
    )


def owner_chunks(plan, value):
    tp, seq = plan.tp, plan.seq
    pairs = []
    for d in range(plan.dp):
        for j in range(tp):
            for z in range(seq):
                o = tp * z + j
                pairs.append(((d * tp + j) * seq + z, (d * tp + o // seq) * seq + o % seq))
    return lax.ppermute(value, ("rep", "seq"), pairs)


def to_owners(plan, chunk, axis):
    if plan.dp == 1:
        return chunk
    part = lax.psum_scatter(
        chunk, "rep", scatter_dimension=axis, tiled=True, axis_index_groups=plan.dp_groups
    )
    tp, seq, dp = plan.tp, plan.seq, plan.dp
    pairs = [
        ((d * tp + t) * seq + z, (t * seq + z) * dp + d)
        for d in range(dp)
        for t in range(tp)
        for z in range(seq)
    ]
    return lax.ppermute(part, ("rep", "seq"), pairs)


def shifted(plan, value, step):
    pairs = [(z, z + step) for z in range(plan.seq) if 0 <= z + step < plan.seq]
    return lax.ppermute(value, "seq", pairs)


def scan_body(reverse, rows, slots, a_ref, b_ref, h_ref, q_ref):
    width = a_ref.shape[1]

    def step(i, carry):
        state, decay = carry
        p = rows - 1 - i if reverse else i
        at = pl.ds(p, slots, stride=rows)
        a = a_ref[at, :]
        state = a * state + b_ref[at, :]
        decay = a * decay
        h_ref[at, :] = state
        q_ref[at, :] = decay
        return state, decay

    lax.fori_loop(
        0,
        rows,
        step,
        (jnp.zeros((slots, width), F32), jnp.ones((slots, width), F32)),
        unroll=8,
    )


def local_scan(a, b, slots, reverse):
    rows = a.shape[0] // slots
    width = 128
    spec = pl.BlockSpec((a.shape[0], width), lambda i: (0, i))
    shape = jax.ShapeDtypeStruct(a.shape, F32)
    return pl.pallas_call(
        partial(scan_body, reverse, rows, slots),
        grid=(a.shape[1] // width,),
        in_specs=[spec, spec],
        out_specs=[spec, spec],
        out_shape=[shape, shape],
        compiler_params=pltpu.CompilerParams(vmem_limit_bytes=40 << 20),
        cost_estimate=pl.CostEstimate(flops=0, bytes_accessed=16 * a.size, transcendentals=0),
    )(a, b)


def carried(plan, decay, state, reverse):
    ends = lax.all_gather(jnp.stack([decay, state]), "seq")
    place = lax.axis_index("seq")
    carry = jnp.zeros_like(state)
    order = range(plan.seq)
    for z in reversed(order) if reverse else order:
        ahead = z > place if reverse else z < place
        carry = jnp.where(ahead, ends[z, 0] * carry + ends[z, 1], carry)
    return carry


def masks_of(plan, lengths, offsets, rows):
    start = lax.axis_index("seq") * rows
    extra = CONV - 1
    positions = start + jnp.arange(rows + 2 * extra, dtype=jnp.int32) - extra
    inside = (positions >= offsets[:, None]) & (positions < (offsets + lengths)[:, None])
    core = inside[:, extra : extra + rows]
    restart = (positions[extra : extra + rows] == 0)[None] | (core != inside[:, extra - 1 : extra - 1 + rows])
    fwd = [
        (core == inside[:, extra - j : extra - j + rows]).astype(F32)[..., None]
        for j in range(1, CONV)
    ]
    back = [
        (core == inside[:, extra + j : extra + j + rows]).astype(F32)[..., None]
        for j in range(1, CONV)
    ]
    return restart.reshape(-1, 1), fwd, back


def layer_forward(plan, residual, w, masks):
    restart, same_fwd, _ = masks
    slots, rows = plan.tp, residual.shape[0]
    head = w["rate"].shape[0]
    normed = rms_scale(residual, w["gain"][0]).astype(BF)
    x = gather_plane(plan, normed)
    both = dot(x, w["col_rec"])
    branch, stream = both[:, :head], both[:, head:]
    stream3 = stream.reshape(slots, rows, head)
    before = shifted(plan, stream3[:, rows - (CONV - 1) :], 1)
    widened = jnp.concatenate([before, stream3], 1)
    taps = w["conv"]
    mixed = w["bias"] + taps[0] * stream3
    for j in range(1, CONV):
        low = CONV - 1 - j
        mixed = mixed + taps[j] * widened[:, low : low + rows] * same_fwd[j - 1]
    conv_low = mixed.astype(BF).reshape(slots * rows, head)
    pre_rate = dot(conv_low, w["rate"])
    pre_admit = dot(conv_low, w["admit"])
    retain, inflow = gate_terms(
        pre_rate, pre_admit, conv_low.astype(F32), w["decay"], w["gbias"], restart
    )
    states, running = local_scan(retain, inflow, slots, False)
    carry = carried(
        plan,
        running.reshape(slots, rows, head)[:, -1],
        states.reshape(slots, rows, head)[:, -1],
        False,
    )
    states = (
        states.reshape(slots, rows, head) + running.reshape(slots, rows, head) * carry[:, None]
    ).reshape(slots * rows, head)
    joined = glu_product(branch, states).astype(BF)
    middle = residual + scatter_plane(plan, dot(joined, w["out"]).astype(BF)).astype(F32)
    normed_two = rms_scale(middle, w["gain"][1]).astype(BF)
    x_two = gather_plane(plan, normed_two)
    up = dot(x_two, w["col_mlp"])
    half = up.shape[1] // 2
    hidden = glu_product(up[:, :half], up[:, half:]).astype(BF)
    output = middle + scatter_plane(plan, dot(hidden, w["down"]).astype(BF)).astype(F32)
    saved = (
        residual, x, branch, widened, conv_low, pre_rate, pre_admit, retain, states, carry,
        joined, middle, x_two, up, hidden,
    )
    return output, saved


def layer_backward(plan, upstream, w, saved, masks):
    (
        residual, x, branch, widened, conv_low, pre_rate, pre_admit, retain, states, carry,
        joined, middle, x_two, up, hidden,
    ) = saved
    restart, same_fwd, same_back = masks
    slots, rows = plan.tp, residual.shape[0]
    seq = plan.seq
    head = w["rate"].shape[0]
    half = up.shape[1] // 2
    down_low = gather_plane(plan, upstream.astype(BF))
    grad_hidden = dot_nt(down_low, w["down"])
    _, glu_pull = jax.vjp(glu_product, up[:, :half], up[:, half:])
    grad_up = jnp.concatenate([p.astype(BF) for p in glu_pull(grad_hidden)], 1)
    grad_two = scatter_plane(plan, dot_nt(grad_up, w["col_mlp"]).astype(BF)).astype(F32)
    g_down = dot_tn(hidden, down_low)
    g_col_mlp = dot_tn(x_two, grad_up)
    _, pull_two = jax.vjp(rms_scale, middle, w["gain"][1])
    part, grad_gain_two = pull_two(grad_two)
    grad_middle = upstream + part
    mid_low = gather_plane(plan, grad_middle.astype(BF))
    g_out = dot_tn(joined, mid_low)
    grad_joined = dot_nt(mid_low, w["out"])
    _, mix_pull = jax.vjp(glu_product, branch, states)
    branch_part, grad_direct = mix_pull(grad_joined)
    retain3 = retain.reshape(slots, rows, head)
    retain_next = jnp.concatenate([retain3[:, 1:], jnp.ones_like(retain3[:, :1])], 1)
    local, suffix = local_scan(retain_next.reshape(-1, head), grad_direct, slots, True)
    local3, suffix3 = local.reshape(retain3.shape), suffix.reshape(retain3.shape)
    first = retain3[:, 0]
    incoming = carried(plan, first * suffix3[:, 0], first * local3[:, 0], True)
    grad_states3 = local3 + suffix3 * incoming[:, None]
    grad_states = grad_states3.reshape(-1, head)
    states3 = states.reshape(retain3.shape)
    previous = jnp.concatenate([carry[:, None], states3[:, :-1]], 1).reshape(-1, head)
    _, gate_pull = jax.vjp(
        partial(gate_terms, restart=restart),
        pre_rate, pre_admit, conv_low.astype(F32), w["decay"], w["gbias"],
    )
    rate_part, admit_part, grad_conv, grad_decay, grad_gbias = gate_pull(
        (grad_states * previous, grad_states)
    )
    grad_pre = jnp.concatenate([rate_part.astype(BF), admit_part.astype(BF)], 1)
    g_gates = dot_tn(conv_low, grad_pre)
    grad_mixed = (
        grad_conv + dot_nt(grad_pre[:, :head], w["rate"]) + dot_nt(grad_pre[:, head:], w["admit"])
    ).reshape(slots, rows, head)
    after = shifted(plan, grad_mixed[:, : CONV - 1], -1)
    wide_grad = jnp.concatenate([grad_mixed, after], 1)
    taps = w["conv"]
    tap_rows = [jnp.sum(grad_mixed * widened[:, CONV - 1 :], axis=(0, 1))]
    grad_stream = taps[0] * grad_mixed
    for j in range(1, CONV):
        low = CONV - 1 - j
        tap_rows.append(
            jnp.sum(grad_mixed * widened[:, low : low + rows] * same_fwd[j - 1], axis=(0, 1))
        )
        grad_stream = grad_stream + taps[j] * wide_grad[:, j : j + rows] * same_back[j - 1]
    grad_bias = jnp.sum(grad_mixed, axis=(0, 1))
    grad_both = jnp.concatenate(
        [branch_part.astype(BF), grad_stream.astype(BF).reshape(-1, head)], 1
    )
    grad_normed = scatter_plane(plan, dot_nt(grad_both, w["col_rec"]).astype(BF)).astype(F32)
    g_col_rec = dot_tn(x, grad_both)
    _, pull_one = jax.vjp(rms_scale, residual, w["gain"][0])
    part, grad_gain_one = pull_one(grad_normed)
    channel = jnp.stack(tap_rows + [grad_bias, grad_gbias[0], grad_gbias[1], grad_decay], 0)
    gains = jnp.stack([grad_gain_one, grad_gain_two], 0)
    return grad_middle + part, (g_col_rec, g_gates, g_out, g_col_mlp, g_down), channel, gains


def local(plan, *args):
    (
        block_input, cotangent, lengths, offsets, norm_gains, branch_proj, stream_proj, conv_kernel,
        conv_bias, rate_proj, admit_proj, gate_bias, decay_logit, out_proj, mlp_gate, mlp_up,
        mlp_down,
    ) = args
    tp, dp, seq = plan.tp, plan.dp, plan.seq
    t = lax.axis_index("rep") % tp
    z = lax.axis_index("seq")
    rows = block_input.shape[0]
    head = branch_proj.shape[2] // tp
    units = mlp_gate.shape[2] // tp

    channels = conv_kernel.shape[2]
    small = jnp.concatenate(
        [
            conv_kernel,
            conv_bias[:, None],
            gate_bias,
            decay_logit[:, None],
        ],
        1,
    )
    packed = jnp.concatenate([small.reshape(-1), norm_gains.reshape(-1)])
    packed = lax.all_gather(packed, "seq")
    small = packed[:, : small.size].reshape(seq, LAYERS, 8, channels)
    small = jnp.moveaxis(small, 0, 2).reshape(LAYERS, 8, seq * channels)
    small = lax.dynamic_slice_in_dim(small, t * head, head, 2).astype(F32)
    gains = packed[:, LAYERS * 8 * channels :].reshape(seq, LAYERS, 2, -1)
    gains = jnp.moveaxis(gains, 0, 2).reshape(LAYERS, 2, -1).astype(F32)
    layout = gather_plane(plan, jnp.stack([lengths, offsets], 1))
    masks = masks_of(plan, layout[:, 0], layout[:, 1], rows)

    def col(weight, layer, width):
        return lax.dynamic_slice_in_dim(weight[layer], t * width, width, 1)

    def chunk(weight, layer):
        size = weight.shape[1] // tp
        return lax.dynamic_slice_in_dim(weight[layer], t * size, size, 0)

    weights = []
    for l in range(LAYERS):
        col_rec = jnp.concatenate([col(branch_proj, l, head), col(stream_proj, l, head)], 1)
        col_mlp = jnp.concatenate([col(mlp_gate, l, units), col(mlp_up, l, units)], 1)
        wide = owner_chunks(plan, jnp.concatenate([chunk(out_proj, l), chunk(mlp_down, l)], 0))
        out_rows = out_proj.shape[1] // tp
        gates = owner_chunks(plan, jnp.concatenate([chunk(rate_proj, l), chunk(admit_proj, l)], 1))
        gates = lax.all_gather(gates, "seq", axis=0, tiled=True)
        weights.append(
            dict(
                gain=gains[l],
                conv=small[l, :CONV],
                bias=small[l, CONV],
                gbias=small[l, CONV + 1 : CONV + 3],
                decay=small[l, CONV + 3],
                col_rec=lax.all_gather(col_rec, "seq", axis=0, tiled=True),
                rate=gates[:, :head],
                admit=gates[:, head:],
                out=lax.all_gather(wide[:out_rows], "seq", axis=0, tiled=True),
                col_mlp=lax.all_gather(col_mlp, "seq", axis=0, tiled=True),
                down=lax.all_gather(wide[out_rows:], "seq", axis=0, tiled=True),
            )
        )

    residual = block_input.astype(F32)
    saved_all = []
    for l in range(LAYERS):
        residual, saved = layer_forward(plan, residual, weights[l], masks)
        saved_all.append(saved)
    positions = z * rows + jnp.arange(rows, dtype=jnp.int32)
    inside = (positions >= offsets[0]) & (positions < offsets[0] + lengths[0])
    gradient = cotangent.astype(F32) * inside.astype(F32)[:, None]

    outs = [None] * LAYERS
    channel_all, gain_all = [None] * LAYERS, [None] * LAYERS

    def over_seq(value):
        return lax.psum_scatter(value, "seq", scatter_dimension=0, tiled=False)

    def exchange(share):
        return lax.all_to_all(
            share, "rep", split_axis=0, concat_axis=0, axis_index_groups=plan.tp_groups
        )

    for l in reversed(range(LAYERS)):
        gradient, big, channel_all[l], gain_all[l] = layer_backward(
            plan, gradient, weights[l], saved_all[l], masks
        )
        g_col_rec, g_gates, g_out, g_col_mlp, g_down = (g.astype(BF) for g in big)

        def by_owner(g):
            return g.reshape(tp, seq, -1, g.shape[1]).swapaxes(0, 1).reshape(seq, -1, g.shape[1])

        def shares(g):
            return over_seq(by_owner(g)).reshape(tp, -1, g.shape[1])

        rec = exchange(shares(g_col_rec))
        mlp = exchange(shares(g_col_mlp))

        def columns(parts, at, width):
            return jnp.moveaxis(parts[:, :, at : at + width], 0, 1).reshape(parts.shape[1], -1)

        gates = over_seq(g_gates.reshape(seq, -1, 2 * head))
        outs[l] = [
            columns(rec, 0, head),
            columns(rec, head, head),
            gates[:, :head],
            gates[:, head:],
            over_seq(g_out.reshape(seq, -1, g_out.shape[1])),
            columns(mlp, 0, units),
            columns(mlp, units, units),
            over_seq(g_down.reshape(seq, -1, g_down.shape[1])),
        ]
        outs[l] = [to_owners(plan, g.astype(F32), 0) for g in outs[l]]
    big = [jnp.stack([outs[l][i] for l in range(LAYERS)]) for i in range(8)]

    channel = jnp.stack(channel_all).reshape(LAYERS * 8, seq, head // seq)
    channel = lax.psum_scatter(channel, "seq", scatter_dimension=1, tiled=False)
    channel = to_owners(plan, channel, 1).reshape(LAYERS, 8, -1)
    gains = lax.psum(jnp.stack(gain_all), ("rep", "seq"))
    width = gains.shape[2] // (plan.rep * seq)
    owner = lax.axis_index(("rep", "seq"))
    gains = lax.dynamic_slice_in_dim(gains, owner * width, width, 2)
    return (
        residual.astype(BF),
        gradient,
        gains,
        big[0],
        big[1],
        channel[:, :CONV],
        channel[:, CONV],
        big[2],
        big[3],
        channel[:, CONV + 1 : CONV + 3],
        channel[:, CONV + 3],
        big[4],
        big[5],
        big[6],
        big[7],
    )


def solution(mesh):
    tokens = P(("rep", "seq"), None)
    rows = P(None, "seq", None)
    last3 = P(None, None, "seq")
    last2 = P(None, "seq")
    own_rows = P(None, ("rep", "seq"), None)
    own3 = P(None, None, ("rep", "seq"))
    own2 = P(None, ("rep", "seq"))

    def whole(*args):
        heads = args[9].shape[1] // args[9].shape[2]
        plan = Plan(mesh, heads)
        return jax.shard_map(
            partial(local, plan),
            mesh=mesh,
            in_specs=(
                tokens, tokens, P("rep"), P("rep"), last3, rows, rows, last3, last2, rows, rows,
                last3, last2, rows, rows, rows, rows,
            ),
            out_specs=(
                tokens, tokens, own3, own_rows, own_rows, own3, own2, own_rows, own_rows, own3,
                own2, own_rows, own_rows, own_rows, own_rows,
            ),
            check_vma=False,
        )(*args)

    return whole
```

time: 6350 us -> 1950 us (0.31)
  waiting for transfers between devices: 4560 us -> 1190 us
  local copies, waits for them, and re-layouts: 851 us -> 92 us
  other arithmetic: 274 us -> 83.4 us
  matrix products: 361 us -> 227 us
    reduce_scatter x16 -> x19, waiting for transfers between devices: 3090 us -> 707 us  [the longest x8 460 us: scatter_plane(): lax.psum_scatter(value, 'rep', scatter_dimension=0, tiled=True, axis_inde...]
    all_gather x16 -> x14, waiting for transfers between devices: 1460 us -> 473 us  [the longest x8 287 us: gather_plane(): lax.all_gather(value, 'rep', axis=0, tiled=True, axis_index_groups=plan.t...]
    slice x241 -> x36, local copies, waits for them, and re-layouts: 510 us -> 39.6 us  [the longest x4 17.3 us: col(): return lax.dynamic_slice_in_dim(weight[layer], t * width, width, 1)]
    pad x112 -> x0, local copies, waits for them, and re-layouts: 209 us -> none  [the longest x56 111 us: layer_forward(): lax.associative_scan(chain, (retain, inflow), axis=0)]
    dot_general x48 -> x34, matrix products: 361 us -> 227 us  [the longest x12 84.6 us: dot_nt(): lax.dot_general(a, b, (((1,), (1,)), ((), ())), preferred_element_type=F32)]
    add x97 -> x4, other arithmetic: 96.6 us -> 5.86 us  [the longest x1 3.73 us: layer_backward(): grad_middle + part]
    rev x4 -> x0, local copies, waits for them, and re-layouts: 67.2 us -> none  [layer_backward(): lax.associative_scan(chain, (retain_next, grad_direct), reverse=True, axi...]
    all_gather x18 -> x10, blocking collectives: 245 us -> 214 us  [the longest x2 97.6 us: local(): gates = lax.all_gather(gates, 'seq', axis=0, tiled=True)]
  transfers between devices with their start and end apart: 37 -> 44, of which waited for: 27 -> 31; matrix products, arithmetic and copies ran while one was open for 12% -> 12% of each run, Pallas kernels for 0% -> 0%
where the time goes in v1:
time: 1950 us; the launch traced here: 1940 us
  waiting for transfers between devices  1190 us (61%)
  blocking collectives  271 us (14%)
  matrix products  227 us (12%)
  local copies, waits for them, and re-layouts  92 us (5%)
  other arithmetic  83.4 us (4%)
  starting transfers between devices  33.8 us (2%)
  Pallas kernels  25.7 us (1%)
    reduce_scatter x8, waiting for transfers between devices, scatter_plane(): lax.psum_scatter(value, 'rep', scatter_dimension=0, tiled=True, axis_inde...  460 us
    all_gather x8, waiting for transfers between devices, gather_plane(): lax.all_gather(value, 'rep', axis=0, tiled=True, axis_index_groups=plan.t...  287 us
    reduce_scatter x10, waiting for transfers between devices, over_seq(): return lax.psum_scatter(value, 'seq', scatter_dimension=0, tiled=False)  234 us
    all_gather x2, waiting for transfers between devices, local(): lax.all_gather(col_mlp, 'seq', axis=0, tiled=True)  131 us
    all_gather x2, blocking collectives, local(): gates = lax.all_gather(gates, 'seq', axis=0, tiled=True)  97.6 us
    dot_general x12, matrix products, dot_nt(): lax.dot_general(a, b, (((1,), (1,)), ((), ())), preferred_element_type=F32)  84.6 us
    dot_general x10, matrix products, dot_tn(): lax.dot_general(a, b, (((0,), (0,)), ((), ())), preferred_element_type=F32)  71.5 us
    dot_general x12, matrix products, dot(): return jnp.dot(a, b, preferred_element_type=F32)  70.6 us
  transfers between devices with their start and end apart: 44, of which 31 were waited for; matrix products, arithmetic and copies ran while one was open for 12% of the time, Pallas kernels for 0%

profile of v1, /device:TPU:0, one launch (start us, length us, event | category | flops | bytes accessed | tf_op | source)
XLA Modules:
  0.0 1942.4 jit_solution(10517542076188796819)
XLA Ops:
  65.8 26.0 %all_gather.92 = bf16[256,512]{1,0:T(8,128)(2,1)S(1)} all-gather(bf16[64,512]{1,0:T(8,128)(2,1)S(1)} %collective-permute-done.1), channel_id=1, replica_groups=mesh['rep'=8,'seq'=4] {'seq'}, dimensions={0}, use_global_device_ids=true | all-gather | bytes 327680 | tf_op jit(solution)/shard_map/all_gather | solution.py:334
  92.8 28.8 %all-gather.22.cloned.1.call-done = bf16[2048,1536]{1,0:T(8,128)(2,1)} async-done(((bf16[256,1536]{1,0:T(8,128)(2,1)}), bf16[2048,1536]{1,0:T(8,128)(2,1)}) %all-gather.22.cloned.1.call-update) | async-done | bytes 6291472 | tf_op jit(solution)/shard_map/all_gather | solution.py:60
  131.2 18.1 all_gather.95
  194.4 46.7 %reduce-scatter.20.cloned.1.call-done = bf16[256,1536]{1,0:T(8,128)(2,1)} async-done(((bf16[2048,1536]{1,0:T(8,128)(2,1)}), bf16[256,1536]{1,0:T(8,128)(2,1)}) %reduce-scatter.20.cloned.1.call-update) | async-done | bytes 786448 | tf_op jit(solution)/shard_map/reduce_scatter | solution.py:64
  246.3 66.8 %all-gather.28.cloned.1.call-done = bf16[1536,1152]{1,0:T(8,128)(2,1)} async-done(((bf16[384,1152]{1,0:T(8,128)(2,1)}), bf16[1536,1152]{1,0:T(8,128)(2,1)}) %all-gather.28.cloned.1.call-update) | async-done | bytes 3538960 | tf_op jit(solution)/shard_map/all_gather | solution.py:346
  313.2 46.6 %all-gather.26.cloned.1.call-done = bf16[2048,1536]{1,0:T(8,128)(2,1)} async-done(((bf16[256,1536]{1,0:T(8,128)(2,1)}), bf16[2048,1536]{1,0:T(8,128)(2,1)}) %all-gather.26.cloned.1.call-update) | async-done | bytes 6291472 | tf_op jit(solution)/shard_map/all_gather | solution.py:60
  377.4 24.9 %all-gather.30.cloned.1.call-done = bf16[576,1536]{1,0:T(8,128)(2,1)} async-done(((bf16[144,1536]{1,0:T(8,128)(2,1)}), bf16[576,1536]{1,0:T(8,128)(2,1)}) %all-gather.30.cloned.1.call-update) | async-done | bytes 1769488 | tf_op jit(solution)/shard_map/all_gather | solution.py:347
  412.9 58.9 %reduce-scatter.22.cloned.1.call-done = bf16[256,1536]{1,0:T(8,128)(2,1)} async-done(((bf16[2048,1536]{1,0:T(8,128)(2,1)}), bf16[256,1536]{1,0:T(8,128)(2,1)}) %reduce-scatter.22.cloned.1.call-update) | async-done | bytes 786448 | tf_op jit(solution)/shard_map/reduce_scatter | solution.py:64
  480.0 71.7 %all_gather.101 = bf16[256,512]{1,0:T(8,128)(2,1)S(1)} all-gather(bf16[64,512]{1,0:T(8,128)(2,1)S(1)} %collective-permute-done.4), channel_id=1, replica_groups=mesh['rep'=8,'seq'=4] {'seq'}, dimensions={0}, use_global_device_ids=true | all-gather | bytes 327680 | tf_op jit(solution)/shard_map/all_gather | solution.py:334
  551.7 34.0 %all-gather.32.cloned.1.call-done = bf16[2048,1536]{1,0:T(8,128)(2,1)} async-done(((bf16[256,1536]{1,0:T(8,128)(2,1)}), bf16[2048,1536]{1,0:T(8,128)(2,1)}) %all-gather.32.cloned.1.call-update) | async-done | bytes 6291472 | tf_op jit(solution)/shard_map/all_gather | solution.py:60
  595.5 18.1 all_gather.104
  648.0 57.4 %reduce-scatter.24.cloned.1.call-done = bf16[256,1536]{1,0:T(8,128)(2,1)} async-done(((bf16[2048,1536]{1,0:T(8,128)(2,1)}), bf16[256,1536]{1,0:T(8,128)(2,1)}) %reduce-scatter.24.cloned.1.call-update) | async-done | bytes 786448 | tf_op jit(solution)/shard_map/reduce_scatter | solution.py:64
  713.3 64.3 %all-gather.38.cloned.1.call-done = bf16[1536,1152]{1,0:T(8,128)(2,1)} async-done(((bf16[384,1152]{1,0:T(8,128)(2,1)}), bf16[1536,1152]{1,0:T(8,128)(2,1)}) %all-gather.38.cloned.1.call-update) | async-done | bytes 3538960 | tf_op jit(solution)/shard_map/all_gather | solution.py:346
  777.6 46.6 %all-gather.36.cloned.1.call-done = bf16[2048,1536]{1,0:T(8,128)(2,1)} async-done(((bf16[256,1536]{1,0:T(8,128)(2,1)}), bf16[2048,1536]{1,0:T(8,128)(2,1)}) %all-gather.36.cloned.1.call-update) | async-done | bytes 6291472 | tf_op jit(solution)/shard_map/all_gather | solution.py:60
  837.1 29.7 %all-gather.40.cloned.1.call-done = bf16[576,1536]{1,0:T(8,128)(2,1)} async-done(((bf16[144,1536]{1,0:T(8,128)(2,1)}), bf16[576,1536]{1,0:T(8,128)(2,1)}) %all-gather.40.cloned.1.call-update) | async-done | bytes 1769488 | tf_op jit(solution)/shard_map/all_gather | solution.py:347
  866.8 46.9 %all-gather.42.cloned.1.call-done = bf16[2048,1536]{1,0:T(8,128)(2,1)} async-done(((bf16[256,1536]{1,0:T(8,128)(2,1)}), bf16[2048,1536]{1,0:T(8,128)(2,1)}) %all-gather.42.cloned.1.call-update) | async-done | bytes 6291472 | tf_op jit(solution)/shard_map/all_gather | solution.py:60
  939.0 61.9 %reduce-scatter.28.cloned.1.call-done = bf16[256,1536]{1,0:T(8,128)(2,1)} async-done(((bf16[2048,1536]{1,0:T(8,128)(2,1)}), bf16[256,1536]{1,0:T(8,128)(2,1)}) %reduce-scatter.28.cloned.1.call-update) | async-done | bytes 786448 | tf_op jit(solution)/shard_map/reduce_scatter | solution.py:64
  1012.9 38.4 %all-gather.44.cloned.1.call-done = bf16[2048,1536]{1,0:T(8,128)(2,1)} async-done(((bf16[256,1536]{1,0:T(8,128)(2,1)}), bf16[2048,1536]{1,0:T(8,128)(2,1)}) %all-gather.44.cloned.1.call-update) | async-done | bytes 6291472 | tf_op jit(solution)/shard_map/all_gather | solution.py:60
  1115.8 49.6 %reduce-scatter.30.cloned.1.call-done = bf16[256,1536]{1,0:T(8,128)(2,1)} async-done(((bf16[2048,1536]{1,0:T(8,128)(2,1)}), bf16[256,1536]{1,0:T(8,128)(2,1)}) %reduce-scatter.30.cloned.1.call-update) | async-done | bytes 786448 | tf_op jit(solution)/shard_map/reduce_scatter | solution.py:64
  1167.6 63.2 %reduce-scatter.26.cloned.1.call-done = bf16[256,1536]{1,0:T(8,128)(2,1)} async-done(((bf16[2048,1536]{1,0:T(8,128)(2,1)}), bf16[256,1536]{1,0:T(8,128)(2,1)}) %reduce-scatter.26.cloned.1.call-update) | async-done | bytes 786448 | tf_op jit(solution)/shard_map/reduce_scatter | solution.py:64
  1235.5 45.6 %all-gather.46.cloned.1.call-done = bf16[2048,1536]{1,0:T(8,128)(2,1)} async-done(((bf16[256,1536]{1,0:T(8,128)(2,1)}), bf16[2048,1536]{1,0:T(8,128)(2,1)}) %all-gather.46.cloned.1.call-update) | async-done | bytes 6291472 | tf_op jit(solution)/shard_map/all_gather | solution.py:60
  1307.2 61.8 %reduce-scatter.32.cloned.1.call-done = bf16[256,1536]{1,0:T(8,128)(2,1)} async-done(((bf16[2048,1536]{1,0:T(8,128)(2,1)}), bf16[256,1536]{1,0:T(8,128)(2,1)}) %reduce-scatter.32.cloned.1.call-update) | async-done | bytes 786448 | tf_op jit(solution)/shard_map/reduce_scatter | solution.py:64
  1524.0 17.1 all_to_all.20
  1553.5 42.2 %reduce-scatter.50.cloned.1.call-done = bf16[1,384,1152]{2,1,0:T(8,128)(2,1)} async-done(((bf16[4,384,1152]{2,1,0:T(8,128)(2,1)}), bf16[1,384,1152]{2,1,0:T(8,128)(2,1)}) %reduce-scatter.50.cloned.1.call-update) | async-done | bytes 884752 | tf_op jit(solution)/shard_map/reduce_scatter | solution.py:364
  1599.8 18.3 reduce-scatter.44.cloned.1.call-done
  1620.9 36.5 %reduce-scatter.56.cloned.1.call-done = bf16[1,144,1536]{2,1,0:T(8,128)(2,1)} async-done(((bf16[4,144,1536]{2,1,0:T(8,128)(2,1)}), bf16[1,144,1536]{2,1,0:T(8,128)(2,1)}) %reduce-scatter.56.cloned.1.call-update) | async-done | bytes 442384 | tf_op jit(solution)/shard_map/reduce_scatter | solution.py:364
  1657.5 40.4 %reduce-scatter.54.cloned.1.call-done = bf16[1,144,1536]{2,1,0:T(8,128)(2,1)} async-done(((bf16[4,144,1536]{2,1,0:T(8,128)(2,1)}), bf16[1,144,1536]{2,1,0:T(8,128)(2,1)}) %reduce-scatter.54.cloned.1.call-update) | async-done | bytes 442384 | tf_op jit(solution)/shard_map/reduce_scatter | solution.py:364
  1740.2 34.3 %reduce-scatter.36.cloned.1.call-done = bf16[1,384,512]{2,1,0:T(8,128)(2,1)} async-done(((bf16[4,384,512]{2,1,0:T(8,128)(2,1)}), bf16[1,384,512]{2,1,0:T(8,128)(2,1)}) %reduce-scatter.36.cloned.1.call-update) | async-done | bytes 393232 | tf_op jit(solution)/shard_map/reduce_scatter | solution.py:364
  1778.9 20.8 %reduce-scatter.48.cloned.1.call-done = bf16[1,64,1536]{2,1,0:T(8,128)(2,1)} async-done(((bf16[4,64,1536]{2,1,0:T(8,128)(2,1)}), bf16[1,64,1536]{2,1,0:T(8,128)(2,1)}) %reduce-scatter.48.cloned.1.call-update) | async-done | bytes 196624 | tf_op jit(solution)/shard_map/reduce_scatter | solution.py:364
  1799.7 25.5 %reduce-scatter.46.cloned.1.call-done = bf16[1,64,1536]{2,1,0:T(8,128)(2,1)} async-done(((bf16[4,64,1536]{2,1,0:T(8,128)(2,1)}), bf16[1,64,1536]{2,1,0:T(8,128)(2,1)}) %reduce-scatter.46.cloned.1.call-update) | async-done | bytes 196624 | tf_op jit(solution)/shard_map/reduce_scatter | solution.py:364
  1829.5 60.0 %reduce-scatter.34.cloned.1.call-done = bf16[256,1536]{1,0:T(8,128)(2,1)} async-done(((bf16[2048,1536]{1,0:T(8,128)(2,1)}), bf16[256,1536]{1,0:T(8,128)(2,1)}) %reduce-scatter.34.cloned.1.call-update) | async-done | bytes 786448 | tf_op jit(solution)/shard_map/reduce_scatter | solution.py:64
  1891.4 39.5 %psum.7 = f32[2,2,1536]{2,1,0:T(2,128)S(1)} all-reduce(f32[2,2,1536]{2,1,0:T(2,128)S(1)} %pad_maximum_fusion.26), channel_id=1, replica_groups=mesh['rep'=8,'seq'=4] {'rep','seq'}, use_global_device_ids=true, to_apply=%region_20.22 | all-reduce | flops 6144 | bytes 49152 | tf_op jit(solution)/shard_map/psum | solution.py:406
  (616 shorter events, 583.3 us)
Async XLA Ops:
  14.8 106.8 %all-gather.22.cloned.1.call-start = ((), (), s32[]{:S(2)}) async-start(), calls=%async_computation.23 | async-start | bytes 7077888 | tf_op jit(solution)/shard_map/all_gather | solution.py:60
  32.2 208.8 %reduce-scatter.20.cloned.1.call-start = ((), (), s32[]{:S(2)}) async-start(), calls=%async_computation.25 | async-start | bytes 7077888 | tf_op jit(solution)/shard_map/reduce_scatter | solution.py:64
  180.7 132.5 %all-gather.28.cloned.1.call-start = ((), (), s32[]{:S(2)}) async-start(), calls=%async_computation.27 | async-start | bytes 4423680 | tf_op jit(solution)/shard_map/all_gather | solution.py:346
  194.3 165.4 %all-gather.26.cloned.1.call-start = ((), (), s32[]{:S(2)}) async-start(), calls=%async_computation.26 | async-start | bytes 7077888 | tf_op jit(solution)/shard_map/all_gather | solution.py:60
  244.4 157.8 %all-gather.30.cloned.1.call-start = ((), (), s32[]{:S(2)}) async-start(), calls=%async_computation.28 | async-start | bytes 2211840 | tf_op jit(solution)/shard_map/all_gather | solution.py:347
  246.3 225.5 %reduce-scatter.22.cloned.1.call-start = ((), (), s32[]{:S(2)}) async-start(), calls=%async_computation.29 | async-start | bytes 7077888 | tf_op jit(solution)/shard_map/reduce_scatter | solution.py:64
  411.0 140.6 %all-gather.34.cloned.1.call-start = ((), (), s32[]{:S(2)}) async-start(), calls=%async_computation.31 | async-start | bytes 1966080 | tf_op jit(solution)/shard_map/all_gather | solution.py:342
  412.9 172.9 %all-gather.32.cloned.1.call-start = ((), (), s32[]{:S(2)}) async-start(), calls=%async_computation.30 | async-start | bytes 7077888 | tf_op jit(solution)/shard_map/all_gather | solution.py:60
  475.7 229.7 %reduce-scatter.24.cloned.1.call-start = ((), (), s32[]{:S(2)}) async-start(), calls=%async_computation.32 | async-start | bytes 7077888 | tf_op jit(solution)/shard_map/reduce_scatter | solution.py:64
  645.0 132.6 %all-gather.38.cloned.1.call-start = ((), (), s32[]{:S(2)}) async-start(), calls=%async_computation.34 | async-start | bytes 4423680 | tf_op jit(solution)/shard_map/all_gather | solution.py:346
  647.9 176.3 %all-gather.36.cloned.1.call-start = ((), (), s32[]{:S(2)}) async-start(), calls=%async_computation.33 | async-start | bytes 7077888 | tf_op jit(solution)/shard_map/all_gather | solution.py:60
  708.9 157.9 %all-gather.40.cloned.1.call-start = ((), (), s32[]{:S(2)}) async-start(), calls=%async_computation.35 | async-start | bytes 2211840 | tf_op jit(solution)/shard_map/all_gather | solution.py:347
  710.7 203.0 %all-gather.42.cloned.1.call-start = ((), (), s32[]{:S(2)}) async-start(), calls=%async_computation.37 | async-start | bytes 7077888 | tf_op jit(solution)/shard_map/all_gather | solution.py:60
  713.1 287.9 %reduce-scatter.28.cloned.1.call-start = ((), (), s32[]{:S(2)}) async-start(), calls=%async_computation.38 | async-start | bytes 7077888 | tf_op jit(solution)/shard_map/reduce_scatter | solution.py:64
  939.0 112.3 %all-gather.44.cloned.1.call-start = ((), (), s32[]{:S(2)}) async-start(), calls=%async_computation.39 | async-start | bytes 7077888 | tf_op jit(solution)/shard_map/all_gather | solution.py:60
  1005.6 159.9 %reduce-scatter.30.cloned.1.call-start = ((), (), s32[]{:S(2)}) async-start(), calls=%async_computation.40 | async-start | bytes 7077888 | tf_op jit(solution)/shard_map/reduce_scatter | solution.py:64
  1105.5 125.4 %reduce-scatter.26.cloned.1.call-start = ((), (), s32[]{:S(2)}) async-start(), calls=%async_computation.36 | async-start | bytes 7077888 | tf_op jit(solution)/shard_map/reduce_scatter | solution.py:64
  1115.7 165.4 %all-gather.46.cloned.1.call-start = ((), (), s32[]{:S(2)}) async-start(), calls=%async_computation.41 | async-start | bytes 7077888 | tf_op jit(solution)/shard_map/all_gather | solution.py:60
  1235.5 133.5 %reduce-scatter.32.cloned.1.call-start = ((), (), s32[]{:S(2)}) async-start(), calls=%async_computation.42 | async-start | bytes 7077888 | tf_op jit(solution)/shard_map/reduce_scatter | solution.py:64
  1307.1 135.2 %all-gather.48.cloned.1.call-start = ((), (), s32[]{:S(2)}) async-start(), calls=%async_computation.43 | async-start | bytes 7077888 | tf_op jit(solution)/shard_map/all_gather | solution.py:60
  1373.9 150.2 %reduce-scatter.52.cloned.1.call-start = ((), (), s32[]{:S(2)}) async-start(), calls=%async_computation.53 | async-start | bytes 4423680 | tf_op jit(solution)/shard_map/reduce_scatter | solution.py:364
  1388.1 153.0 %reduce-scatter.38.cloned.1.call-start = ((), (), s32[]{:S(2)}) async-start(), calls=%async_computation.46 | async-start | bytes 1966080 | tf_op jit(solution)/shard_map/reduce_scatter | solution.py:364
  1397.1 198.6 %reduce-scatter.50.cloned.1.call-start = ((), (), s32[]{:S(2)}) async-start(), calls=%async_computation.52 | async-start | bytes 4423680 | tf_op jit(solution)/shard_map/reduce_scatter | solution.py:364
  1412.2 205.9 %reduce-scatter.44.cloned.1.call-start = ((), (), s32[]{:S(2)}) async-start(), calls=%async_computation.49 | async-start | bytes 327680 | tf_op jit(solution)/shard_map/reduce_scatter | solution.py:364
  1416.4 241.1 %reduce-scatter.56.cloned.1.call-start = ((), (), s32[]{:S(2)}) async-start(), calls=%async_computation.55 | async-start | bytes 2211840 | tf_op jit(solution)/shard_map/reduce_scatter | solution.py:364
  1425.2 272.6 %reduce-scatter.54.cloned.1.call-start = ((), (), s32[]{:S(2)}) async-start(), calls=%async_computation.54 | async-start | bytes 2211840 | tf_op jit(solution)/shard_map/reduce_scatter | solution.py:364
  1439.1 279.6 %reduce-scatter.40.cloned.1.call-start = ((), (), s32[]{:S(2)}) async-start(), calls=%async_computation.47 | async-start | bytes 40960 | tf_op jit(solution)/shard_map/reduce_scatter | solution.py:404
  1490.2 248.5 %reduce-scatter.42.cloned.1.call-start = ((), (), s32[]{:S(2)}) async-start(), calls=%async_computation.48 | async-start | bytes 327680 | tf_op jit(solution)/shard_map/reduce_scatter | solution.py:364
  1493.6 281.0 %reduce-scatter.36.cloned.1.call-start = ((), (), s32[]{:S(2)}) async-start(), calls=%async_computation.45 | async-start | bytes 1966080 | tf_op jit(solution)/shard_map/reduce_scatter | solution.py:364
  1504.5 295.2 %reduce-scatter.48.cloned.1.call-start = ((), (), s32[]{:S(2)}) async-start(), calls=%async_computation.51 | async-start | bytes 983040 | tf_op jit(solution)/shard_map/reduce_scatter | solution.py:364
  1510.4 314.8 %reduce-scatter.46.cloned.1.call-start = ((), (), s32[]{:S(2)}) async-start(), calls=%async_computation.50 | async-start | bytes 983040 | tf_op jit(solution)/shard_map/reduce_scatter | solution.py:364
  1516.1 373.4 %reduce-scatter.34.cloned.1.call-start = ((), (), s32[]{:S(2)}) async-start(), calls=%async_computation.44 | async-start | bytes 7077888 | tf_op jit(solution)/shard_map/reduce_scatter | solution.py:64
  (154 other events, 5011.0 us)
Sparse Core Ops, SparseCore 0:
  14.9 59.5 all-gather.23
  76.9 44.6 all-gather.21
  180.8 60.2 reduce-scatter.19
  243.2 69.9 all-gather.27
  315.6 44.1 all-gather.25
  361.9 40.3 all-gather.29
  411.2 60.6 reduce-scatter.21
  474.0 64.7 all-gather.33
  541.3 44.3 all-gather.31
  645.1 60.2 reduce-scatter.23
  707.6 69.9 all-gather.37
  780.1 44.1 all-gather.35
  826.5 40.3 all-gather.39
  869.3 44.3 all-gather.41
  939.1 61.7 reduce-scatter.27
  1005.7 45.4 all-gather.43
  1105.6 59.8 reduce-scatter.29
  1169.0 61.7 reduce-scatter.25
  1235.6 45.4 all-gather.45
  1307.2 61.7 reduce-scatter.31
  1374.0 45.4 all-gather.47
  1421.9 67.4 reduce-scatter.51
  1492.4 35.6 reduce-scatter.37
  1530.4 65.3 reduce-scatter.49
  1598.1 19.9 reduce-scatter.43
  1620.8 36.5 reduce-scatter.55
  1660.3 37.4 reduce-scatter.53
  1700.6 18.0 reduce-scatter.39
  1740.9 33.5 reduce-scatter.35
  1777.4 22.2 reduce-scatter.47
  1802.6 22.5 reduce-scatter.45
  1828.4 61.0 reduce-scatter.33
  (1 shorter events, 17.6 us)

commit v2 on v1

--- a/solution.py
+++ b/solution.py
@@ -96,6 +96,461 @@
 def shifted(plan, value, step):
     pairs = [(z, z + step) for z in range(plan.seq) if 0 <= z + step < plan.seq]
     return lax.ppermute(value, "seq", pairs)
+
+
+MESH = pl.DeviceIdType.MESH
+ANY = pl.BlockSpec(memory_space=pl.ANY)
+VM = pl.BlockSpec(memory_space=pltpu.VMEM)
+TP = 8
+
+
+class Net:
+    def __init__(self):
+        rep = lax.axis_index("rep")
+        self.z = lax.axis_index("seq")
+        self.t = lax.rem(rep, TP)
+        self.base = rep - self.t
+        chip = self.t // 2
+        self.k = lax.rem(self.t, 2)
+        self.b0 = lax.rem(chip, 2)
+        self.b1 = chip // 2
+
+    def slot(self, m, s):
+        b0 = lax.rem(self.b0 + m % 2, 2)
+        b1 = lax.rem(self.b1 + m // 2, 2)
+        return (b1 * 2 + b0) * 2 + lax.rem(self.k + s, 2)
+
+    def device(self, m, s):
+        return (self.base + self.slot(m, s), self.z)
+
+    def enter(self, extra=()):
+        barrier = pltpu.get_barrier_semaphore()
+        devices = [self.device(1, 0), self.device(2, 0), self.device(0, 1)] + list(extra)
+        for device in devices:
+            pl.semaphore_signal(barrier, inc=1, device_id=device, device_id_type=MESH)
+        pl.semaphore_wait(barrier, len(devices))
+
+
+def remote(src, dst, send, recv, device):
+    return pltpu.make_async_remote_copy(
+        src_ref=src, dst_ref=dst, send_sem=send, recv_sem=recv, device_id=device,
+        device_id_type=MESH,
+    )
+
+
+class Gather:
+    def __init__(self, net, full, send, recv):
+        self.net, self.full, self.send, self.recv = net, full, send, recv
+        half = full.shape[1] // 2
+        a, b, whole = pl.ds(0, half), pl.ds(half, half), pl.ds(0, 2 * half)
+        x, y, sib = net.device(1, 0), net.device(2, 0), net.device(0, 1)
+        self.plan = [
+            (0, a, x, 1), (0, b, y, 2), (0, b, x, 1), (0, a, y, 2), (2, b, x, 3), (1, a, y, 3),
+            (0, whole, sib, 0), (1, whole, sib, 1), (2, whole, sib, 2), (3, whole, sib, 3),
+        ]
+
+    def copy(self, i):
+        m, rows, to, _ = self.plan[i]
+        at = self.full.at[self.net.slot(m, 0), rows]
+        return remote(at, at, self.send.at[i], self.recv.at[i], to)
+
+    def arrived(self, i):
+        _, rows, to, m = self.plan[i]
+        at = self.full.at[self.net.slot(m, 0 if i < 6 else 1), rows]
+        remote(at, at, self.send.at[i], self.recv.at[i], to).wait_recv()
+
+    def begin(self):
+        for i in (0, 1, 2, 3, 6):
+            self.copy(i).start()
+
+    def before(self, n):
+        if n == 1:
+            self.arrived(6)
+        if n == 2:
+            self.arrived(0)
+            self.copy(5).start()
+            self.arrived(1)
+            self.copy(4).start()
+            self.arrived(2)
+            self.copy(7).start()
+        if n == 3:
+            self.arrived(7)
+        if n == 4:
+            self.arrived(3)
+            self.copy(8).start()
+        if n == 5:
+            self.arrived(8)
+        if n == 6:
+            self.arrived(4)
+            self.arrived(5)
+            self.copy(9).start()
+        if n == 7:
+            self.arrived(9)
+
+    def finish(self):
+        for i in range(10):
+            self.copy(i).wait_send()
+
+
+class Scatter:
+    def __init__(self, net, part, near, wide, far, send, recv):
+        self.net, self.part, self.near = net, part, near
+        self.wide, self.far, self.send, self.recv = wide, far, send, recv
+        self.rows = part.shape[2]
+        half = self.rows // 2
+        a, b, whole = pl.ds(0, half), pl.ds(half, half), pl.ds(0, 2 * half)
+        self.a, self.b = a, b
+        x, y, sib = net.device(1, 0), net.device(2, 0), net.device(0, 1)
+        self.plan = [
+            (part.at[1, m], near.at[m], sib) for m in range(4)
+        ] + [
+            (part.at[0, 3, a], wide.at[0], x),
+            (part.at[0, 3, b], wide.at[1], y),
+            (part.at[0, 1, a], far.at[0, a], x),
+            (part.at[0, 2, b], far.at[1, b], y),
+            (part.at[0, 1, b], far.at[0, b], x),
+            (part.at[0, 2, a], far.at[1, a], y),
+        ]
+
+    def copy(self, i):
+        src, dst, to = self.plan[i]
+        return remote(src, dst, self.send.at[i], self.recv.at[i], to)
+
+    def add(self, m, start, count, other):
+        def some(i, carry):
+            at = pl.ds(pl.multiple_of(start + i * 64, 64), 64)
+            from_at = pl.ds(pl.multiple_of(i * 64, 64), 64)
+            total = self.part[0, m, at].astype(F32) + other[from_at].astype(F32)
+            self.part[0, m, at] = total.astype(BF)
+            return carry
+
+        lax.fori_loop(0, count // 64, some, 0)
+
+    def after(self, n):
+        if n == 1:
+            self.copy(0).start()
+        if n == 3:
+            self.copy(1).start()
+        if n == 4:
+            self.copy(1).wait_recv()
+            self.add(1, 0, self.rows, self.near.at[1])
+            self.copy(6).start()
+        if n == 5:
+            self.copy(2).start()
+        if n == 6:
+            self.copy(2).wait_recv()
+            self.add(2, 0, self.rows, self.near.at[2])
+            self.copy(7).start()
+        if n == 7:
+            self.copy(3).start()
+
+    def corner(self):
+        self.copy(3).wait_recv()
+        self.add(3, 0, self.rows, self.near.at[3])
+        self.copy(4).start()
+        self.copy(5).start()
+
+    def edges(self):
+        half = self.rows // 2
+        self.copy(4).wait_recv()
+        self.add(2, 0, half, self.wide.at[0])
+        self.copy(9).start()
+        self.copy(5).wait_recv()
+        self.add(1, half, half, self.wide.at[1])
+        self.copy(8).start()
+        self.copy(0).wait_recv()
+
+    def finish(self):
+        for i in (6, 7, 8, 9):
+            self.copy(i).wait_recv()
+        for i in range(10):
+            self.copy(i).wait_send()
+
+    def total(self, at):
+        own = self.part[0, 0, at].astype(F32) + self.near[0, at].astype(F32)
+        return own + self.far[0, at].astype(F32) + self.far[1, at].astype(F32)
+
+
+def plane_scratch(rows, width):
+    dma = pltpu.SemaphoreType.DMA
+    return [
+        pltpu.VMEM((TP, rows, width), BF),
+        pltpu.VMEM((2, 4, rows, width), BF),
+        pltpu.VMEM((4, rows, width), BF),
+        pltpu.VMEM((2, rows // 2, width), BF),
+        pltpu.VMEM((2, rows, width), BF),
+        dma((10,)), dma((10,)), dma((10,)), dma((10,)),
+    ]
+
+
+def steps(gather, scatter, compute):
+    def one(i, carry):
+        for n in range(1, 2 * 4):
+            @pl.when(i == n)
+            def _():
+                if gather is not None:
+                    gather.before(n)
+
+        compute(i // 2, lax.rem(i, 2))
+        for n in range(2 * 4):
+            @pl.when(i == n)
+            def _():
+                if scatter is not None:
+                    scatter.after(n)
+
+        return carry
+
+    lax.fori_loop(0, 2 * 4, one, 0)
+
+
+def end_forward(scatter, residual, gain, out, normed):
+    rows, chunk = out.shape[0], 32
+
+    def some(i, carry):
+        at = pl.ds(pl.multiple_of(i * chunk, chunk), chunk)
+        value = residual[at] + scatter.total(at)
+        out[at] = value
+        scale = lax.rsqrt(jnp.mean(value * value, axis=-1, keepdims=True) + EPSILON)
+        normed[at] = (value * scale * gain[...]).astype(BF)
+        return carry
+
+    lax.fori_loop(0, rows // chunk, some, 0)
+
+
+def end_backward(scatter, upstream, values, gain, grad, grad_low, grad_gain):
+    rows, chunk = grad.shape[0], 32
+    grad_gain[...] = jnp.zeros_like(grad_gain)
+
+    def some(i, carry):
+        at = pl.ds(pl.multiple_of(i * chunk, chunk), chunk)
+        value, given = values[at], scatter.total(at)
+        scale = lax.rsqrt(jnp.mean(value * value, axis=-1, keepdims=True) + EPSILON)
+        scaled = given * gain[...]
+        mean = jnp.mean(value * scaled, axis=-1, keepdims=True)
+        result = upstream[at] + scale * scaled - value * (scale * scale * scale * mean)
+        grad[at] = result
+        grad_low[at] = result.astype(BF)
+        grad_gain[...] += jnp.sum(given * value * scale, axis=0, keepdims=True)
+        return carry
+
+    lax.fori_loop(0, rows // chunk, some, 0)
+
+
+GELU_A = 0.7978845608028654
+GELU_B = 0.044715
+
+
+def gelu_parts(v):
+    square = v * v
+    tanh = jnp.tanh(GELU_A * (v + GELU_B * v * square))
+    half = 0.5 * (1.0 + tanh)
+    slope = half + 0.5 * v * (1.0 - tanh * tanh) * (GELU_A * (1.0 + 3.0 * GELU_B * square))
+    return v * half, slope
+
+
+def mlp_weight_copies(col_ref, down_ref, wg, wu, wd, sem):
+    seq, _, rows, _ = col_ref.shape
+    copies = []
+    for i, w in enumerate((wg, wu)):
+        for z in range(seq):
+            copies.append(
+                pltpu.make_async_copy(
+                    col_ref.at[z, i], w.at[pl.ds(z * rows, rows)], sem.at[i * seq + z]
+                )
+            )
+    copies.append(pltpu.make_async_copy(down_ref, wd, sem.at[2 * seq]))
+    return copies
+
+
+def mlp_forward_kernel(
+    x_ref, residual_ref, gain_ref, col_ref, down_ref,
+    out_ref, normed_ref, full_out, gate_out, value_out,
+    full, part, near, wide, far, gs, gr, ss, sr, wg, wu, wd, gate, value, sem,
+):
+    net = Net()
+    gather = Gather(net, full, gs, gr)
+    scatter = Scatter(net, part, near, wide, far, ss, sr)
+    n = 2 * col_ref.shape[0] + 1
+    own = pltpu.make_async_copy(x_ref, full.at[net.t], sem.at[n])
+    own.start()
+    weights = mlp_weight_copies(col_ref, down_ref, wg, wu, wd, sem)
+    for copy in weights:
+        copy.start()
+    net.enter()
+    own.wait()
+    gather.begin()
+    for copy in weights:
+        copy.wait()
+
+    def compute(m, s):
+        slot = net.slot(m, s)
+        x = full[slot]
+        up_gate, up_value = dot(x, wg[...]), dot(x, wu[...])
+        gate[slot] = up_gate.astype(BF)
+        value[slot] = up_value.astype(BF)
+        hidden = glu_product(up_gate, up_value).astype(BF)
+        part[s, m] = dot(hidden, wd[...]).astype(BF)
+
+    steps(gather, scatter, compute)
+    saves = [
+        pltpu.make_async_copy(full, full_out, sem.at[n + 1]),
+        pltpu.make_async_copy(gate, gate_out, sem.at[n + 2]),
+        pltpu.make_async_copy(value, value_out, sem.at[n + 3]),
+    ]
+    for copy in saves:
+        copy.start()
+    scatter.corner()
+    scatter.edges()
+    scatter.finish()
+    end_forward(scatter, residual_ref, gain_ref, out_ref, normed_ref)
+    gather.finish()
+    for copy in saves:
+        copy.wait()
+
+
+def mlp_forward(x, residual, gain, col, down):
+    rows, width = x.shape
+    seq, _, part_rows, units = col.shape
+    shape = jax.ShapeDtypeStruct
+    return pl.pallas_call(
+        mlp_forward_kernel,
+        in_specs=[ANY, VM, VM, ANY, ANY],
+        out_specs=[VM, VM, ANY, ANY, ANY],
+        out_shape=[
+            shape((rows, width), F32),
+            shape((rows, width), BF),
+            shape((TP, rows, width), BF),
+            shape((TP, rows, units), BF),
+            shape((TP, rows, units), BF),
+        ],
+        scratch_shapes=plane_scratch(rows, width)
+        + [
+            pltpu.VMEM((width, units), BF),
+            pltpu.VMEM((width, units), BF),
+            pltpu.VMEM((units, width), BF),
+            pltpu.VMEM((TP, rows, units), BF),
+            pltpu.VMEM((TP, rows, units), BF),
+            pltpu.SemaphoreType.DMA((2 * seq + 5,)),
+        ],
+        compiler_params=pltpu.CompilerParams(
+            collective_id=1, has_side_effects=True, vmem_limit_bytes=58 << 20
+        ),
+        cost_estimate=pl.CostEstimate(
+            flops=60 * 10**9, bytes_accessed=30 << 20, transcendentals=0
+        ),
+        name="mlp_forward",
+    )(x, residual, gain.reshape(1, -1), col, down)
+
+
+def mlp_backward_kernel(
+    g_ref, upstream_ref, values_ref, gain_ref, col_ref, down_ref, x_ref, gate_ref, value_ref,
+    grad_ref, low_ref, gain_out, gcol_ref, gdown_ref,
+    full, part, near, wide, far, gs, gr, ss, sr, wg, wu, wd, xs, gate, value, hid, sem,
+):
+    net = Net()
+    gather = Gather(net, full, gs, gr)
+    scatter = Scatter(net, part, near, wide, far, ss, sr)
+    seq = col_ref.shape[0]
+    n = 2 * seq + 1
+    own = pltpu.make_async_copy(g_ref, full.at[net.t], sem.at[n])
+    own.start()
+    loads = mlp_weight_copies(col_ref, down_ref, wg, wu, wd, sem) + [
+        pltpu.make_async_copy(gate_ref, gate, sem.at[n + 1]),
+        pltpu.make_async_copy(value_ref, value, sem.at[n + 2]),
+    ]
+    late = pltpu.make_async_copy(x_ref, xs, sem.at[n + 3])
+    for copy in loads + [late]:
+        copy.start()
+    net.enter()
+    own.wait()
+    gather.begin()
+    for copy in loads:
+        copy.wait()
+    rows = full.shape[1]
+
+    def compute(m, s):
+        slot = net.slot(m, s)
+        at = pl.ds(pl.multiple_of(slot * rows, rows), rows)
+        grad_hidden = dot_nt(full[slot], wd[...])
+        act, slope = gelu_parts(gate[at].astype(F32))
+        up_value = value[at].astype(F32)
+        hid[at] = (act * up_value).astype(BF)
+        grad_gate = (grad_hidden * up_value * slope).astype(BF)
+        grad_value = (grad_hidden * act).astype(BF)
+        gate[at] = grad_gate
+        value[at] = grad_value
+        part[s, m] = (dot_nt(grad_gate, wg[...]) + dot_nt(grad_value, wu[...])).astype(BF)
+
+    steps(gather, scatter, compute)
+    late.wait()
+    scatter.corner()
+    width = full.shape[2]
+    own_rows = width // (TP * seq)
+    tile = 2 * seq * own_rows
+
+    def columns(j, carry):
+        x = xs[:, pl.ds(pl.multiple_of(j * tile, 128), tile)]
+        for i, grads in enumerate((gate, value)):
+            product = dot_tn(x, grads[...]).astype(BF)
+            for r in range(2):
+                for z in range(seq):
+                    low = (r * seq + z) * own_rows
+                    at = pl.ds(pl.multiple_of((2 * j + r) * own_rows, own_rows), own_rows)
+                    gcol_ref[z, i, at] = product[low : low + own_rows]
+        return carry
+
+    lax.fori_loop(0, TP // 2, columns, 0)
+    scatter.edges()
+
+    tokens = full.shape[0] * rows
+    third = width // 3
+
+    for j in range(3):
+        at = pl.ds(j * third, third)
+        gdown_ref[:, at] = dot_tn(hid[...], full[:, :, at].reshape(tokens, third)).astype(BF)
+    scatter.finish()
+    end_backward(scatter, upstream_ref, values_ref, gain_ref, grad_ref, low_ref, gain_out)
+    gather.finish()
+
+
+def mlp_backward(g, upstream, values, gain, col, down, x, gate, value):
+    rows, width = g.shape
+    seq, _, part_rows, units = col.shape
+    tokens = TP * rows
+    shape = jax.ShapeDtypeStruct
+    return pl.pallas_call(
+        mlp_backward_kernel,
+        in_specs=[ANY, VM, VM, VM, ANY, ANY, ANY, ANY, ANY],
+        out_specs=[VM, VM, VM, VM, VM],
+        out_shape=[
+            shape((rows, width), F32),
+            shape((rows, width), BF),
+            shape((1, width), F32),
+            shape((seq, 2, part_rows, units), BF),
+            shape((units, width), BF),
+        ],
+        scratch_shapes=plane_scratch(rows, width)
+        + [
+            pltpu.VMEM((width, units), BF),
+            pltpu.VMEM((width, units), BF),
+            pltpu.VMEM((units, width), BF),
+            pltpu.VMEM((tokens, width), BF),
+            pltpu.VMEM((tokens, units), BF),
+            pltpu.VMEM((tokens, units), BF),
+            pltpu.VMEM((tokens, units), BF),
+            pltpu.SemaphoreType.DMA((2 * seq + 5,)),
+        ],
+        compiler_params=pltpu.CompilerParams(
+            collective_id=2, has_side_effects=True, vmem_limit_bytes=60 << 20
+        ),
+        cost_estimate=pl.CostEstimate(
+            flops=70 * 10**9, bytes_accessed=30 << 20, transcendentals=0
+        ),
+        name="mlp_backward",
+    )(
+        g, upstream, values, gain.reshape(1, -1), col, down, x.reshape(tokens, width),
+        gate.reshape(tokens, units), value.reshape(tokens, units),
+    )
 
 
 def scan_body(reverse, rows, slots, a_ref, b_ref, h_ref, q_ref):
@@ -166,11 +621,10 @@
     return restart.reshape(-1, 1), fwd, back
 
 
-def layer_forward(plan, residual, w, masks):
+def layer_forward(plan, residual, normed, w, next_gain, masks):
     restart, same_fwd, _ = masks
     slots, rows = plan.tp, residual.shape[0]
     head = w["rate"].shape[0]
-    normed = rms_scale(residual, w["gain"][0]).astype(BF)
     x = gather_plane(plan, normed)
     both = dot(x, w["col_rec"])
     branch, stream = both[:, :head], both[:, head:]
@@ -201,39 +655,29 @@
     joined = glu_product(branch, states).astype(BF)
     middle = residual + scatter_plane(plan, dot(joined, w["out"]).astype(BF)).astype(F32)
     normed_two = rms_scale(middle, w["gain"][1]).astype(BF)
-    x_two = gather_plane(plan, normed_two)
-    up = dot(x_two, w["col_mlp"])
-    half = up.shape[1] // 2
-    hidden = glu_product(up[:, :half], up[:, half:]).astype(BF)
-    output = middle + scatter_plane(plan, dot(hidden, w["down"]).astype(BF)).astype(F32)
+    output, next_normed, x_two, gate, value = mlp_forward(
+        normed_two, middle, next_gain, w["col_mlp"], w["down"]
+    )
     saved = (
         residual, x, branch, widened, conv_low, pre_rate, pre_admit, retain, states, carry,
-        joined, middle, x_two, up, hidden,
-    )
-    return output, saved
-
-
-def layer_backward(plan, upstream, w, saved, masks):
+        joined, middle, x_two, gate, value,
+    )
+    return output, next_normed, saved
+
+
+def layer_backward(plan, upstream, upstream_low, w, saved, masks):
     (
         residual, x, branch, widened, conv_low, pre_rate, pre_admit, retain, states, carry,
-        joined, middle, x_two, up, hidden,
+        joined, middle, x_two, gate, value,
     ) = saved
     restart, same_fwd, same_back = masks
     slots, rows = plan.tp, residual.shape[0]
     seq = plan.seq
     head = w["rate"].shape[0]
-    half = up.shape[1] // 2
-    down_low = gather_plane(plan, upstream.astype(BF))
-    grad_hidden = dot_nt(down_low, w["down"])
-    _, glu_pull = jax.vjp(glu_product, up[:, :half], up[:, half:])
-    grad_up = jnp.concatenate([p.astype(BF) for p in glu_pull(grad_hidden)], 1)
-    grad_two = scatter_plane(plan, dot_nt(grad_up, w["col_mlp"]).astype(BF)).astype(F32)
-    g_down = dot_tn(hidden, down_low)
-    g_col_mlp = dot_tn(x_two, grad_up)
-    _, pull_two = jax.vjp(rms_scale, middle, w["gain"][1])
-    part, grad_gain_two = pull_two(grad_two)
-    grad_middle = upstream + part
-    mid_low = gather_plane(plan, grad_middle.astype(BF))
+    grad_middle, mid_low, grad_gain_two, g_col_mlp, g_down = mlp_backward(
+        upstream_low, upstream, middle, w["gain"][1], w["col_mlp"], w["down"], x_two, gate, value
+    )
+    mid_low = gather_plane(plan, mid_low)
     g_out = dot_tn(joined, mid_low)
     grad_joined = dot_nt(mid_low, w["out"])
     _, mix_pull = jax.vjp(glu_product, branch, states)
@@ -280,7 +724,7 @@
     _, pull_one = jax.vjp(rms_scale, residual, w["gain"][0])
     part, grad_gain_one = pull_one(grad_normed)
     channel = jnp.stack(tap_rows + [grad_bias, grad_gbias[0], grad_gbias[1], grad_decay], 0)
-    gains = jnp.stack([grad_gain_one, grad_gain_two], 0)
+    gains = jnp.stack([grad_gain_one, grad_gain_two[0]], 0)
     return grad_middle + part, (g_col_rec, g_gates, g_out, g_col_mlp, g_down), channel, gains
 
 
@@ -327,7 +771,7 @@
     weights = []
     for l in range(LAYERS):
         col_rec = jnp.concatenate([col(branch_proj, l, head), col(stream_proj, l, head)], 1)
-        col_mlp = jnp.concatenate([col(mlp_gate, l, units), col(mlp_up, l, units)], 1)
+        col_mlp = jnp.stack([col(mlp_gate, l, units), col(mlp_up, l, units)], 0)
         wide = owner_chunks(plan, jnp.concatenate([chunk(out_proj, l), chunk(mlp_down, l)], 0))
         out_rows = out_proj.shape[1] // tp
         gates = owner_chunks(plan, jnp.concatenate([chunk(rate_proj, l), chunk(admit_proj, l)], 1))
@@ -343,15 +787,19 @@
                 rate=gates[:, :head],
                 admit=gates[:, head:],
                 out=lax.all_gather(wide[:out_rows], "seq", axis=0, tiled=True),
-                col_mlp=lax.all_gather(col_mlp, "seq", axis=0, tiled=True),
+                col_mlp=lax.all_gather(col_mlp, "seq"),
                 down=lax.all_gather(wide[out_rows:], "seq", axis=0, tiled=True),
             )
         )
 
     residual = block_input.astype(F32)
+    normed = rms_scale(residual, gains[0, 0]).astype(BF)
     saved_all = []
     for l in range(LAYERS):
-        residual, saved = layer_forward(plan, residual, weights[l], masks)
+        next_gain = gains[(l + 1) % LAYERS, 0]
+        residual, normed, saved = layer_forward(
+            plan, residual, normed, weights[l], next_gain, masks
+        )
         saved_all.append(saved)
     positions = z * rows + jnp.arange(rows, dtype=jnp.int32)
     inside = (positions >= offsets[0]) & (positions < offsets[0] + lengths[0])
@@ -370,31 +818,29 @@
 
     for l in reversed(range(LAYERS)):
         gradient, big, channel_all[l], gain_all[l] = layer_backward(
-            plan, gradient, weights[l], saved_all[l], masks
+            plan, gradient, gradient.astype(BF), weights[l], saved_all[l], masks
         )
         g_col_rec, g_gates, g_out, g_col_mlp, g_down = (g.astype(BF) for g in big)
 
         def by_owner(g):
             return g.reshape(tp, seq, -1, g.shape[1]).swapaxes(0, 1).reshape(seq, -1, g.shape[1])
 
-        def shares(g):
-            return over_seq(by_owner(g)).reshape(tp, -1, g.shape[1])
-
-        rec = exchange(shares(g_col_rec))
-        mlp = exchange(shares(g_col_mlp))
-
-        def columns(parts, at, width):
-            return jnp.moveaxis(parts[:, :, at : at + width], 0, 1).reshape(parts.shape[1], -1)
+        rec = exchange(over_seq(by_owner(g_col_rec)).reshape(tp, -1, 2 * head))
+        mlp = over_seq(g_col_mlp.reshape(seq, -1, units)).reshape(2, tp, -1, units)
+        mlp = exchange(mlp.swapaxes(0, 1).reshape(tp, -1, units)).reshape(tp, 2, -1, units)
+
+        def columns(parts):
+            return jnp.moveaxis(parts, 0, 1).reshape(parts.shape[1], -1)
 
         gates = over_seq(g_gates.reshape(seq, -1, 2 * head))
         outs[l] = [
-            columns(rec, 0, head),
-            columns(rec, head, head),
+            columns(rec[:, :, :head]),
+            columns(rec[:, :, head:]),
             gates[:, :head],
             gates[:, head:],
             over_seq(g_out.reshape(seq, -1, g_out.shape[1])),
-            columns(mlp, 0, units),
-            columns(mlp, units, units),
+            columns(mlp[:, 0]),
+            columns(mlp[:, 1]),
             over_seq(g_down.reshape(seq, -1, g_down.shape[1])),
         ]
         outs[l] = [to_owners(plan, g.astype(F32), 0) for g in outs[l]]

time: 1950 us -> 1580 us (0.81)
  waiting for transfers between devices: 1190 us -> 706 us
  Pallas kernels: 25.7 us -> 302 us
  matrix products: 227 us -> 94.4 us
    pallas_call x0 -> x4, Pallas kernels: none -> 277 us  [the longest x2 143 us: mlp_backward(): pl.pallas_call(mlp_backward_kernel, in_specs=[ANY, VM, VM, VM, ANY, ANY,...]
    reduce_scatter x8 -> x4, waiting for transfers between devices: 460 us -> 236 us  [scatter_plane(): lax.psum_scatter(value, 'rep', scatter_dimension=0, tiled=True, axis_inde...]
    all_gather x8 -> x4, waiting for transfers between devices: 287 us -> 77 us  [gather_plane(): lax.all_gather(value, 'rep', axis=0, tiled=True, axis_index_groups=plan.t...]
    all_gather x2, waiting for transfers between devices: 131 us -> 19.6 us  [local(): lax.all_gather(col_mlp, 'seq')]
    dot_general x12 -> x8, matrix products: 84.6 us -> 35.2 us  [dot_nt(): lax.dot_general(a, b, (((1,), (1,)), ((), ())), preferred_element_type=F32)]
    dot_general x12 -> x8, matrix products: 70.6 us -> 28.9 us  [dot(): return jnp.dot(a, b, preferred_element_type=F32)]
    dot_general x10 -> x6, matrix products: 71.5 us -> 30.2 us  [dot_tn(): lax.dot_general(a, b, (((0,), (0,)), ((), ())), preferred_element_type=F32)]
    reduce_scatter x10, waiting for transfers between devices: 234 us -> 273 us  [over_seq(): return lax.psum_scatter(value, 'seq', scatter_dimension=0, tiled=False)]
  transfers between devices with their start and end apart: 44 -> 36, of which waited for: 31 -> 24; matrix products, arithmetic and copies ran while one was open for 12% -> 12% of each run, Pallas kernels for 0% -> 5%
where the time goes in v2:
time: 1580 us; the launch traced here: 1570 us
  waiting for transfers between devices  706 us (45%)
  Pallas kernels  302 us (19%)
  blocking collectives  266 us (17%)
  matrix products  94.4 us (6%)
  local copies, waits for them, and re-layouts  86.5 us (5%)
  other arithmetic  66.8 us (4%)
  starting transfers between devices  33.2 us (2%)
  between operations  18.1 us (1%)
    reduce_scatter x10, waiting for transfers between devices, over_seq(): return lax.psum_scatter(value, 'seq', scatter_dimension=0, tiled=False)  273 us
    reduce_scatter x4, waiting for transfers between devices, scatter_plane(): lax.psum_scatter(value, 'rep', scatter_dimension=0, tiled=True, axis_inde...  236 us
    pallas_call x2, Pallas kernels, mlp_backward(): pl.pallas_call(mlp_backward_kernel, in_specs=[ANY, VM, VM, VM, ANY, ANY,...  143 us
    pallas_call x2, Pallas kernels, mlp_forward(): pl.pallas_call(mlp_forward_kernel, in_specs=[ANY, VM, VM, ANY, ANY], out_...  134 us
    all_gather x4, waiting for transfers between devices, gather_plane(): lax.all_gather(value, 'rep', axis=0, tiled=True, axis_index_groups=plan.t...  77 us
    all_gather x2, waiting for transfers between devices, local(): lax.all_gather(wide[out_rows:], 'seq', axis=0, tiled=True)  76.1 us
    all_gather x2, blocking collectives, local(): gates = lax.all_gather(gates, 'seq', axis=0, tiled=True)  62.7 us
    all_gather x2, blocking collectives, local(): lax.all_gather(wide[:out_rows], 'seq', axis=0, tiled=True)  59.6 us
  transfers between devices with their start and end apart: 36, of which 24 were waited for; matrix products, arithmetic and copies ran while one was open for 12% of the time, Pallas kernels for 5%

profile of v2, /device:TPU:0, one launch (start us, length us, event | category | flops | bytes accessed | tf_op | source)
XLA Modules:
  0.0 1574.1 jit_solution(8906481474974498358)
XLA Ops:
  15.5 15.6 all-gather.7
  67.3 16.7 %all-gather.8 = s32[8,1,2]{2,1,0:T(1,128)S(1)} all-gather(s32[1,1,2]{2,1,0:T(1,128)S(1)} %add_bitcast_fusion), channel_id=1, replica_groups=mesh['rep'=8,'seq'=4] {'rep'}, dimensions={0}, use_global_device_ids=true | all-gather | bytes 72 | tf_op jit(solution)/shard_map/all_gather | solution.py:60
  86.9 19.2 %all_gather.86 = bf16[256,512]{1,0:T(8,128)(2,1)} all-gather(bf16[64,512]{1,0:T(8,128)(2,1)} %collective-permute-done.1), channel_id=1, replica_groups=mesh['rep'=8,'seq'=4] {'seq'}, dimensions={0}, use_global_device_ids=true | all-gather | bytes 327680 | tf_op jit(solution)/shard_map/all_gather | solution.py:778
  126.5 29.8 %all_gather.89 = bf16[256,1536]{1,0:T(8,128)(2,1)S(1)} all-gather(bf16[64,1536]{1,0:T(8,128)(2,1)S(1)} %slice.660), channel_id=1, replica_groups=mesh['rep'=8,'seq'=4] {'seq'}, dimensions={0}, use_global_device_ids=true | all-gather | bytes 983040 | tf_op jit(solution)/shard_map/all_gather | solution.py:789
  168.3 13.9 all-gather.1
  207.8 58.0 %reduce-scatter.16.cloned.1.call-done = bf16[256,1536]{1,0:T(8,128)(2,1)} async-done(((bf16[2048,1536]{1,0:T(8,128)(2,1)}), bf16[256,1536]{1,0:T(8,128)(2,1)}) %reduce-scatter.16.cloned.1.call-update) | async-done | bytes 786448 | tf_op jit(solution)/shard_map/reduce_scatter | solution.py:64
  269.0 39.1 %all-gather.24.cloned.1.call-done.down_ref = bf16[576,1536]{1,0:T(8,128)(2,1)} async-done(((bf16[144,1536]{1,0:T(8,128)(2,1)}), bf16[576,1536]{1,0:T(8,128)(2,1)}) %all-gather.24.cloned.1.call-update) | async-done | bytes 1769488 | tf_op jit(solution)/shard_map/all_gather | solution.py:791
  308.2 66.8 %mlp_forward.2 = (f32[256,1536]{1,0:T(8,128)}, bf16[256,1536]{1,0:T(8,128)(2,1)}, bf16[8,256,1536]{2,1,0:T(8,128)(2,1)}, bf16[8,256,576]{2,1,0:T(8,128)(2,1)}, bf16[8,256,576]{2,1,0:T(8,128)(2,1)}) custom-call(bf16[256,1536]{1,0:T(8,128)(2,1)} %get-tuple-element.142.x_ref, f32[256,1536]{1,0:T(8,128)} %get-tuple-element.141.residual_ref.values_ref, ...), custom_call_target="tpu_custom_call" | custom-call | flops 60000002048 | bytes 31457280 | tf_op jit(solution)/shard_map/mlp_forward/pallas_call | solution.py:415
  380.5 43.5 %all_gather.95 = bf16[256,512]{1,0:T(8,128)(2,1)S(1)} all-gather(bf16[64,512]{1,0:T(8,128)(2,1)S(1)} %collective-permute-done.4), channel_id=1, replica_groups=mesh['rep'=8,'seq'=4] {'seq'}, dimensions={0}, use_global_device_ids=true | all-gather | bytes 327680 | tf_op jit(solution)/shard_map/all_gather | solution.py:778
  441.2 29.8 %all_gather.98 = bf16[256,1536]{1,0:T(8,128)(2,1)S(1)} all-gather(bf16[64,1536]{1,0:T(8,128)(2,1)S(1)} %slice.691), channel_id=1, replica_groups=mesh['rep'=8,'seq'=4] {'seq'}, dimensions={0}, use_global_device_ids=true | all-gather | bytes 983040 | tf_op jit(solution)/shard_map/all_gather | solution.py:789
  482.9 14.1 all-gather.3
  522.5 58.6 %reduce-scatter.18.cloned.1.call-done = bf16[256,1536]{1,0:T(8,128)(2,1)} async-done(((bf16[2048,1536]{1,0:T(8,128)(2,1)}), bf16[256,1536]{1,0:T(8,128)(2,1)}) %reduce-scatter.18.cloned.1.call-update) | async-done | bytes 786448 | tf_op jit(solution)/shard_map/reduce_scatter | solution.py:64
  585.9 37.0 %all-gather.30.cloned.1.call-done.down_ref = bf16[576,1536]{1,0:T(8,128)(2,1)} async-done(((bf16[144,1536]{1,0:T(8,128)(2,1)}), bf16[576,1536]{1,0:T(8,128)(2,1)}) %all-gather.30.cloned.1.call-update) | async-done | bytes 1769488 | tf_op jit(solution)/shard_map/all_gather | solution.py:791
  622.9 66.8 %mlp_forward.3 = (f32[256,1536]{1,0:T(8,128)}, bf16[256,1536]{1,0:T(8,128)(2,1)}, bf16[8,256,1536]{2,1,0:T(8,128)(2,1)}, bf16[8,256,576]{2,1,0:T(8,128)(2,1)}, bf16[8,256,576]{2,1,0:T(8,128)(2,1)}) custom-call(bf16[256,1536]{1,0:T(8,128)(2,1)} %multiply_convert_fusion.2.x_ref, f32[256,1536]{1,0:T(8,128)} %copy-done.41, ...), custom_call_target="tpu_custom_call" | custom-call | flops 60000002048 | bytes 31457280 | tf_op jit(solution)/shard_map/mlp_forward/pallas_call | solution.py:415
  689.7 71.2 %mlp_backward.2 = (f32[256,1536]{1,0:T(8,128)}, bf16[256,1536]{1,0:T(8,128)(2,1)}, f32[1,1536]{1,0:T(1,128)}, bf16[4,2,384,576]{3,2,1,0:T(8,128)(2,1)}, bf16[576,1536]{1,0:T(8,128)(2,1)}) custom-call(bf16[256,1536]{1,0:T(8,128)(2,1)} %get-tuple-element.148.g_ref, f32[256,1536]{1,0:T(8,128)} %get-tuple-element.147.upstream_ref, f32[256,1536]{1,0:T(8,128)} %copy-done.41, ...), custom_call_target="tpu_custom_call" | custom-call | flops 70000001024 | bytes 31457280 | tf_op jit(solution)/shard_map/mlp_backward/pallas_call | solution.py:521
  768.2 36.5 %all-gather.32.cloned.1.call-done = bf16[2048,1536]{1,0:T(8,128)(2,1)} async-done(((bf16[256,1536]{1,0:T(8,128)(2,1)}), bf16[2048,1536]{1,0:T(8,128)(2,1)}) %all-gather.32.cloned.1.call-update) | async-done | bytes 6291472 | tf_op jit(solution)/shard_map/all_gather | solution.py:60
  859.8 59.3 %reduce-scatter.20.cloned.1.call-done = bf16[256,1536]{1,0:T(8,128)(2,1)} async-done(((bf16[2048,1536]{1,0:T(8,128)(2,1)}), bf16[256,1536]{1,0:T(8,128)(2,1)}) %reduce-scatter.20.cloned.1.call-update) | async-done | bytes 786448 | tf_op jit(solution)/shard_map/reduce_scatter | solution.py:64
  922.9 71.8 %mlp_backward.3 = (f32[256,1536]{1,0:T(8,128)}, bf16[256,1536]{1,0:T(8,128)(2,1)}, f32[1,1536]{1,0:T(1,128)}, bf16[4,2,384,576]{3,2,1,0:T(8,128)(2,1)}, bf16[576,1536]{1,0:T(8,128)(2,1)}) custom-call(bf16[256,1536]{1,0:T(8,128)(2,1)} %get-tuple-element.112.g_ref, f32[256,1536]{1,0:T(8,128)} %get-tuple-element.113.upstream_ref, ...), custom_call_target="tpu_custom_call" | custom-call | flops 70000001024 | bytes 31457280 | tf_op jit(solution)/shard_map/mlp_backward/pallas_call | solution.py:521
  1016.7 23.6 %all-gather.34.cloned.1.call-done = bf16[2048,1536]{1,0:T(8,128)(2,1)} async-done(((bf16[256,1536]{1,0:T(8,128)(2,1)}), bf16[2048,1536]{1,0:T(8,128)(2,1)}) %all-gather.34.cloned.1.call-update) | async-done | bytes 6291472 | tf_op jit(solution)/shard_map/all_gather | solution.py:60
  1123.8 17.2 %all_to_all.20 = bf16[8,96,576]{2,1,0:T(8,128)(2,1)S(1)} all-to-all(bf16[8,96,576]{2,1,0:T(8,128)(2,1)S(1)} %bitcast.624), channel_id=1, replica_groups=mesh['rep'=8,'seq'=4] {'rep'}, dimensions={0} | all-to-all | bytes 1769472 | tf_op jit(solution)/shard_map/all_to_all | solution.py:815
  1141.1 14.5 reduce-scatter.26.cloned.1.call-done
  1161.2 68.4 %reduce-scatter.38.cloned.1.call-done = bf16[1,768,576]{2,1,0:T(8,128)(2,1)} async-done(((bf16[4,768,576]{2,1,0:T(8,128)(2,1)}), bf16[1,768,576]{2,1,0:T(8,128)(2,1)}) %reduce-scatter.38.cloned.1.call-update) | async-done | bytes 884752 | tf_op jit(solution)/shard_map/reduce_scatter | solution.py:812
  1235.6 16.8 %reduce-scatter.32.cloned.1.call-done = bf16[1,64,512]{2,1,0:T(8,128)(2,1)} async-done(((bf16[4,64,512]{2,1,0:T(8,128)(2,1)}), bf16[1,64,512]{2,1,0:T(8,128)(2,1)}) %reduce-scatter.32.cloned.1.call-update) | async-done | bytes 65552 | tf_op jit(solution)/shard_map/reduce_scatter | solution.py:812
  1254.1 37.0 %reduce-scatter.44.cloned.1.call-done = bf16[1,144,1536]{2,1,0:T(8,128)(2,1)} async-done(((bf16[4,144,1536]{2,1,0:T(8,128)(2,1)}), bf16[1,144,1536]{2,1,0:T(8,128)(2,1)}) %reduce-scatter.44.cloned.1.call-update) | async-done | bytes 442384 | tf_op jit(solution)/shard_map/reduce_scatter | solution.py:812
  1291.2 40.0 %reduce-scatter.42.cloned.1.call-done = bf16[1,144,1536]{2,1,0:T(8,128)(2,1)} async-done(((bf16[4,144,1536]{2,1,0:T(8,128)(2,1)}), bf16[1,144,1536]{2,1,0:T(8,128)(2,1)}) %reduce-scatter.42.cloned.1.call-update) | async-done | bytes 442384 | tf_op jit(solution)/shard_map/reduce_scatter | solution.py:812
  1337.2 14.6 reduce-scatter.28.cloned.1.call-done
  1355.7 16.3 %reduce-scatter.30.cloned.1.call-done = bf16[1,64,512]{2,1,0:T(8,128)(2,1)} async-done(((bf16[4,64,512]{2,1,0:T(8,128)(2,1)}), bf16[1,64,512]{2,1,0:T(8,128)(2,1)}) %reduce-scatter.30.cloned.1.call-update) | async-done | bytes 65552 | tf_op jit(solution)/shard_map/reduce_scatter | solution.py:812
  1373.5 34.5 %reduce-scatter.24.cloned.1.call-done = bf16[1,384,512]{2,1,0:T(8,128)(2,1)} async-done(((bf16[4,384,512]{2,1,0:T(8,128)(2,1)}), bf16[1,384,512]{2,1,0:T(8,128)(2,1)}) %reduce-scatter.24.cloned.1.call-update) | async-done | bytes 393232 | tf_op jit(solution)/shard_map/reduce_scatter | solution.py:812
  1412.5 20.6 %reduce-scatter.36.cloned.1.call-done = bf16[1,64,1536]{2,1,0:T(8,128)(2,1)} async-done(((bf16[4,64,1536]{2,1,0:T(8,128)(2,1)}), bf16[1,64,1536]{2,1,0:T(8,128)(2,1)}) %reduce-scatter.36.cloned.1.call-update) | async-done | bytes 196624 | tf_op jit(solution)/shard_map/reduce_scatter | solution.py:812
  1433.1 25.3 %reduce-scatter.34.cloned.1.call-done = bf16[1,64,1536]{2,1,0:T(8,128)(2,1)} async-done(((bf16[4,64,1536]{2,1,0:T(8,128)(2,1)}), bf16[1,64,1536]{2,1,0:T(8,128)(2,1)}) %reduce-scatter.34.cloned.1.call-update) | async-done | bytes 196624 | tf_op jit(solution)/shard_map/reduce_scatter | solution.py:812
  1462.7 60.2 %reduce-scatter.22.cloned.1.call-done = bf16[256,1536]{1,0:T(8,128)(2,1)} async-done(((bf16[2048,1536]{1,0:T(8,128)(2,1)}), bf16[256,1536]{1,0:T(8,128)(2,1)}) %reduce-scatter.22.cloned.1.call-update) | async-done | bytes 786448 | tf_op jit(solution)/shard_map/reduce_scatter | solution.py:64
  1525.5 39.6 %psum.7 = f32[2,2,1536]{2,1,0:T(2,128)S(1)} all-reduce(f32[2,2,1536]{2,1,0:T(2,128)S(1)} %pad_maximum_fusion.20), channel_id=1, replica_groups=mesh['rep'=8,'seq'=4] {'rep','seq'}, use_global_device_ids=true, to_apply=%region_12.14 | all-reduce | flops 6144 | bytes 49152 | tf_op jit(solution)/shard_map/psum | solution.py:852
  (578 shorter events, 379.8 us)
Async XLA Ops:
  7.2 99.9 %all-gather.22.cloned.1.call-start = ((), (), s32[]{:S(2)}) async-start(), calls=%async_computation.20 | async-start | bytes 1966080 | tf_op jit(solution)/shard_map/all_gather | solution.py:786
  15.2 101.4 %all-gather.20.cloned.1.call-start = ((), (), s32[]{:S(2)}) async-start(), calls=%async_computation.19 | async-start | bytes 7077888 | tf_op jit(solution)/shard_map/all_gather | solution.py:60
  35.1 166.7 %all-gather.36.cloned.1.call-start = ((), (), s32[]{:S(2)}) async-start(), calls=%async_computation.42 | async-start | bytes 4423680 | tf_op jit(solution)/shard_map/all_gather | solution.py:790
  37.3 49.6 %collective-permute-start.1 = (bf16[64,512]{1,0:T(8,128)(2,1)}, bf16[64,512]{1,0:T(8,128)(2,1)}, u32[]{:S(2)}, u32[]{:S(2)}) collective-permute-start(bf16[64,512]{1,0:T(8,128)(2,1)} %pad_maximum_fusion.18), channel_id=1, source_target_pairs={{0,0},{1,8},{2,16},{3,24},{4,1},{5,9},{6,17},{7,25},{8,2},{9,10},{... | collective-permute-start | bytes 196616 | tf_op jit(solution)/shard_map/ppermute | solution.py:77
  48.9 216.8 %reduce-scatter.16.cloned.1.call-start = ((), (), s32[]{:S(2)}) async-start(), calls=%async_computation.21 | async-start | bytes 7077888 | tf_op jit(solution)/shard_map/reduce_scatter | solution.py:64
  60.8 45.3 %collective-permute-start.2 = (bf16[208,1536]{1,0:T(8,128)(2,1)}, bf16[208,1536]{1,0:T(8,128)(2,1)}, u32[]{:S(2)}, u32[]{:S(2)}) collective-permute-start(bf16[208,1536]{1,0:T(8,128)(2,1)} %pad_maximum_fusion.14), channel_id=1, source_target_pairs={{0,0},{1,8},{2,16},{3,24},{4,1},{5,9},{6,17},{7,25},{8,2},{9,10},{... | collective-permute-start | bytes 1916936 | tf_op jit(solution)/shard_map/ppermute | solution.py:77
  122.9 33.4 %collective-permute-start = (f32[8,3,256]{2,1,0:T(4,128)S(1)}, f32[8,3,256]{2,1,0:T(4,128)S(1)}, u32[]{:S(2)}, u32[]{:S(2)}) collective-permute-start(f32[8,3,256]{2,1,0:T(4,128)S(1)} %slice.636), channel_id=1, source_target_pairs={{0,1},{1,2},{2,3},{4,5},{5,6},{6,7},{8,9},{9,10},{10,11},{12,13},{... | collective-permute-start | bytes 73736 | tf_op jit(solution)/shard_map/ppermute | solution.py:98
  188.7 119.5 %all-gather.24.cloned.1.call-start = ((), (), s32[]{:S(2)}) async-start(), calls=%async_computation.22 | async-start | bytes 2211840 | tf_op jit(solution)/shard_map/all_gather | solution.py:791
  190.6 233.4 %all-gather.28.cloned.1.call-start = ((), (), s32[]{:S(2)}) async-start(), calls=%async_computation.24 | async-start | bytes 1966080 | tf_op jit(solution)/shard_map/all_gather | solution.py:786
  192.5 238.9 %all-gather.26.cloned.1.call-start = ((), (), s32[]{:S(2)}) async-start(), calls=%async_computation.23 | async-start | bytes 7077888 | tf_op jit(solution)/shard_map/all_gather | solution.py:60
  374.9 141.6 %all-gather.38.cloned.1.call-start = ((), (), s32[]{:S(2)}) async-start(), calls=%async_computation.43 | async-start | bytes 4423680 | tf_op jit(solution)/shard_map/all_gather | solution.py:790
  376.5 204.6 %reduce-scatter.18.cloned.1.call-start = ((), (), s32[]{:S(2)}) async-start(), calls=%async_computation.25 | async-start | bytes 7077888 | tf_op jit(solution)/shard_map/reduce_scatter | solution.py:64
  377.7 46.2 %collective-permute-start.5 = (bf16[208,1536]{1,0:T(8,128)(2,1)S(1)}, bf16[208,1536]{1,0:T(8,128)(2,1)S(1)}, u32[]{:S(2)}, u32[]{:S(2)}) collective-permute-start(bf16[208,1536]{1,0:T(8,128)(2,1)S(1)} %pad_maximum_fusion.15), channel_id=1, source_target_pairs={{0,0},{1,8},{2,16},{3,24},{4,1},{5,9},{6,17},{7,25},{8,2},{9,10},{... | collective-permute-start | bytes 1916936 | tf_op jit(solution)/shard_map/ppermute | solution.py:77
  503.3 119.5 %all-gather.30.cloned.1.call-start = ((), (), s32[]{:S(2)}) async-start(), calls=%async_computation.26 | async-start | bytes 2211840 | tf_op jit(solution)/shard_map/all_gather | solution.py:791
  504.2 300.5 %all-gather.32.cloned.1.call-start = ((), (), s32[]{:S(2)}) async-start(), calls=%async_computation.27 | async-start | bytes 7077888 | tf_op jit(solution)/shard_map/all_gather | solution.py:60
  760.9 158.2 %reduce-scatter.20.cloned.1.call-start = ((), (), s32[]{:S(2)}) async-start(), calls=%async_computation.28 | async-start | bytes 7077888 | tf_op jit(solution)/shard_map/reduce_scatter | solution.py:64
  859.1 181.2 %all-gather.34.cloned.1.call-start = ((), (), s32[]{:S(2)}) async-start(), calls=%async_computation.29 | async-start | bytes 7077888 | tf_op jit(solution)/shard_map/all_gather | solution.py:60
  994.7 127.7 %reduce-scatter.40.cloned.1.call-start = ((), (), s32[]{:S(2)}) async-start(), calls=%async_computation.39 | async-start | bytes 4915200 | tf_op jit(solution)/shard_map/reduce_scatter | solution.py:812
  995.3 160.3 %reduce-scatter.26.cloned.1.call-start = ((), (), s32[]{:S(2)}) async-start(), calls=%async_computation.32 | async-start | bytes 1966080 | tf_op jit(solution)/shard_map/reduce_scatter | solution.py:812
  1003.8 225.8 %reduce-scatter.38.cloned.1.call-start = ((), (), s32[]{:S(2)}) async-start(), calls=%async_computation.38 | async-start | bytes 4915200 | tf_op jit(solution)/shard_map/reduce_scatter | solution.py:812
  1004.4 248.0 %reduce-scatter.32.cloned.1.call-start = ((), (), s32[]{:S(2)}) async-start(), calls=%async_computation.35 | async-start | bytes 327680 | tf_op jit(solution)/shard_map/reduce_scatter | solution.py:812
  1007.6 283.6 %reduce-scatter.44.cloned.1.call-start = ((), (), s32[]{:S(2)}) async-start(), calls=%async_computation.41 | async-start | bytes 2211840 | tf_op jit(solution)/shard_map/reduce_scatter | solution.py:812
  1008.1 323.0 %reduce-scatter.42.cloned.1.call-start = ((), (), s32[]{:S(2)}) async-start(), calls=%async_computation.40 | async-start | bytes 2211840 | tf_op jit(solution)/shard_map/reduce_scatter | solution.py:812
  1013.5 338.3 %reduce-scatter.28.cloned.1.call-start = ((), (), s32[]{:S(2)}) async-start(), calls=%async_computation.33 | async-start | bytes 40960 | tf_op jit(solution)/shard_map/reduce_scatter | solution.py:850
  1087.9 284.1 %reduce-scatter.30.cloned.1.call-start = ((), (), s32[]{:S(2)}) async-start(), calls=%async_computation.34 | async-start | bytes 327680 | tf_op jit(solution)/shard_map/reduce_scatter | solution.py:812
  1091.0 316.9 %reduce-scatter.24.cloned.1.call-start = ((), (), s32[]{:S(2)}) async-start(), calls=%async_computation.31 | async-start | bytes 1966080 | tf_op jit(solution)/shard_map/reduce_scatter | solution.py:812
  1103.9 329.2 %reduce-scatter.36.cloned.1.call-start = ((), (), s32[]{:S(2)}) async-start(), calls=%async_computation.37 | async-start | bytes 983040 | tf_op jit(solution)/shard_map/reduce_scatter | solution.py:812
  1109.8 348.6 %reduce-scatter.34.cloned.1.call-start = ((), (), s32[]{:S(2)}) async-start(), calls=%async_computation.36 | async-start | bytes 983040 | tf_op jit(solution)/shard_map/reduce_scatter | solution.py:812
  1115.5 407.3 %reduce-scatter.22.cloned.1.call-start = ((), (), s32[]{:S(2)}) async-start(), calls=%async_computation.30 | async-start | bytes 7077888 | tf_op jit(solution)/shard_map/reduce_scatter | solution.py:64
  1155.6 76.2 %all-to-all-start.1 = ((bf16[8,48,512]{2,1,0:T(8,128)(2,1)}), bf16[8,48,512]{2,1,0:T(8,128)(2,1)S(1)}, u32[]{:S(2)}, u32[]{:S(2)}) async-start(bf16[8,48,512]{2,1,0:T(8,128)(2,1)} %bitcast.642), calls=%async_computation.7 | async-start | bytes 786432 | tf_op jit(solution)/shard_map/all_to_all | solution.py:815
  1231.8 101.8 %all-to-all-start.2 = ((bf16[8,96,576]{2,1,0:T(8,128)(2,1)}), bf16[8,96,576]{2,1,0:T(8,128)(2,1)S(1)}, u32[]{:S(2)}, u32[]{:S(2)}) async-start(bf16[8,96,576]{2,1,0:T(8,128)(2,1)} %bitcast.181), calls=%async_computation.14 | async-start | bytes 1966080 | tf_op jit(solution)/shard_map/all_to_all | solution.py:815
  1407.9 52.5 %all-to-all-start = ((bf16[8,48,512]{2,1,0:T(8,128)(2,1)}), bf16[8,48,512]{2,1,0:T(8,128)(2,1)S(1)}, u32[]{:S(2)}, u32[]{:S(2)}) async-start(bf16[8,48,512]{2,1,0:T(8,128)(2,1)} %bitcast.643), calls=%async_computation.5 | async-start | bytes 786432 | tf_op jit(solution)/shard_map/all_to_all | solution.py:815
  (145 other events, 3161.5 us)
Sparse Core Ops, SparseCore 0:
  15.3 43.1 all-gather.21
  61.0 55.5 all-gather.19
  118.8 82.9 all-gather.35
  205.1 60.6 reduce-scatter.15
  267.8 40.2 all-gather.23
  310.2 35.9 all-gather.27
  375.1 56.2 all-gather.25
  433.6 82.9 all-gather.37
  520.3 60.7 reduce-scatter.17
  582.5 40.2 all-gather.29
  761.0 43.6 all-gather.31
  859.2 59.8 reduce-scatter.19
  994.8 45.5 all-gather.33
  1042.6 74.3 reduce-scatter.39
  1119.9 35.6 reduce-scatter.25
  1157.8 71.6 reduce-scatter.37
  1232.3 20.0 reduce-scatter.31
  1254.5 36.5 reduce-scatter.43
  1293.6 37.4 reduce-scatter.41
  1333.8 18.0 reduce-scatter.27
  1354.2 17.7 reduce-scatter.29
  1374.3 33.5 reduce-scatter.23
  1410.8 22.2 reduce-scatter.35
  1435.8 22.5 reduce-scatter.33
  1461.8 60.9 reduce-scatter.21

commit v3 on v2

v3 whole, which is shorter than its diff:
```python
from functools import partial

import jax
import jax.numpy as jnp
from jax import lax
from jax.experimental import pallas as pl
from jax.experimental.pallas import tpu as pltpu
from jax.sharding import PartitionSpec as P

CONV = 4
LAYERS = 2
EPSILON = 1e-06
BF = jnp.bfloat16
F32 = jnp.float32


def dot(a, b):
    return jnp.dot(a, b, preferred_element_type=F32)


def dot_tn(a, b):
    return lax.dot_general(a, b, (((0,), (0,)), ((), ())), preferred_element_type=F32)


def dot_nt(a, b):
    return lax.dot_general(a, b, (((1,), (1,)), ((), ())), preferred_element_type=F32)


def glu_product(gate_in, value_in):
    return jax.nn.gelu(gate_in, approximate=True) * value_in


class Plan:
    def __init__(self, mesh, heads):
        self.rep = mesh.shape["rep"]
        self.seq = mesh.shape["seq"]
        self.tp = min(heads, self.rep)
        self.dp = self.rep // self.tp
        tp, dp = self.tp, self.dp
        self.tp_groups = None if dp == 1 else [[d * tp + t for t in range(tp)] for d in range(dp)]
        self.dp_groups = [[d * tp + t for d in range(dp)] for t in range(tp)]


def owner_chunks(plan, value):
    tp, seq = plan.tp, plan.seq
    pairs = []
    for d in range(plan.dp):
        for j in range(tp):
            for z in range(seq):
                o = tp * z + j
                pairs.append(((d * tp + j) * seq + z, (d * tp + o // seq) * seq + o % seq))
    return lax.ppermute(value, ("rep", "seq"), pairs)


def to_owners(plan, chunk, axis):
    if plan.dp == 1:
        return chunk
    part = lax.psum_scatter(
        chunk, "rep", scatter_dimension=axis, tiled=True, axis_index_groups=plan.dp_groups
    )
    tp, seq, dp = plan.tp, plan.seq, plan.dp
    pairs = [
        ((d * tp + t) * seq + z, (t * seq + z) * dp + d)
        for d in range(dp)
        for t in range(tp)
        for z in range(seq)
    ]
    return lax.ppermute(part, ("rep", "seq"), pairs)


MESH = pl.DeviceIdType.MESH
ANY = pl.BlockSpec(memory_space=pl.ANY)
VM = pl.BlockSpec(memory_space=pltpu.VMEM)
TP = 8
LATER = 3


class Net:
    def __init__(self):
        rep = lax.axis_index("rep")
        self.z = lax.axis_index("seq")
        self.t = lax.rem(rep, TP)
        self.base = rep - self.t
        chip = self.t // 2
        self.k = lax.rem(self.t, 2)
        self.b0 = lax.rem(chip, 2)
        self.b1 = chip // 2

    def slot(self, m, s):
        b0 = lax.rem(self.b0 + m % 2, 2)
        b1 = lax.rem(self.b1 + m // 2, 2)
        return (b1 * 2 + b0) * 2 + lax.rem(self.k + s, 2)

    def device(self, m, s):
        return (self.base + self.slot(m, s), self.z)

    def enter(self, extra=()):
        barrier = pltpu.get_barrier_semaphore()
        devices = [self.device(1, 0), self.device(2, 0), self.device(0, 1)] + list(extra)
        for device in devices:
            pl.semaphore_signal(barrier, inc=1, device_id=device, device_id_type=MESH)
        pl.semaphore_wait(barrier, len(devices))


def remote(src, dst, send, recv, device):
    return pltpu.make_async_remote_copy(
        src_ref=src, dst_ref=dst, send_sem=send, recv_sem=recv, device_id=device,
        device_id_type=MESH,
    )


class Gather:
    def __init__(self, net, full, send, recv):
        self.net, self.full, self.send, self.recv = net, full, send, recv
        half = full.shape[1] // 2
        a, b, whole = pl.ds(0, half), pl.ds(half, half), pl.ds(0, 2 * half)
        x, y, sib = net.device(1, 0), net.device(2, 0), net.device(0, 1)
        self.plan = [
            (0, a, x, 1), (0, b, y, 2), (0, b, x, 1), (0, a, y, 2), (2, b, x, 3), (1, a, y, 3),
            (0, whole, sib, 0), (1, whole, sib, 1), (2, whole, sib, 2), (3, whole, sib, 3),
        ]

    def copy(self, i):
        m, rows, to, _ = self.plan[i]
        at = self.full.at[self.net.slot(m, 0), rows]
        return remote(at, at, self.send.at[i], self.recv.at[i], to)

    def arrived(self, i):
        _, rows, to, m = self.plan[i]
        at = self.full.at[self.net.slot(m, 0 if i < 6 else 1), rows]
        remote(at, at, self.send.at[i], self.recv.at[i], to).wait_recv()

    def begin(self):
        for i in (0, 1, 2, 3, 6):
            self.copy(i).start()

    def before(self, n):
        if n == 1:
            self.arrived(6)
        if n == 2:
            self.arrived(0)
            self.copy(5).start()
            self.arrived(1)
            self.copy(4).start()
            self.arrived(2)
            self.copy(7).start()
        if n == 3:
            self.arrived(7)
        if n == 4:
            self.arrived(3)
            self.copy(8).start()
        if n == 5:
            self.arrived(8)
        if n == 6:
            self.arrived(4)
            self.arrived(5)
            self.copy(9).start()
        if n == 7:
            self.arrived(9)

    def finish(self):
        for i in range(10):
            self.copy(i).wait_send()


class Scatter:
    def __init__(self, net, part, near, wide, far, send, recv):
        self.net, self.part, self.near = net, part, near
        self.wide, self.far, self.send, self.recv = wide, far, send, recv
        self.rows = part.shape[2]
        half = self.rows // 2
        a, b, whole = pl.ds(0, half), pl.ds(half, half), pl.ds(0, 2 * half)
        self.a, self.b = a, b
        x, y, sib = net.device(1, 0), net.device(2, 0), net.device(0, 1)
        self.plan = [
            (part.at[1, m], near.at[m], sib) for m in range(4)
        ] + [
            (part.at[0, 3, a], wide.at[0], x),
            (part.at[0, 3, b], wide.at[1], y),
            (part.at[0, 1, a], far.at[0, a], x),
            (part.at[0, 2, b], far.at[1, b], y),
            (part.at[0, 1, b], far.at[0, b], x),
            (part.at[0, 2, a], far.at[1, a], y),
        ]

    def copy(self, i):
        src, dst, to = self.plan[i]
        return remote(src, dst, self.send.at[i], self.recv.at[i], to)

    def add(self, m, start, count, other):
        def some(i, carry):
            at = pl.ds(pl.multiple_of(start + i * 64, 64), 64)
            from_at = pl.ds(pl.multiple_of(i * 64, 64), 64)
            total = self.part[0, m, at].astype(F32) + other[from_at].astype(F32)
            self.part[0, m, at] = total.astype(BF)
            return carry

        lax.fori_loop(0, count // 64, some, 0)

    def after(self, n):
        if n == 1:
            self.copy(0).start()
        if n == 3:
            self.copy(1).start()
        if n == 4:
            self.copy(1).wait_recv()
            self.add(1, 0, self.rows, self.near.at[1])
            self.copy(6).start()
        if n == 5:
            self.copy(2).start()
        if n == 6:
            self.copy(2).wait_recv()
            self.add(2, 0, self.rows, self.near.at[2])
            self.copy(7).start()
        if n == 7:
            self.copy(3).start()

    def corner(self):
        self.copy(3).wait_recv()
        self.add(3, 0, self.rows, self.near.at[3])
        self.copy(4).start()
        self.copy(5).start()

    def edges(self):
        half = self.rows // 2
        self.copy(4).wait_recv()
        self.add(2, 0, half, self.wide.at[0])
        self.copy(9).start()
        self.copy(5).wait_recv()
        self.add(1, half, half, self.wide.at[1])
        self.copy(8).start()
        self.copy(0).wait_recv()

    def finish(self):
        for i in (6, 7, 8, 9):
            self.copy(i).wait_recv()
        for i in range(10):
            self.copy(i).wait_send()

    def total(self, at):
        own = self.part[0, 0, at].astype(F32) + self.near[0, at].astype(F32)
        return own + self.far[0, at].astype(F32) + self.far[1, at].astype(F32)


def plane_scratch(rows, width):
    dma = pltpu.SemaphoreType.DMA
    return [
        pltpu.VMEM((TP, rows, width), BF),
        pltpu.VMEM((2, 4, rows, width), BF),
        pltpu.VMEM((4, rows, width), BF),
        pltpu.VMEM((2, rows // 2, width), BF),
        pltpu.VMEM((2, rows, width), BF),
        dma((10,)), dma((10,)), dma((10,)), dma((10,)),
    ]


def steps(gather, scatter, compute):
    def one(i, carry):
        for n in range(1, 2 * 4):
            @pl.when(i == n)
            def _():
                if gather is not None:
                    gather.before(n)

        compute(i // 2, lax.rem(i, 2))
        for n in range(2 * 4):
            @pl.when(i == n)
            def _():
                if scatter is not None:
                    scatter.after(n)

        return carry

    lax.fori_loop(0, 2 * 4, one, 0)


def end_forward(scatter, residual, gain, out, normed):
    rows, chunk = out.shape[0], 32

    def some(i, carry):
        at = pl.ds(pl.multiple_of(i * chunk, chunk), chunk)
        value = residual[at] + scatter.total(at)
        out[at] = value
        scale = lax.rsqrt(jnp.mean(value * value, axis=-1, keepdims=True) + EPSILON)
        normed[at] = (value * scale * gain[...]).astype(BF)
        return carry

    lax.fori_loop(0, rows // chunk, some, 0)


def end_backward(scatter, upstream, values, gain, grad, grad_low, grad_gain):
    rows, chunk = grad.shape[0], 32
    grad_gain[...] = jnp.zeros_like(grad_gain)

    def some(i, carry):
        at = pl.ds(pl.multiple_of(i * chunk, chunk), chunk)
        value, given = values[at], scatter.total(at)
        scale = lax.rsqrt(jnp.mean(value * value, axis=-1, keepdims=True) + EPSILON)
        scaled = given * gain[...]
        mean = jnp.mean(value * scaled, axis=-1, keepdims=True)
        result = upstream[at] + scale * scaled - value * (scale * scale * scale * mean)
        grad[at] = result
        grad_low[at] = result.astype(BF)
        grad_gain[...] += jnp.sum(given * value * scale, axis=0, keepdims=True)
        return carry

    lax.fori_loop(0, rows // chunk, some, 0)


GELU_A = 0.7978845608028654
GELU_B = 0.044715


def gelu_parts(v):
    square = v * v
    tanh = jnp.tanh(GELU_A * (v + GELU_B * v * square))
    half = 0.5 * (1.0 + tanh)
    slope = half + 0.5 * v * (1.0 - tanh * tanh) * (GELU_A * (1.0 + 3.0 * GELU_B * square))
    return v * half, slope


def copy_list(pairs, sem, first):
    return [
        pltpu.make_async_copy(src, dst, sem.at[first + n]) for n, (src, dst) in enumerate(pairs)
    ]


def unpack_rec(pack, col, wout, gates, sem, first):
    seq, both = pack.shape[0], pack.shape[2]
    rows, part = col.shape[0] // seq, gates.shape[0] // seq
    pairs = []
    for z in range(seq):
        pairs.append((pack.at[z, pl.ds(0, rows)], col.at[pl.ds(z * rows, rows)]))
        own = pl.ds(z * part, part)
        for j in range(3):
            pairs.append(
                (pack.at[z, pl.ds(rows + j * part, part)], wout.at[own, pl.ds(j * both, both)])
            )
        pairs.append((pack.at[z, pl.ds(rows + 3 * part, part)], gates.at[own]))
    return copy_list(pairs, sem, first)


def mlp_split(width, twice):
    rest = width - twice
    return rest, twice // rest


def unpack_mlp(pack, col, down, sem, first):
    seq, twice = pack.shape[0], pack.shape[2]
    rows, part = col.shape[0] // seq, down.shape[0] // seq
    rest, blocks = mlp_split(down.shape[1], twice)
    low = part // blocks
    pairs = []
    for z in range(seq):
        pairs.append((pack.at[z, pl.ds(0, rows)], col.at[pl.ds(z * rows, rows)]))
        pairs.append(
            (pack.at[z, pl.ds(rows, part)], down.at[pl.ds(z * part, part), pl.ds(0, twice)])
        )
        for n in range(blocks):
            pairs.append(
                (
                    pack.at[z, pl.ds(rows + part, low), pl.ds(n * rest, rest)],
                    down.at[pl.ds(z * part + n * low, low), pl.ds(twice, rest)],
                )
            )
    return copy_list(pairs, sem, first)


def mlp_forward_kernel(
    x_ref, residual_ref, gain_ref, pack_ref,
    out_ref, normed_ref, full_out, up_out,
    full, part, near, wide, far, gs, gr, ss, sr, col, wd, ups, sem,
):
    net = Net()
    gather = Gather(net, full, gs, gr)
    scatter = Scatter(net, part, near, wide, far, ss, sr)
    n = 5 * pack_ref.shape[0]
    own = pltpu.make_async_copy(x_ref, full.at[net.t], sem.at[n])
    own.start()
    weights = unpack_mlp(pack_ref, col, wd, sem, 0)
    for copy in weights:
        copy.start()
    net.enter()
    own.wait()
    gather.begin()
    for copy in weights:
        copy.wait()

    units = wd.shape[0]

    def compute(m, s):
        slot = net.slot(m, s)
        x = full[slot]
        up = dot(x, col[...])
        ups[slot] = up.astype(BF)
        hidden = glu_product(up[:, :units], up[:, units:]).astype(BF)
        part[s, m] = dot(hidden, wd[...]).astype(BF)

    steps(gather, scatter, compute)
    saves = [
        pltpu.make_async_copy(full, full_out, sem.at[n + 1]),
        pltpu.make_async_copy(ups, up_out, sem.at[n + 2]),
    ]
    for copy in saves:
        copy.start()
    scatter.corner()
    scatter.edges()
    scatter.finish()
    end_forward(scatter, residual_ref, gain_ref, out_ref, normed_ref)
    gather.finish()
    for copy in saves:
        copy.wait()


def mlp_forward(x, residual, gain, pack):
    rows, width = x.shape
    seq, _, twice = pack.shape
    shape = jax.ShapeDtypeStruct
    return pl.pallas_call(
        mlp_forward_kernel,
        in_specs=[ANY, VM, VM, ANY],
        out_specs=[VM, VM, ANY, ANY],
        out_shape=[
            shape((rows, width), F32),
            shape((rows, width), BF),
            shape((TP, rows, width), BF),
            shape((TP, rows, twice), BF),
        ],
        scratch_shapes=plane_scratch(rows, width)
        + [
            pltpu.VMEM((width, twice), BF),
            pltpu.VMEM((twice // 2, width), BF),
            pltpu.VMEM((TP, rows, twice), BF),
            pltpu.SemaphoreType.DMA((5 * seq + 4,)),
        ],
        compiler_params=pltpu.CompilerParams(
            collective_id=1, has_side_effects=True, vmem_limit_bytes=58 << 20
        ),
        cost_estimate=pl.CostEstimate(
            flops=60 * 10**9, bytes_accessed=30 << 20, transcendentals=0
        ),
        name="mlp_forward",
    )(x, residual, gain.reshape(1, -1), pack)


def mlp_backward_kernel(
    g_ref, upstream_ref, values_ref, gain_ref, pack_ref, x_ref, up_ref,
    grad_ref, low_ref, gain_out, gcol_ref,
    full, part, near, wide, far, gs, gr, ss, sr, col, wd, xs, ups, hid, sem,
):
    net = Net()
    gather = Gather(net, full, gs, gr)
    scatter = Scatter(net, part, near, wide, far, ss, sr)
    seq = pack_ref.shape[0]
    n = 5 * seq
    own = pltpu.make_async_copy(g_ref, full.at[net.t], sem.at[n])
    own.start()
    loads = unpack_mlp(pack_ref, col, wd, sem, 0) + [
        pltpu.make_async_copy(up_ref, ups, sem.at[n + 1]),
    ]
    late = pltpu.make_async_copy(x_ref, xs, sem.at[n + 3])
    for copy in loads + [late]:
        copy.start()
    net.enter()
    own.wait()
    gather.begin()
    for copy in loads:
        copy.wait()
    rows, units = full.shape[1], wd.shape[0]

    def compute(m, s):
        slot = net.slot(m, s)
        at = pl.ds(pl.multiple_of(slot * rows, rows), rows)
        grad_hidden = dot_nt(full[slot], wd[...])
        up = ups[at].astype(F32)
        act, slope = gelu_parts(up[:, :units])
        up_value = up[:, units:]
        hid[at] = (act * up_value).astype(BF)
        grads = jnp.concatenate([grad_hidden * up_value * slope, grad_hidden * act], 1).astype(BF)
        ups[at] = grads
        part[s, m] = dot_nt(grads, col[...]).astype(BF)

    steps(gather, scatter, compute)
    late.wait()
    scatter.corner()
    width = full.shape[2]
    own_rows = width // (TP * seq)
    tile = 2 * seq * own_rows
    base = width // seq

    def columns(j, carry):
        x = xs[:, pl.ds(pl.multiple_of(j * tile, 128), tile)]
        product = dot_tn(x, ups[...]).astype(BF)
        for r in range(2):
            for z in range(seq):
                low = (r * seq + z) * own_rows
                at = pl.ds(pl.multiple_of((2 * j + r) * own_rows, own_rows), own_rows)
                gcol_ref[z, at] = product[low : low + own_rows]
        return carry

    lax.fori_loop(0, TP // 2, columns, 0)
    scatter.edges()

    tokens = full.shape[0] * rows
    part_units = units // seq
    rest, blocks = mlp_split(width, 2 * units)
    low = part_units // blocks
    hidden = hid[...]
    for first in range(0, width, width // 2):
        at = pl.ds(first, width // 2)
        product = dot_tn(hidden, full[:, :, at].reshape(tokens, width // 2)).astype(BF)
        beside = min(2 * units - first, width // 2)
        for z in range(seq):
            own = product[z * part_units : (z + 1) * part_units]
            gcol_ref[z, base : base + part_units, first : first + beside] = own[:, :beside]
            if beside < width // 2:
                for n in range(blocks):
                    gcol_ref[z, base + part_units :, n * rest : (n + 1) * rest] = own[
                        n * low : (n + 1) * low, beside:
                    ]
    scatter.finish()
    end_backward(scatter, upstream_ref, values_ref, gain_ref, grad_ref, low_ref, gain_out)
    gather.finish()


def mlp_backward(g, upstream, values, gain, pack, x, up):
    rows, width = g.shape
    seq, _, twice = pack.shape
    tokens = TP * rows
    shape = jax.ShapeDtypeStruct
    return pl.pallas_call(
        mlp_backward_kernel,
        in_specs=[ANY, VM, VM, VM, ANY, ANY, ANY],
        out_specs=[VM, VM, VM, VM],
        out_shape=[
            shape((rows, width), F32),
            shape((rows, width), BF),
            shape((1, width), F32),
            shape(pack.shape, BF),
        ],
        scratch_shapes=plane_scratch(rows, width)
        + [
            pltpu.VMEM((width, twice), BF),
            pltpu.VMEM((twice // 2, width), BF),
            pltpu.VMEM((tokens, width), BF),
            pltpu.VMEM((tokens, twice), BF),
            pltpu.VMEM((tokens, twice // 2), BF),
            pltpu.SemaphoreType.DMA((5 * seq + 4,)),
        ],
        compiler_params=pltpu.CompilerParams(
            collective_id=2, has_side_effects=True, vmem_limit_bytes=60 << 20
        ),
        cost_estimate=pl.CostEstimate(
            flops=70 * 10**9, bytes_accessed=30 << 20, transcendentals=0
        ),
        name="mlp_backward",
    )(
        g, upstream, values, gain.reshape(1, -1), pack, x.reshape(tokens, width),
        up.reshape(tokens, twice),
    )


def after_corner_first(scatter, n):
    if n % 2 == 0:
        scatter.copy(3 - n // 2).start()
    if n == 3:
        scatter.corner()
    if n == 5:
        scatter.copy(2).wait_recv()
        scatter.add(2, 0, scatter.rows, scatter.near.at[2])
        scatter.copy(7).start()
    if n == 7:
        scatter.copy(1).wait_recv()
        scatter.add(1, 0, scatter.rows, scatter.near.at[1])
        scatter.copy(6).start()


class Line:
    def __init__(self, net, count):
        self.net, self.count = net, count
        self.others = [(net.base + net.t, lax.rem(net.z + d, count)) for d in range(1, count)]
        self.next = (net.base + net.t, net.z + 1)
        self.before = (net.base + net.t, net.z - 1)

    def to_all(self, ends, send, recv):
        at = ends.at[self.net.z]
        copies = [
            remote(at, at, send.at[d], recv.at[d], to) for d, to in enumerate(self.others)
        ]
        for copy in copies:
            copy.start()
        for d, copy in enumerate(copies):
            source = lax.rem(self.net.z + self.count - 1 - d, self.count)
            from_at = ends.at[source]
            remote(from_at, from_at, send.at[d], recv.at[d], self.others[d]).wait_recv()
        for copy in copies:
            copy.wait_send()


def inside_of(positions, offset, length):
    return jnp.where((positions >= offset) & (positions < offset + length), 1.0, 0.0)


def read_halves(ref, at):
    return jnp.concatenate([ref[n, at] for n in range(ref.shape[0])], 1)


def write_halves(ref, at, value):
    for n in range(ref.shape[0]):
        ref[n, at] = value[:, n * 128 : (n + 1) * 128]


def one_minus_exp(v):
    series = 1.0 + v * (1.0 / 7.0)
    for n in (6.0, 5.0, 4.0, 3.0, 2.0):
        series = 1.0 + v * (1.0 / n) * series
    return jnp.where(v > -0.35, -v * series, 1.0 - jnp.exp(v))


def sigmoid(v):
    return 1.0 / (1.0 + jnp.exp(-v))


def rec_forward_kernel(
    gathered,
    x_ref, residual_ref, gain_ref, pack_ref, small_ref, slots_ref,
    out_ref, normed_ref, full_out, branch_out, stream_out, conv_out, state_out,
    full, part, near, wide, far, gs, gr, ss, sr,
    col, gates, wout, branch, stream, conv, state, retain, inflow, ends, carry, hs, hr, es, er, sem,
):
    net = Net()
    seq = ends.shape[0]
    line = Line(net, seq)
    gather = Gather(net, full, gs, gr)
    scatter = Scatter(net, part, near, wide, far, ss, sr)
    rows = full.shape[1]
    head = gates.shape[0]
    own = pltpu.make_async_copy(x_ref, full if gathered else full.at[net.t], sem.at[0])
    loads = unpack_rec(pack_ref, col, wout, gates, sem, 9)
    for load in [own] + loads:
        load.start()
    net.enter(line.others)
    own.wait()
    if not gathered:
        gather.begin()

    @pl.when(net.z == 0)
    def _():
        stream[:, pl.ds(0, 8), :] = jnp.zeros((TP, 8, head), F32)

    for load in loads:
        load.wait()

    def halo(i):
        slot = net.slot(i // 2, lax.rem(i, 2))
        return remote(
            stream.at[slot, pl.ds(rows, 8)], stream.at[slot, pl.ds(0, 8)],
            hs.at[i], hr.at[i], line.next,
        )

    def project(i):
        slot = net.slot(i // 2, lax.rem(i, 2))
        both = dot(full[slot], col[...])
        branch[slot] = both[:, :head]
        stream[slot, pl.ds(8, rows)] = both[:, head:]

        @pl.when(net.z < seq - 1)
        def _():
            halo(i).start()

    def gate(i):
        slot = net.slot(i // 2, lax.rem(i, 2))

        @pl.when(net.z > 0)
        def _():
            halo(i).wait_recv()

        length, offset = slots_ref[slot, 0], slots_ref[slot, 1]
        positions = net.z * rows + lax.broadcasted_iota(jnp.int32, (rows, head), 0)
        inside = inside_of(positions, offset, length)
        mixed = small_ref[pl.ds(CONV, 1), :] + small_ref[pl.ds(0, 1), :] * stream[slot, pl.ds(8, rows)]
        restart = positions == 0
        for j in range(1, CONV):
            same = jnp.where(inside == inside_of(positions - j, offset, length), 1.0, 0.0)
            if j == 1:
                restart = restart | (same == 0.0)
            mixed += small_ref[pl.ds(j, 1), :] * stream[slot, pl.ds(8 - j, rows)] * same
        low = mixed.astype(BF)
        conv[slot] = low
        pre = dot(low, gates[...])
        rate = sigmoid(pre[:, :head] + small_ref[pl.ds(CONV + 1, 1), :])
        admit = sigmoid(pre[:, head:] + small_ref[pl.ds(CONV + 2, 1), :])
        log_retain = rate * small_ref[pl.ds(CONV + 3, 1), :]
        at = pl.ds(pl.multiple_of(slot * rows, rows), rows)
        write_halves(retain, at, jnp.where(restart, 0.0, jnp.exp(log_retain)))
        scale = jnp.where(restart, 1.0, jnp.sqrt(one_minus_exp(2.0 * log_retain)))
        write_halves(inflow, at, scale * admit * low.astype(F32))

    def one(i, _):
        for n in range(1, TP):
            @pl.when(i == n)
            def _():
                if not gathered:
                    gather.before(n)

        @pl.when(i < TP)
        def _():
            project(i)

        @pl.when(i >= LATER)
        def _():
            gate(i - LATER)

        return 0

    lax.fori_loop(0, TP + LATER, one, 0)
    saves = [
        pltpu.make_async_copy(branch, branch_out, sem.at[5]),
        pltpu.make_async_copy(stream, stream_out, sem.at[6]),
        pltpu.make_async_copy(conv, conv_out, sem.at[7]),
    ]
    if not gathered:
        saves.append(pltpu.make_async_copy(full, full_out, sem.at[4]))
    for save in saves:
        save.start()

    lanes = [pl.ds(i, 128) for i in range(0, head, 128)]

    def step(p, carried):
        at = pl.ds(p, TP, stride=rows)
        result = []
        for n, (value, decay) in enumerate(carried):
            a = retain[n, at]
            value = a * value + inflow[n, at]
            decay = a * decay
            inflow[n, at] = value
            retain[n, at] = decay
            result.append((value, decay))
        return tuple(result)

    start = tuple((jnp.zeros((TP, 128), F32), jnp.ones((TP, 128), F32)) for _ in lanes)
    last = lax.fori_loop(0, rows, step, start, unroll=8)
    for lane, (value, decay) in zip(lanes, last):
        ends[net.z, pl.ds(0, TP), lane] = decay
        ends[net.z, pl.ds(TP, TP), lane] = value
    line.to_all(ends, es, er)
    entering = jnp.zeros((TP, head), F32)
    for z in range(seq - 1):
        later = ends[z, pl.ds(0, TP)] * entering + ends[z, pl.ds(TP, TP)]
        entering = jnp.where(z < net.z, later, entering)
    carry[...] = entering

    def join(i, _):
        m, s = 3 - i // 2, 1 - lax.rem(i, 2)
        slot = net.slot(m, s)
        at = pl.ds(pl.multiple_of(slot * rows, rows), rows)
        first = carry[pl.ds(slot, 1), :]
        states = read_halves(inflow, at) + read_halves(retain, at) * first
        state[slot, pl.ds(0, 8)] = jnp.broadcast_to(first, (8, head))
        state[slot, pl.ds(8, rows)] = states
        joined = glu_product(branch[slot], states).astype(BF)
        part[s, m] = dot(joined, wout[...]).astype(BF)
        for n in range(TP):
            @pl.when(i == n)
            def _():
                after_corner_first(scatter, n)

        return 0

    lax.fori_loop(0, TP, join, 0)
    saves.append(pltpu.make_async_copy(state, state_out, sem.at[8]))
    saves[-1].start()
    scatter.edges()

    @pl.when(net.z < seq - 1)
    def _():
        lax.fori_loop(0, TP, lambda i, _: (halo(i).wait_send(), 0)[1], 0)

    scatter.finish()
    end_forward(scatter, residual_ref, gain_ref, out_ref, normed_ref)
    if not gathered:
        gather.finish()
    for save in saves:
        save.wait()


def rec_scratch(pack, width):
    seq, _, both = pack.shape
    return [
        pltpu.VMEM((width, both), BF),
        pltpu.VMEM((both // 2, both), BF),
        pltpu.VMEM((both // 2, width), BF),
    ]


def rec_forward(x, residual, gain, pack, small, slots):
    gathered = x.ndim == 3
    rows, width = residual.shape
    seq, _, head = pack.shape
    head = head // 2
    shape = jax.ShapeDtypeStruct
    dma = pltpu.SemaphoreType.DMA
    tokens = TP * rows
    result = list(pl.pallas_call(
        partial(rec_forward_kernel, gathered),
        in_specs=[ANY, VM, VM, ANY, VM, pl.BlockSpec(memory_space=pltpu.SMEM)],
        out_specs=[VM, VM, ANY, ANY, ANY, ANY, ANY],
        out_shape=[
            shape((rows, width), F32),
            shape((rows, width), BF),
            shape((8, 128) if gathered else (TP, rows, width), BF),
            shape((TP, rows, head), F32),
            shape((TP, rows + 8, head), F32),
            shape((TP, rows, head), BF),
            shape((TP, rows + 8, head), F32),
        ],
        scratch_shapes=plane_scratch(rows, width)
        + rec_scratch(pack, width)
        + [
            pltpu.VMEM((TP, rows, head), F32),
            pltpu.VMEM((TP, rows + 8, head), F32),
            pltpu.VMEM((TP, rows, head), BF),
            pltpu.VMEM((TP, rows + 8, head), F32),
            pltpu.VMEM((head // 128, tokens, 128), F32),
            pltpu.VMEM((head // 128, tokens, 128), F32),
            pltpu.VMEM((seq, 2 * TP, head), F32),
            pltpu.VMEM((TP, head), F32),
            dma((TP,)), dma((TP,)), dma((seq - 1,)), dma((seq - 1,)), dma((9 + 5 * seq,)),
        ],
        compiler_params=pltpu.CompilerParams(
            collective_id=5 if gathered else 3, has_side_effects=True, vmem_limit_bytes=58 << 20
        ),
        cost_estimate=pl.CostEstimate(
            flops=70 * 10**9, bytes_accessed=30 << 20, transcendentals=0
        ),
        name="rec_forward_first" if gathered else "rec_forward",
    )(x, residual, gain.reshape(1, -1), pack, small, slots))
    if gathered:
        result[2] = x
    return result


def rec_backward_kernel(
    g_ref, upstream_ref, values_ref, gain_ref, pack_ref, small_ref, slots_ref,
    x_ref, branch_ref, stream_ref, conv_ref, state_ref,
    grad_ref, low_ref, gain_out, gcol_ref, channel_ref,
    full, part, near, wide, far, gs, gr, ss, sr,
    col, gates, wout, xs, branch, stream, conv, state,
    retain, direct, suffix, joined, both, gpre, mixed, ends, carry, hs, hr, es, er, sem,
):
    net = Net()
    seq = ends.shape[0]
    line = Line(net, seq)
    gather = Gather(net, full, gs, gr)
    scatter = Scatter(net, part, near, wide, far, ss, sr)
    rows, width = full.shape[1], full.shape[2]
    head = gates.shape[0]
    own = pltpu.make_async_copy(g_ref, full.at[net.t], sem.at[0])
    loads = [
        pltpu.make_async_copy(a, b, sem.at[1 + n])
        for n, (a, b) in enumerate(
            (
                (branch_ref, branch), (state_ref, state), (conv_ref, conv), (stream_ref, stream),
                (x_ref, xs),
            )
        )
    ]
    loads = unpack_rec(pack_ref, col, wout, gates, sem, 9) + loads
    for load in [own] + loads:
        load.start()
    net.enter(line.others)
    own.wait()
    gather.begin()

    @pl.when(net.z == seq - 1)
    def _():
        mixed[:, pl.ds(rows, 8), :] = jnp.zeros((TP, 8, head), F32)

    channel_ref[...] = jnp.zeros_like(channel_ref)
    for load in loads[:-2]:
        load.wait()

    def gate_parts(slot):
        positions = net.z * rows + lax.broadcasted_iota(jnp.int32, (rows, head), 0)
        length, offset = slots_ref[slot, 0], slots_ref[slot, 1]
        inside = inside_of(positions, offset, length)
        restart = (positions == 0) | (inside != inside_of(positions - 1, offset, length))
        pre = dot(conv[slot], gates[...])
        rate = sigmoid(pre[:, :head] + small_ref[pl.ds(CONV + 1, 1), :])
        admit = sigmoid(pre[:, head:] + small_ref[pl.ds(CONV + 2, 1), :])
        log_retain = rate * small_ref[pl.ds(CONV + 3, 1), :]
        return positions, offset, length, inside, restart, rate, admit, log_retain

    def open_block(m, s):
        slot = net.slot(m, s)
        at = pl.ds(pl.multiple_of(slot * rows, rows), rows)
        grad_joined = dot_nt(full[slot], wout[...])
        act, slope = gelu_parts(branch[slot])
        states = state[slot, pl.ds(8, rows)]
        joined[at] = (act * states).astype(BF)
        both[at, :head] = (grad_joined * states * slope).astype(BF)
        write_halves(direct, at, grad_joined * act)
        _, _, _, _, restart, _, _, log_retain = gate_parts(slot)
        write_halves(retain, at, jnp.where(restart, 0.0, jnp.exp(log_retain)))

    steps(gather, None, open_block)
    lanes = [pl.ds(i, 128) for i in range(0, head, 128)]

    def step(i, carried):
        at = pl.ds(rows - 1 - i, TP, stride=rows)
        result = []
        for n, (value, decay, ahead) in enumerate(carried):
            value = ahead * value + direct[n, at]
            decay = ahead * decay
            direct[n, at] = value
            suffix[n, at] = decay
            result.append((value, decay, retain[n, at]))
        return tuple(result)

    one = jnp.minimum(retain[0, pl.ds(0, TP)] + 2.0, 1.0)
    last = lax.fori_loop(
        0, rows, step, tuple((jnp.zeros((TP, 128), F32), one, one) for _ in lanes), unroll=8
    )
    for lane, (value, decay, first) in zip(lanes, last):
        ends[net.z, pl.ds(0, TP), lane] = first * decay
        ends[net.z, pl.ds(TP, TP), lane] = first * value
    line.to_all(ends, es, er)
    entering = jnp.zeros((TP, head), F32)
    for z in range(seq - 1, 0, -1):
        earlier = ends[z, pl.ds(0, TP)] * entering + ends[z, pl.ds(TP, TP)]
        entering = jnp.where(z > net.z, earlier, entering)
    carry[...] = entering
    loads[-2].wait()

    def halo(i):
        slot = net.slot(3 - i // 2, 1 - lax.rem(i, 2))
        return remote(
            mixed.at[slot, pl.ds(0, 8)], mixed.at[slot, pl.ds(rows, 8)],
            hs.at[i], hr.at[i], line.before,
        )

    def through_gates(i):
        slot = net.slot(3 - i // 2, 1 - lax.rem(i, 2))
        at = pl.ds(pl.multiple_of(slot * rows, rows), rows)
        grad_states = read_halves(direct, at) + read_halves(suffix, at) * carry[pl.ds(slot, 1), :]
        positions, offset, length, inside, restart, rate, admit, log_retain = gate_parts(slot)
        low = conv[slot].astype(F32)
        kept = jnp.exp(log_retain)
        root = jnp.sqrt(one_minus_exp(2.0 * log_retain))
        scale = jnp.where(restart, 1.0, root)
        grad_admit = grad_states * scale * low
        grad_scale = grad_states * admit * low
        grad_log = grad_states * state[slot, pl.ds(7, rows)] * kept - grad_scale * kept * kept / root
        grad_log = jnp.where(restart, 0.0, grad_log)
        rate_part = grad_log * small_ref[pl.ds(CONV + 3, 1), :] * rate * (1.0 - rate)
        admit_part = grad_admit * admit * (1.0 - admit)
        gpre[at, :head] = rate_part.astype(BF)
        gpre[at, head:] = admit_part.astype(BF)
        grad_mixed = grad_states * scale * admit + dot_nt(gpre[at], gates[...])
        mixed[slot, pl.ds(0, rows)] = grad_mixed

        @pl.when(net.z > 0)
        def _():
            halo(i).start()

        sums = [jnp.sum(grad_mixed * stream[slot, pl.ds(8, rows)], axis=0, keepdims=True)]
        for j in range(1, CONV):
            same = jnp.where(inside == inside_of(positions - j, offset, length), 1.0, 0.0)
            sums.append(
                jnp.sum(
                    grad_mixed * stream[slot, pl.ds(8 - j, rows)] * same, axis=0, keepdims=True
                )
            )
        for term in (grad_mixed, rate_part, admit_part, grad_log * rate):
            sums.append(jnp.sum(term, axis=0, keepdims=True))
        for n, term in enumerate(sums):
            channel_ref[pl.ds(n, 1), :] += term

    def to_input(i):
        m, s = 3 - i // 2, 1 - lax.rem(i, 2)
        slot = net.slot(m, s)
        at = pl.ds(pl.multiple_of(slot * rows, rows), rows)

        @pl.when(net.z < seq - 1)
        def _():
            halo(i).wait_recv()

        positions = net.z * rows + lax.broadcasted_iota(jnp.int32, (rows, head), 0)
        length, offset = slots_ref[slot, 0], slots_ref[slot, 1]
        inside = inside_of(positions, offset, length)
        grad_stream = small_ref[pl.ds(0, 1), :] * mixed[slot, pl.ds(0, rows)]
        for j in range(1, CONV):
            same = jnp.where(inside == inside_of(positions + j, offset, length), 1.0, 0.0)
            grad_stream += small_ref[pl.ds(j, 1), :] * mixed[slot, pl.ds(j, rows)] * same
        both[at, head:] = grad_stream.astype(BF)
        part[s, m] = dot_nt(both[at], col[...]).astype(BF)

    def one_block(i, _):
        @pl.when(i < TP)
        def _():
            through_gates(i)

        @pl.when(i >= LATER)
        def _():
            to_input(i - LATER)

        for n in range(TP):
            @pl.when(i == n + LATER)
            def _():
                after_corner_first(scatter, n)

        return 0

    lax.fori_loop(0, TP + LATER, one_block, 0)
    scatter.edges()
    loads[-1].wait()
    own_rows = width // (TP * seq)
    tile = 2 * seq * own_rows

    def columns(j, _):
        x = xs[:, pl.ds(pl.multiple_of(j * tile, 128), tile)]
        product = dot_tn(x, both[...]).astype(BF)
        for r in range(2):
            for z in range(seq):
                low = (r * seq + z) * own_rows
                at = pl.ds(pl.multiple_of((2 * j + r) * own_rows, own_rows), own_rows)
                gcol_ref[z, at] = product[low : low + own_rows]
        return 0

    lax.fori_loop(0, TP // 2, columns, 0)
    low_conv = conv[...].reshape(TP * rows, head)
    product = dot_tn(low_conv, gpre[...]).astype(BF)
    third, base, part_head = width // 3, width // seq, head // seq
    for z in range(seq):
        low = base + 3 * part_head
        gcol_ref[z, low : low + part_head] = product[z * part_head : (z + 1) * part_head]
    for j in range(3):
        at = pl.ds(j * third, third)
        product = dot_tn(joined[...], full[:, :, at].reshape(TP * rows, third)).astype(BF)
        for z in range(seq):
            low = base + j * part_head
            gcol_ref[z, low : low + part_head] = product[z * part_head : (z + 1) * part_head]

    @pl.when(net.z > 0)
    def _():
        lax.fori_loop(0, TP, lambda i, _: (halo(i).wait_send(), 0)[1], 0)

    scatter.finish()
    end_backward(scatter, upstream_ref, values_ref, gain_ref, grad_ref, low_ref, gain_out)
    gather.finish()


def rec_backward(g, upstream, values, gain, pack, small, slots, saved):
    rows, width = g.shape
    seq, _, head = pack.shape
    head = head // 2
    tokens = TP * rows
    shape = jax.ShapeDtypeStruct
    dma = pltpu.SemaphoreType.DMA
    x, branch, stream, conv, state = saved
    return pl.pallas_call(
        rec_backward_kernel,
        in_specs=[ANY, VM, VM, VM, ANY, VM, pl.BlockSpec(memory_space=pltpu.SMEM)]
        + [ANY] * 5,
        out_specs=[VM] * 5,
        out_shape=[
            shape((rows, width), F32),
            shape((rows, width), BF),
            shape((1, width), F32),
            shape(pack.shape, BF),
            shape((8, head), F32),
        ],
        scratch_shapes=plane_scratch(rows, width)
        + rec_scratch(pack, width)
        + [
            pltpu.VMEM((tokens, width), BF),
            pltpu.VMEM(branch.shape, F32),
            pltpu.VMEM(stream.shape, F32),
            pltpu.VMEM(conv.shape, BF),
            pltpu.VMEM(state.shape, F32),
            pltpu.VMEM((head // 128, tokens, 128), F32),
            pltpu.VMEM((head // 128, tokens, 128), F32),
            pltpu.VMEM((head // 128, tokens, 128), F32),
            pltpu.VMEM((tokens, head), BF),
            pltpu.VMEM((tokens, 2 * head), BF),
            pltpu.VMEM((tokens, 2 * head), BF),
            pltpu.VMEM((TP, rows + 8, head), F32),
            pltpu.VMEM((seq, 2 * TP, head), F32),
            pltpu.VMEM((TP, head), F32),
            dma((TP,)), dma((TP,)), dma((seq - 1,)), dma((seq - 1,)), dma((9 + 5 * seq,)),
        ],
        compiler_params=pltpu.CompilerParams(
            collective_id=4, has_side_effects=True, vmem_limit_bytes=60 << 20
        ),
        cost_estimate=pl.CostEstimate(
            flops=80 * 10**9, bytes_accessed=30 << 20, transcendentals=0
        ),
        name="rec_backward",
    )(
        g, upstream, values, gain.reshape(1, -1), pack, small, slots,
        x.reshape(tokens, width), branch, stream, conv, state,
    )


def open_kernel(
    x_ref, small_ref, gain_ref, slot_ref, pack_ref,
    small_out, gain_out, slot_out, full_out, pack_out,
    full, smalls, gains, slots, gs, gr, ps, pr, sem,
):
    net = Net()
    seq = smalls.shape[0]
    line = Line(net, seq)
    gather = Gather(net, full, gs, gr)
    plane = [net.device(m, s) for m in range(4) for s in range(2)][1:]
    mine = [
        pltpu.make_async_copy(small_ref, smalls.at[net.z], sem.at[0]),
        pltpu.make_async_copy(gain_ref, gains.at[net.z], sem.at[1]),
        pltpu.make_async_copy(slot_ref, slots.at[net.t], sem.at[2]),
    ]
    own_pack = pltpu.make_async_copy(pack_ref, pack_out.at[net.z], sem.at[4])
    for copy in mine + [own_pack]:
        copy.start()
    net.enter(line.others + [net.device(1, 1), net.device(2, 1), net.device(3, 0), net.device(3, 1)])
    for copy in mine:
        copy.wait()

    sends, arrivals = [], []

    def push(ref, own, source, to):
        n = len(sends)
        at, from_at = ref.at[own], ref.at[source]
        sends.append(remote(at, at, ps.at[n], pr.at[n], to))
        arrivals.append(remote(from_at, from_at, ps.at[n], pr.at[n], to))

    for ref in (gains, smalls):
        for d, to in enumerate(line.others):
            push(ref, net.z, lax.rem(net.z + seq - 1 - d, seq), to)
    for n, to in enumerate(plane):
        m, s = (n + 1) // 2, (n + 1) % 2
        push(slots, net.t, net.slot(m, s), to)
    for copy in sends:
        copy.start()
    small_sends, small_arrivals = list(sends), list(arrivals)
    for d, to in enumerate(line.others):
        n = len(sends)
        source = lax.rem(net.z + seq - 1 - d, seq)
        sends.append(remote(pack_ref, pack_out.at[net.z], ps.at[n], pr.at[n], to))
        arrivals.append(remote(pack_ref, pack_out.at[source], ps.at[n], pr.at[n], to))
        sends[-1].start()
    for copy in arrivals[: seq - 1]:
        copy.wait_recv()
    rows, width = x_ref.shape
    part, chunk = width // seq, 32

    def norm(i, _):
        at = pl.ds(pl.multiple_of(i * chunk, chunk), chunk)
        value = x_ref[at].astype(F32)
        scale = lax.rsqrt(jnp.mean(value * value, axis=-1, keepdims=True) + EPSILON)
        for z in range(seq):
            low = z * part
            full[net.t, at, low : low + part] = (
                value[:, low : low + part] * scale * gains[z, pl.ds(0, 1), :]
            ).astype(BF)
        return 0

    lax.fori_loop(0, rows // chunk, norm, 0)
    gather.begin()
    for copy in small_arrivals[seq - 1 :]:
        copy.wait_recv()
    saves = [
        pltpu.make_async_copy(a, b, sem.at[n])
        for n, (a, b) in enumerate(((smalls, small_out), (gains, gain_out), (slots, slot_out)))
    ]
    for save in saves:
        save.start()
    for n in range(1, TP):
        gather.before(n)
    gather.finish()
    saves.append(pltpu.make_async_copy(full, full_out, sem.at[3]))
    saves[-1].start()
    for copy in arrivals[len(small_arrivals) :]:
        copy.wait_recv()
    for copy in sends:
        copy.wait_send()
    own_pack.wait()
    for save in saves:
        save.wait()


def opening(seq, x, small, gain, slot, pack):
    rows, width = x.shape
    shape = jax.ShapeDtypeStruct
    dma = pltpu.SemaphoreType.DMA
    pushes = 3 * (seq - 1) + TP - 1
    return pl.pallas_call(
        open_kernel,
        in_specs=[VM, ANY, ANY, ANY, ANY],
        out_specs=[ANY] * 5,
        out_shape=[
            shape((seq,) + small.shape, F32),
            shape((seq,) + gain.shape, F32),
            shape((TP,) + slot.shape, jnp.int32),
            shape((TP, rows, width), BF),
            shape((seq,) + pack.shape, BF),
        ],
        scratch_shapes=[
            pltpu.VMEM((TP, rows, width), BF),
            pltpu.VMEM((seq,) + small.shape, F32),
            pltpu.VMEM((seq,) + gain.shape, F32),
            pltpu.VMEM((TP,) + slot.shape, jnp.int32),
            dma((10,)), dma((10,)), dma((pushes,)), dma((pushes,)), dma((5,)),
        ],
        compiler_params=pltpu.CompilerParams(
            collective_id=6, has_side_effects=True, vmem_limit_bytes=40 << 20
        ),
        cost_estimate=pl.CostEstimate(
            flops=40 * 10**9, bytes_accessed=10 << 20, transcendentals=0
        ),
        name="opening",
    )(x, small, gain, slot, pack)


def close_kernel(
    gain_ref, channel_ref, *refs
):
    count = (len(refs) - 8) // 2
    blocks, (gain_out, channel_out), moved = refs[:count], refs[count : count + 2], refs[
        count + 2 : 2 * count + 2
    ]
    plane_gain, line_gain, line_channel, ps, pr, sem = refs[2 * count + 2 :]
    net = Net()
    seq = line_gain.shape[0]
    line = Line(net, seq)
    plane = [net.device(m, s) for m in range(4) for s in range(2)][1:]
    slots = [net.slot(m, s) for m in range(4) for s in range(2)][1:]
    own = [
        pltpu.make_async_copy(block.at[net.t], out.at[net.t], sem.at[n])
        for n, (block, out) in enumerate(zip(blocks, moved))
    ]
    plane_gain[net.t] = gain_ref[...]
    line_channel[net.z] = channel_ref[...]
    for copy in own:
        copy.start()
    net.enter(line.others + [net.device(1, 1), net.device(2, 1), net.device(3, 0), net.device(3, 1)])
    used = []

    def push(src, dst, landed, to):
        n = len(used)
        used.append(remote(src, dst, ps.at[n], pr.at[n], to))
        used[-1].start()
        return remote(src, landed, ps.at[n], pr.at[n], to)

    gains = [
        push(plane_gain.at[net.t], plane_gain.at[net.t], plane_gain.at[slot], to)
        for slot, to in zip(slots, plane)
    ]
    sources = [lax.rem(net.z + seq - 1 - d, seq) for d in range(seq - 1)]
    rest = [
        push(line_channel.at[net.z], line_channel.at[net.z], line_channel.at[source], to)
        for source, to in zip(sources, line.others)
    ]
    for block, out in zip(blocks, moved):
        for slot, to in zip(slots, plane):
            rest.append(push(block.at[slot], out.at[net.t], out.at[slot], to))
    for copy in gains:
        copy.wait_recv()
    total = plane_gain[0]
    for t in range(1, TP):
        total += plane_gain[t]
    line_gain[net.z] = total
    for source, to in zip(sources, line.others):
        rest.append(push(line_gain.at[net.z], line_gain.at[net.z], line_gain.at[source], to))
    for copy in rest:
        copy.wait_recv()
    total, channel = line_gain[0], line_channel[0]
    for z in range(1, seq):
        total += line_gain[z]
        channel += line_channel[z]
    gain_out[...] = total
    channel_out[...] = channel
    for copy in used:
        copy.wait_send()
    for copy in own:
        copy.wait()


def closing(seq, gains, channels, blocks):
    shape = jax.ShapeDtypeStruct
    dma = pltpu.SemaphoreType.DMA
    pushes = (TP - 1) * (1 + len(blocks)) + 2 * (seq - 1)
    return pl.pallas_call(
        close_kernel,
        in_specs=[VM, VM] + [ANY] * len(blocks),
        out_specs=[VM, VM] + [ANY] * len(blocks),
        out_shape=[shape(gains.shape, F32), shape(channels.shape, F32)]
        + [shape(block.shape, block.dtype) for block in blocks],
        scratch_shapes=[
            pltpu.VMEM((TP,) + gains.shape, F32),
            pltpu.VMEM((seq,) + gains.shape, F32),
            pltpu.VMEM((seq,) + channels.shape, F32),
            dma((pushes,)), dma((pushes,)), dma((len(blocks),)),
        ],
        compiler_params=pltpu.CompilerParams(
            collective_id=7, has_side_effects=True, vmem_limit_bytes=40 << 20
        ),
        cost_estimate=pl.CostEstimate(
            flops=40 * 10**9, bytes_accessed=10 << 20, transcendentals=0
        ),
        name="closing",
    )(gains, channels, *blocks)


def layer_backward(upstream, upstream_low, w, saved, slots, pending):
    residual, kept, middle, kept_two = saved
    pending_mlp, pending_rec = pending
    upstream_low, pending_mlp = lax.optimization_barrier((upstream_low, pending_mlp))
    grad_middle, mid_low, grad_gain_two, g_mlp = mlp_backward(
        upstream_low, upstream, middle, w["gain"][1], w["mlp"], *kept_two
    )
    mlp_share = over_seq(g_mlp)
    mid_low, pending_rec = lax.optimization_barrier((mid_low, pending_rec))
    grad, grad_low, grad_gain_one, g_rec, channel = rec_backward(
        mid_low, grad_middle, residual, w["gain"][0], w["rec"], w["small"], slots, kept
    )
    g_rec, mlp_share = lax.optimization_barrier((g_rec, mlp_share))
    rec_share = over_seq(g_rec)
    slope = 8.0 * jax.nn.sigmoid(-w["decay"])
    channel = jnp.concatenate([channel[:7], channel[7:] * slope], 0)
    gains = jnp.concatenate([grad_gain_one, grad_gain_two], 0)
    return grad, grad_low, (mlp_share, rec_share), channel, gains, (pending_mlp, pending_rec)


def over_seq(value):
    return lax.psum_scatter(value, "seq", scatter_dimension=0, tiled=False)


def columns(parts):
    return jnp.moveaxis(parts, 0, 1).reshape(parts.shape[1], -1)


def owned_grads(plan, mlp_share, rec_share, mlp, rec, width, head, units):
    base = width // plan.seq
    h, u = head // plan.seq, units // plan.seq
    out = [rec_share[base + i * h : base + (i + 1) * h] for i in range(3)]
    gates = rec_share[base + 3 * h :]
    rest, blocks = mlp_split(width, 2 * units)
    down = [mlp_share[base + u :, i * rest : (i + 1) * rest] for i in range(blocks)]
    grads = [
        columns(rec[:, :, :head]),
        columns(rec[:, :, head:]),
        gates[:, :head],
        gates[:, head:],
        jnp.concatenate(out, 1),
        columns(mlp[:, :, :units]),
        columns(mlp[:, :, units:]),
        jnp.concatenate([mlp_share[base : base + u], jnp.concatenate(down, 0)], 1),
    ]
    return [to_owners(plan, g.astype(F32), 0) for g in grads]


def local(plan, *args):
    (
        block_input, cotangent, lengths, offsets, norm_gains, branch_proj, stream_proj, conv_kernel,
        conv_bias, rate_proj, admit_proj, gate_bias, decay_logit, out_proj, mlp_gate, mlp_up,
        mlp_down,
    ) = args
    tp, dp, seq = plan.tp, plan.dp, plan.seq
    t = lax.axis_index("rep") % tp
    z = lax.axis_index("seq")
    rows = block_input.shape[0]
    head = branch_proj.shape[2] // tp
    units = mlp_gate.shape[2] // tp

    channels = conv_kernel.shape[2]
    small = jnp.concatenate([conv_kernel, conv_bias[:, None], gate_bias, decay_logit[:, None]], 1)
    small = small.reshape(LAYERS * 8, channels).astype(F32)
    slot = jnp.pad(jnp.stack([lengths, offsets], 1), ((0, 7), (0, 126)))
    def col(weight, layer, width):
        return lax.dynamic_slice_in_dim(weight[layer], t * width, width, 1)

    def chunk(weight, layer):
        size = weight.shape[1] // tp
        return lax.dynamic_slice_in_dim(weight[layer], t * size, size, 0)

    def below(rows, twice):
        rest, blocks = mlp_split(rows.shape[1], twice)
        low = rows.shape[0] // blocks
        side = [rows[i * low : (i + 1) * low, twice:] for i in range(blocks)]
        return jnp.concatenate([rows[:, :twice], jnp.concatenate(side, 1)], 0)

    def rec_pack(l, ready):
        out = chunk(out_proj, l)
        gates = jnp.concatenate([chunk(rate_proj, l), chunk(admit_proj, l)], 1)
        out = [out[:, i * 2 * head : (i + 1) * 2 * head] for i in range(3)] + [gates]
        out, ready = lax.optimization_barrier((jnp.concatenate(out, 0), ready))
        rec = jnp.concatenate([col(branch_proj, l, head), col(stream_proj, l, head)], 1)
        return jnp.concatenate([rec, owner_chunks(plan, out)], 0), ready

    def mlp_pack(l, ready):
        down, ready = lax.optimization_barrier((below(chunk(mlp_down, l), 2 * units), ready))
        mlp = jnp.concatenate([col(mlp_gate, l, units), col(mlp_up, l, units)], 1)
        return jnp.concatenate([mlp, owner_chunks(plan, down)], 0), ready

    pack, _ = rec_pack(0, ())
    smalls, gains, layout, normed, rec = opening(
        seq, block_input, small, norm_gains.reshape(2 * LAYERS, -1).astype(F32), slot, pack
    )
    layout = layout[:, 0, :2]
    gains = jnp.moveaxis(gains, 0, 1).reshape(LAYERS, 2, -1)
    smalls = jnp.moveaxis(smalls, 0, 1).reshape(LAYERS, 8, -1)
    smalls = lax.dynamic_slice_in_dim(smalls, t * head, head, 2)


    residual = block_input.astype(F32)
    saved_all, weights = [], []
    for l in range(LAYERS):
        if l == 0:
            pack, rec = mlp_pack(l, rec)
        else:
            pack, normed = mlp_pack(l, normed)
        w = dict(
            gain=gains[l],
            small=jnp.concatenate([smalls[l, :7], -8.0 * jax.nn.softplus(-smalls[l, 7:])], 0),
            decay=smalls[l, 7:],
            rec=rec,
            mlp=lax.all_gather(pack, "seq"),
        )
        weights.append(w)
        kept = rec_forward(normed, residual, w["gain"][1], w["rec"], w["small"], layout)
        middle, normed_two, *kept = kept
        if l + 1 < LAYERS:
            pack, normed_two = rec_pack(l + 1, normed_two)
            rec = lax.all_gather(pack, "seq")
        output, normed, *kept_two = mlp_forward(
            normed_two, middle, gains[(l + 1) % LAYERS, 0], w["mlp"]
        )
        saved_all.append((residual, kept, middle, kept_two))
        residual = output
    positions = z * rows + jnp.arange(rows, dtype=jnp.int32)
    inside = (positions >= offsets[0]) & (positions < offsets[0] + lengths[0])
    gradient = cotangent.astype(F32) * inside.astype(F32)[:, None]

    gradient_low = gradient.astype(BF)
    shares = [None] * LAYERS
    channel_all, gain_all = [None] * LAYERS, [None] * LAYERS
    for l in reversed(range(LAYERS)):
        gradient, gradient_low, shares[l], channel_all[l], gain_all[l], pending = layer_backward(
            gradient, gradient_low, weights[l], saved_all[l], layout,
            ((), ()) if l + 1 == LAYERS else shares[l + 1],
        )
        if l + 1 < LAYERS:
            shares[l + 1] = pending
    width = block_input.shape[1]
    base = width // seq

    def by_slot(share):
        return share[:base].reshape(tp, -1, share.shape[1])

    blocks = [by_slot(shares[l][0]) for l in range(LAYERS)]
    blocks += [by_slot(shares[l][1]) for l in range(1, LAYERS)]
    gains, channel, *blocks = closing(
        seq, jnp.concatenate(gain_all, 0), jnp.concatenate(channel_all, 0), blocks
    )
    last = lax.all_to_all(
        by_slot(shares[0][1]), "rep", split_axis=0, concat_axis=0, axis_index_groups=plan.tp_groups
    )
    mlps, recs = blocks[:LAYERS], [last] + blocks[LAYERS:]
    outs = [
        owned_grads(plan, *shares[l], mlps[l], recs[l], width, head, units) for l in range(LAYERS)
    ]
    big = [jnp.stack([outs[l][i] for l in range(LAYERS)]) for i in range(8)]

    channel = lax.dynamic_slice_in_dim(channel, z * (head // seq), head // seq, 1)
    channel = to_owners(plan, channel, 1).reshape(LAYERS, 8, -1)
    if dp > 1:
        gains = lax.psum(gains, "rep", axis_index_groups=plan.dp_groups)
    own = gains.shape[1] // (plan.rep * seq)
    owner = lax.axis_index(("rep", "seq"))
    gains = lax.dynamic_slice_in_dim(gains, owner * own, own, 1).reshape(LAYERS, 2, own)
    return (
        residual.astype(BF),
        gradient,
        gains,
        big[0],
        big[1],
        channel[:, :CONV],
        channel[:, CONV],
        big[2],
        big[3],
        channel[:, CONV + 1 : CONV + 3],
        channel[:, CONV + 3],
        big[4],
        big[5],
        big[6],
        big[7],
    )


def solution(mesh):
    tokens = P(("rep", "seq"), None)
    rows = P(None, "seq", None)
    last3 = P(None, None, "seq")
    last2 = P(None, "seq")
    own_rows = P(None, ("rep", "seq"), None)
    own3 = P(None, None, ("rep", "seq"))
    own2 = P(None, ("rep", "seq"))

    def whole(*args):
        heads = args[9].shape[1] // args[9].shape[2]
        plan = Plan(mesh, heads)
        return jax.shard_map(
            partial(local, plan),
            mesh=mesh,
            in_specs=(
                tokens, tokens, P("rep"), P("rep"), last3, rows, rows, last3, last2, rows, rows,
                last3, last2, rows, rows, rows, rows,
            ),
            out_specs=(
                tokens, tokens, own3, own_rows, own_rows, own3, own2, own_rows, own_rows, own3,
                own2, own_rows, own_rows, own_rows, own_rows,
            ),
            check_vma=False,
        )(*args)

    return whole
```

time: 1580 us -> 939 us (0.59)
  waiting for transfers between devices: 706 us -> 81.3 us
  Pallas kernels: 302 us -> 737 us
  blocking collectives: 266 us -> 0 us
  matrix products: 94.4 us -> 0 us
  other arithmetic: 66.8 us -> 22.9 us
  local copies, waits for them, and re-layouts: 86.5 us -> 61.7 us
  starting transfers between devices: 33.2 us -> 9.74 us
    pallas_call x6 -> x8, Pallas kernels: 159 us -> 595 us  [the longest x2 197 us: rec_forward(): pl.pallas_call(partial(rec_forward_kernel, gathered), in_specs=[ANY, VM,...]
    reduce_scatter x10 -> x4, waiting for transfers between devices: 273 us -> 16.1 us  [over_seq(): return lax.psum_scatter(value, 'seq', scatter_dimension=0, tiled=False)]
    reduce_scatter x5 -> x0, waiting for transfers between devices: 251 us -> none  [the longest x4 236 us: scatter_plane(): lax.psum_scatter(value, 'rep', scatter_dimension=0, tiled=True, axis_inde...]
    all_gather x10 -> x0, blocking collectives: 210 us -> none  [the longest x2 62.7 us: local(): gates = lax.all_gather(gates, 'seq', axis=0, tiled=True)]
    all_gather x10 -> x3, waiting for transfers between devices: 173 us -> 60 us  [the longest x2 60 us: local(): lax.all_gather(pack, 'seq')]
    dot_general x22 -> x0, matrix products: 94.4 us -> none  [the longest x8 35.2 us: dot_nt(): lax.dot_general(a, b, (((1,), (1,)), ((), ())), preferred_element_type=F32)]
    psum x1 -> x0, blocking collectives: 39.6 us -> none  [local(): gains = lax.psum(jnp.stack(gain_all), ('rep', 'seq'))]
    reduce_sum x10 -> x0, other arithmetic: 21.8 us -> none  [the longest x2 7.6 us: gate_terms(): log_retain = -8.0 * rate_gate * jax.nn.softplus(-decay_logit)]
  transfers between devices with their start and end apart: 36 -> 12, of which waited for: 24 -> 5; matrix products, arithmetic and copies ran while one was open for 12% -> 6% of each run, Pallas kernels for 5% -> 59%
where the time goes in v3:
time: 939 us; the launch traced here: 929 us
  Pallas kernels  737 us (78%)
  waiting for transfers between devices  81.3 us (9%)
  local copies, waits for them, and re-layouts  61.7 us (7%)
  other arithmetic  22.9 us (2%)
  between operations  16.5 us (2%)
  starting transfers between devices  9.74 us (1%)
    pallas_call x2, Pallas kernels, rec_forward(): pl.pallas_call(partial(rec_forward_kernel, gathered), in_specs=[ANY, VM,...  197 us
    pallas_call x2, Pallas kernels, rec_backward(): pl.pallas_call(rec_backward_kernel, in_specs=[ANY, VM, VM, VM, ANY, VM, p...  182 us
    pallas_call x2, Pallas kernels, mlp_backward(): pl.pallas_call(mlp_backward_kernel, in_specs=[ANY, VM, VM, VM, ANY, ANY,...  142 us
    pallas_call x2, Pallas kernels, mlp_forward(): pl.pallas_call(mlp_forward_kernel, in_specs=[ANY, VM, VM, ANY], out_specs...  133 us
    all_gather x2, waiting for transfers between devices, local(): lax.all_gather(pack, 'seq')  60 us
    pallas_call x1, Pallas kernels, opening(): pl.pallas_call(open_kernel, in_specs=[VM, ANY, ANY, ANY, ANY], out_specs=...  54 us
    pallas_call x1, Pallas kernels, closing(): pl.pallas_call(close_kernel, in_specs=[VM, VM] + [ANY] * len(blocks), out...  30 us
  transfers between devices with their start and end apart: 12, of which 5 were waited for; matrix products, arithmetic and copies ran while one was open for 6% of the time, Pallas kernels for 59%

profile of v3, /device:TPU:0, one launch (start us, length us, event | category | flops | bytes accessed | tf_op | source)
XLA Modules:
  0.0 929.4 jit_solution(7603502565371378764)
XLA Ops:
  7.2 1.9 fusion.23
  9.1 1.8 fusion.24
  10.9 2.1 fusion.19
  17.2 3.7 collective-permute-start
  22.3 4.1 fusion.17
  26.4 1.9 fusion.18
  28.3 4.0 fusion.14
  33.0 2.3 fusion.15
  36.7 3.3 fusion.16
  40.0 2.0 dynamic-slice_bitcast_fusion.4
  43.4 1.9 dynamic-slice_bitcast_fusion.9
  45.3 1.8 dynamic-slice_bitcast_fusion.6
  47.1 2.4 dynamic-slice_bitcast_fusion.2
  51.8 54.0 %opening.1 = (f32[4,16,512]{2,1,0:T(8,128)S(1)}, f32[4,4,384]{2,1,0:T(4,128)S(1)}, s32[8,8,128]{2,1,0:T(8,128)S(1)}, bf16[8,256,1536]{2,1,0:T(8,128)(2,1)S(1)}, bf16[4,640,512]{2,1,0:T(8,128)(2,1)S(1)}) custom-call(bf16[256,1536]{1,0:T(8,128)(2,1)S(1)} %copy-done, f32[16,512]{1,0:T(8,128)S(1)} %fusion.2.small_ref, f32[4,384]{1,0:T(4,128)S(1)} %reshape.531.gain_ref, ...), custom_call_target="tpu_custom_call" | custom-call | flops 40000000000 | bytes 10485760 | tf_op jit(solution)/shard_map/opening/pallas_call | solution.py:1195
  105.8 2.6 copy-done.1
  115.8 97.9 %rec_forward_first.1 = (f32[256,1536]{1,0:T(8,128)}, bf16[256,1536]{1,0:T(8,128)(2,1)}, bf16[8,128]{1,0:T(8,128)(2,1)}, f32[8,256,256]{2,1,0:T(8,128)}, f32[8,26...) custom-call(bf16[8,256,1536]{2,1,0:T(8,128)(2,1)} %copy-done.1, ...), custom_call_target="tpu_custom_call" | custom-call | flops 70000001024 | bytes 31457280 | tf_op jit(solution)/shard_map/rec_forward_first/pallas_call | solution.py:804
  215.9 42.6 %all-gather.7.cloned.1.call-done = bf16[2304,1152]{1,0:T(8,128)(2,1)} async-done(((bf16[576,1152]{1,0:T(8,128)(2,1)}), bf16[2304,1152]{1,0:T(8,128)(2,1)}) %all-gather.7.cloned.1.call-update) | async-done | bytes 5308432 | tf_op jit(solution)/shard_map/all_gather | solution.py:1426
  258.5 66.1 %mlp_forward.2 = (f32[256,1536]{1,0:T(8,128)}, bf16[256,1536]{1,0:T(8,128)(2,1)}, bf16[8,256,1536]{2,1,0:T(8,128)(2,1)}, bf16[8,256,1152]{2,1,0:T(8,128)(2,1)}) custom-call(bf16[256,1536]{1,0:T(8,128)(2,1)} %get-tuple-element.83.x_ref, f32[256,1536]{1,0:T(8,128)} %get-tuple-element.84.residual_ref.values_ref, f32[1,1536]{1,0:T(1,128)} %get-tuple-element.203.gain_ref, ...), custom_call_target="tpu_custom_call" | custom-call | flops 60000002048 | bytes 31457280 | tf_op jit(solution)/shard_map/mlp_forward/pallas_call | solution.py:419
  325.3 1.7 dynamic-slice_bitcast_fusion
  330.7 99.2 %rec_forward.1 = (f32[256,1536]{1,0:T(8,128)}, bf16[256,1536]{1,0:T(8,128)(2,1)}, bf16[8,256,1536]{2,1,0:T(8,128)(2,1)}, f32[8,256,256]{2,1,0:T(8,128)}, f32[8,2...) custom-call(bf16[256,1536]{1,0:T(8,128)(2,1)} %get-tuple-element.87.x_ref, ...), custom_call_target="tpu_custom_call" | custom-call | flops 70000001024 | bytes 31457280 | tf_op jit(solution)/shard_map/rec_forward/pallas_call | solution.py:804
  430.0 17.4 %all-gather.11.cloned.1.call-done = bf16[2304,1152]{1,0:T(8,128)(2,1)} async-done(((bf16[576,1152]{1,0:T(8,128)(2,1)}), bf16[2304,1152]{1,0:T(8,128)(2,1)}) %all-gather.11.cloned.1.call-update) | async-done | bytes 5308432 | tf_op jit(solution)/shard_map/all_gather | solution.py:1426
  447.4 66.5 %mlp_forward.3 = (f32[256,1536]{1,0:T(8,128)}, bf16[256,1536]{1,0:T(8,128)(2,1)}, bf16[8,256,1536]{2,1,0:T(8,128)(2,1)}, bf16[8,256,1152]{2,1,0:T(8,128)(2,1)}) custom-call(bf16[256,1536]{1,0:T(8,128)(2,1)} %get-tuple-element.90.x_ref, f32[256,1536]{1,0:T(8,128)} %get-tuple-element.91.residual_ref.values_ref, f32[1,1536]{1,0:T(1,128)} %get-tuple-element.202.gain_ref, ...), custom_call_target="tpu_custom_call" | custom-call | flops 60000002048 | bytes 31457280 | tf_op jit(solution)/shard_map/mlp_forward/pallas_call | solution.py:419
  513.9 70.6 %mlp_backward.2 = (f32[256,1536]{1,0:T(8,128)}, bf16[256,1536]{1,0:T(8,128)(2,1)}, f32[1,1536]{1,0:T(1,128)}, bf16[4,576,1152]{2,1,0:T(8,128)(2,1)}) custom-call(bf16[256,1536]{1,0:T(8,128)(2,1)} %get-tuple-element.160.g_ref, f32[256,1536]{1,0:T(8,128)} %get-tuple-element.159.upstream_ref, f32[256,1536]{1,0:T(8,128)} %get-tuple-element.91.residual_ref.values_ref, ...), custom_call_target="tpu_custom_call" | custom-call | flops 70000001024 | bytes 31457280 | tf_op jit(solution)/shard_map/mlp_backward/pallas_call | solution.py:531
  584.6 89.2 %rec_backward.2 = (f32[256,1536]{1,0:T(8,128)}, bf16[256,1536]{1,0:T(8,128)(2,1)}, f32[1,1536]{1,0:T(1,128)}, bf16[4,640,512]{2,1,0:T(8,128)(2,1)}, f32[8,256]{1,0:T(8,128)}) custom-call(bf16[256,1536]{1,0:T(8,128)(2,1)} %get-tuple-element.96.g_ref, f32[256,1536]{1,0:T(8,128)} %get-tuple-element.97.upstream_ref, ...), custom_call_target="tpu_custom_call" | custom-call | flops 80000000000 | bytes 31457280 | tf_op jit(solution)/shard_map/rec_backward/pallas_call | solution.py:1061
  673.8 6.5 reduce-scatter.5.cloned.1.call-done
  680.4 71.4 %mlp_backward.3 = (f32[256,1536]{1,0:T(8,128)}, bf16[256,1536]{1,0:T(8,128)(2,1)}, f32[1,1536]{1,0:T(1,128)}, bf16[4,576,1152]{2,1,0:T(8,128)(2,1)}) custom-call(bf16[256,1536]{1,0:T(8,128)(2,1)} %get-tuple-element.107.g_ref, f32[256,1536]{1,0:T(8,128)} %get-tuple-element.108.upstream_ref, f32[256,1536]{1,0:T(8,128)} %get-tuple-element.84.residual_ref.values_ref, ...), custom_call_target="tpu_custom_call" | custom-call | flops 70000001024 | bytes 31457280 | tf_op jit(solution)/shard_map/mlp_backward/pallas_call | solution.py:531
  755.7 92.4 %rec_backward.3 = (f32[256,1536]{1,0:T(8,128)}, bf16[256,1536]{1,0:T(8,128)(2,1)}, f32[1,1536]{1,0:T(1,128)}, bf16[4,640,512]{2,1,0:T(8,128)(2,1)}, f32[8,256]{1,0:T(8,128)}) custom-call(bf16[256,1536]{1,0:T(8,128)(2,1)} %get-tuple-element.113.g_ref, f32[256,1536]{1,0:T(8,128)} %get-tuple-element.114.upstream_ref, ...), custom_call_target="tpu_custom_call" | custom-call | flops 80000000000 | bytes 31457280 | tf_op jit(solution)/shard_map/rec_backward/pallas_call | solution.py:1061
  853.1 30.0 %closing.1 = (f32[4,1536]{1,0:T(4,128)S(1)}, f32[16,256]{1,0:T(8,128)S(1)}, bf16[8,48,1152]{2,1,0:T(8,128)(2,1)S(1)}, bf16[8,48,1152]{2,1,0:T(8,128)(2,1)S(1)}, bf16[8,48,512]{2,1,0:T(8,128)(2,1)S(1)}) custom-call(f32[4,1536]{1,0:T(4,128)S(1)} %pad_maximum_fusion.4.gain_ref, f32[16,256]{1,0:T(8,128)S(1)} %pad_maximum_fusion.5.channel_ref, ...), custom_call_target="tpu_custom_call" | custom-call | flops 40000000000 | bytes 10485760 | tf_op jit(solution)/shard_map/closing/pallas_call | solution.py:1291
  895.5 9.6 %reduce-scatter.11.cloned.1.call-done = bf16[1,640,512]{2,1,0:T(8,128)(2,1)} async-done(((bf16[4,640,512]{2,1,0:T(8,128)(2,1)}), bf16[1,640,512]{2,1,0:T(8,128)(2,1)}) %reduce-scatter.11.cloned.1.call-update) | async-done | bytes 655376 | tf_op jit(solution)/shard_map/reduce_scatter | solution.py:1334
  905.1 1.8 slice.379
  906.9 3.7 all-to-all-start
  913.9 5.0 all-to-all-done
  (204 shorter events, 51.6 us)
Async XLA Ops:
  7.2 251.3 %all-gather.7.cloned.1.call-start = ((), (), s32[]{:S(2)}) async-start(), calls=%async_computation.9 | async-start | bytes 6635520 | tf_op jit(solution)/shard_map/all_gather | solution.py:1426
  12.9 9.2 copy-start.37
  13.0 9.2 copy-start.38
  16.4 11.8 %slice-start = ((s8[7077888]{0:T(1024)(128)(4,1)}), s8[2883584]{0:T(1024)(128)(4,1)S(1)}, s32[]{:S(2)}) async-start(s8[7077888]{0:T(1024)(128)(4,1)} %bitcast.169), calls=%async_computation.12 | async-start | bytes 5767168
  17.2 33.4 %collective-permute-start = (bf16[256,512]{1,0:T(8,128)(2,1)}, bf16[256,512]{1,0:T(8,128)(2,1)}, u32[]{:S(2)}, u32[]{:S(2)}) collective-permute-start(bf16[256,512]{1,0:T(8,128)(2,1)} %maximum_maximum_fusion.3), channel_id=1, source_target_pairs={{0,0},{1,8},{2,16},{3,24},{4,1},{5,9},{6,17},{7,25},{8,2},{9,10},{... | collective-permute-start | bytes 786440 | tf_op jit(solution)/shard_map/ppermute | solution.py:52
  51.8 58.8 %copy-start.6 = (bf16[144,1536]{1,0:T(8,128)(2,1)S(1)}, bf16[144,1536]{1,0:T(8,128)(2,1)}, u32[]{:S(2)}) copy-start(bf16[144,1536]{1,0:T(8,128)(2,1)} %get-tuple-element.207) | copy-start | bytes 1327108
  51.8 58.9 %copy-start.18 = (bf16[64,1536]{1,0:T(8,128)(2,1)S(1)}, bf16[64,1536]{1,0:T(8,128)(2,1)}, u32[]{:S(2)}) copy-start(bf16[64,1536]{1,0:T(8,128)(2,1)} %get-tuple-element.211) | copy-start | bytes 589828
  51.8 58.9 %copy-start.4 = (bf16[384,576]{1,0:T(8,128)(2,1)S(1)}, bf16[384,576]{1,0:T(8,128)(2,1)}, u32[]{:S(2)}) copy-start(bf16[384,576]{1,0:T(8,128)(2,1)} %get-tuple-element.220) | copy-start | bytes 1327108
  51.8 58.9 %copy-start.5 = (bf16[384,576]{1,0:T(8,128)(2,1)S(1)}, bf16[384,576]{1,0:T(8,128)(2,1)}, u32[]{:S(2)}) copy-start(bf16[384,576]{1,0:T(8,128)(2,1)} %get-tuple-element.221) | copy-start | bytes 1327108
  109.9 0.8 collective-permute-start.1
  112.1 218.6 %all-gather.9.cloned.1.call-start = ((), (), s32[]{:S(2)}) async-start(), calls=%async_computation.10 | async-start | bytes 3276800 | tf_op jit(solution)/shard_map/all_gather | solution.py:1433
  114.4 99.2 %copy-start.25 = (f32[2,8,2048]{2,1,0:T(8,128)}, f32[2,8,2048]{2,1,0:T(8,128)S(1)}, u32[]{:S(2)}) copy-start(f32[2,8,2048]{2,1,0:T(8,128)S(1)} %reshape.516) | copy-start | bytes 393220
  115.8 99.2 %copy-start.16 = (bf16[384,256]{1,0:T(8,128)(2,1)S(1)}, bf16[384,256]{1,0:T(8,128)(2,1)}, u32[]{:S(2)}) copy-start(bf16[384,256]{1,0:T(8,128)(2,1)} %get-tuple-element.214) | copy-start | bytes 589828
  115.8 99.2 %copy-start.17 = (bf16[384,256]{1,0:T(8,128)(2,1)S(1)}, bf16[384,256]{1,0:T(8,128)(2,1)}, u32[]{:S(2)}) copy-start(bf16[384,256]{1,0:T(8,128)(2,1)} %get-tuple-element.215) | copy-start | bytes 589828
  213.7 1.3 collective-permute-start.2
  215.9 231.5 %all-gather.11.cloned.1.call-start = ((), (), s32[]{:S(2)}) async-start(), calls=%async_computation.11 | async-start | bytes 6635520 | tf_op jit(solution)/shard_map/all_gather | solution.py:1426
  324.6 2.4 collective-permute-start.3
  328.4 351.9 %reduce-scatter.5.cloned.1.call-start = ((), (), s32[]{:S(2)}) async-start(), calls=%async_computation.5 | async-start | bytes 6635520 | tf_op jit(solution)/shard_map/reduce_scatter | solution.py:1334
  584.5 171.1 %reduce-scatter.7.cloned.1.call-start = ((), (), s32[]{:S(2)}) async-start(), calls=%async_computation.6 | async-start | bytes 3276800 | tf_op jit(solution)/shard_map/reduce_scatter | solution.py:1334
  680.3 171.4 %reduce-scatter.9.cloned.1.call-start = ((), (), s32[]{:S(2)}) async-start(), calls=%async_computation.7 | async-start | bytes 6635520 | tf_op jit(solution)/shard_map/reduce_scatter | solution.py:1334
  751.8 153.3 %reduce-scatter.11.cloned.1.call-start = ((), (), s32[]{:S(2)}) async-start(), calls=%async_computation.8 | async-start | bytes 3276800 | tf_op jit(solution)/shard_map/reduce_scatter | solution.py:1334
  755.6 92.4 %copy-start.20 = (bf16[1,640,512]{2,1,0:T(8,128)(2,1)S(1)}, bf16[1,640,512]{2,1,0:T(8,128)(2,1)}, u32[]{:S(2)}) copy-start(bf16[1,640,512]{2,1,0:T(8,128)(2,1)} %reduce-scatter.7.cloned.1.call-done) | copy-start | bytes 1966084
  755.6 92.5 %copy-start.30 = (f32[8,256]{1,0:T(8,128)S(1)}, f32[8,256]{1,0:T(8,128)}, u32[]{:S(2)}) copy-start(f32[8,256]{1,0:T(8,128)} %get-tuple-element.125) | copy-start | bytes 24580
  755.7 94.0 %copy-start.32 = (f32[1,1536]{1,0:T(1,128)S(1)}, f32[1,1536]{1,0:T(1,128)}, u32[]{:S(2)}) copy-start(f32[1,1536]{1,0:T(1,128)} %get-tuple-element.123) | copy-start | bytes 18436
  755.7 94.0 %copy-start.33 = (f32[1,1536]{1,0:T(1,128)S(1)}, f32[1,1536]{1,0:T(1,128)}, u32[]{:S(2)}) copy-start(f32[1,1536]{1,0:T(1,128)} %get-tuple-element.122) | copy-start | bytes 18436
  755.7 94.0 %copy-start.34 = (f32[1,1536]{1,0:T(1,128)S(1)}, f32[1,1536]{1,0:T(1,128)}, u32[]{:S(2)}) copy-start(f32[1,1536]{1,0:T(1,128)} %get-tuple-element.121) | copy-start | bytes 18436
  895.5 16.0 %copy-start.29 = (bf16[1,64,256]{2,1,0:T(8,128)(2,1)S(1)}, bf16[1,64,256]{2,1,0:T(8,128)(2,1)}, u32[]{:S(2)}) copy-start(bf16[1,64,256]{2,1,0:T(8,128)(2,1)} %get-tuple-element.168) | copy-start | bytes 98308
  895.5 16.7 %copy-start.28 = (bf16[1,64,256]{2,1,0:T(8,128)(2,1)S(1)}, bf16[1,64,256]{2,1,0:T(8,128)(2,1)}, u32[]{:S(2)}) copy-start(bf16[1,64,256]{2,1,0:T(8,128)(2,1)} %get-tuple-element.169) | copy-start | bytes 98308
  895.5 17.4 %copy-start.22 = (bf16[1,64,512]{2,1,0:T(8,128)(2,1)S(1)}, bf16[1,64,512]{2,1,0:T(8,128)(2,1)}, u32[]{:S(2)}) copy-start(bf16[1,64,512]{2,1,0:T(8,128)(2,1)} %get-tuple-element.165) | copy-start | bytes 196612
  895.5 17.4 %copy-start.23 = (bf16[1,64,512]{2,1,0:T(8,128)(2,1)S(1)}, bf16[1,64,512]{2,1,0:T(8,128)(2,1)}, u32[]{:S(2)}) copy-start(bf16[1,64,512]{2,1,0:T(8,128)(2,1)} %get-tuple-element.166) | copy-start | bytes 196612
  895.5 17.4 %copy-start.24 = (bf16[1,64,512]{2,1,0:T(8,128)(2,1)S(1)}, bf16[1,64,512]{2,1,0:T(8,128)(2,1)}, u32[]{:S(2)}) copy-start(bf16[1,64,512]{2,1,0:T(8,128)(2,1)} %get-tuple-element.167) | copy-start | bytes 196612
  906.9 12.0 %all-to-all-start = ((bf16[8,48,512]{2,1,0:T(8,128)(2,1)}), bf16[8,48,512]{2,1,0:T(8,128)(2,1)S(1)}, u32[]{:S(2)}, u32[]{:S(2)}) async-start(bf16[8,48,512]{2,1,0:T(8,128)(2,1)} %bitcast.54), calls=%async_computation.4 | async-start | bytes 786432 | tf_op jit(solution)/shard_map/all_to_all | solution.py:1464
  (25 other events, 93.7 us)
Sparse Core Ops, SparseCore 0:
  112.2 146.2 all-gather.6
  260.6 53.9 all-gather.8
  328.5 118.8 all-gather.10
  584.7 95.6 reduce-scatter.4
  682.6 52.5 reduce-scatter.6
  751.9 96.7 reduce-scatter.8
  851.9 53.1 reduce-scatter.10

commit v4 on v3

--- a/solution.py
+++ b/solution.py
@@ -94,12 +94,12 @@
     def device(self, m, s):
         return (self.base + self.slot(m, s), self.z)
 
-    def enter(self, extra=()):
+    def enter(self, extra=(), more=0):
         barrier = pltpu.get_barrier_semaphore()
         devices = [self.device(1, 0), self.device(2, 0), self.device(0, 1)] + list(extra)
         for device in devices:
             pl.semaphore_signal(barrier, inc=1, device_id=device, device_id_type=MESH)
-        pl.semaphore_wait(barrier, len(devices))
+        pl.semaphore_wait(barrier, len(devices) + more)
 
 
 def remote(src, dst, send, recv, device):
@@ -1103,8 +1103,8 @@
 
 
 def open_kernel(
-    x_ref, small_ref, gain_ref, slot_ref, pack_ref,
-    small_out, gain_out, slot_out, full_out, pack_out,
+    x_ref, small_ref, gain_ref, slot_ref, pack_ref, col_ref, rows_ref, later_ref,
+    small_out, gain_out, slot_out, full_out, pack_out, mlp_out, later_out,
     full, smalls, gains, slots, gs, gr, ps, pr, sem,
 ):
     net = Net()
@@ -1117,10 +1117,27 @@
         pltpu.make_async_copy(gain_ref, gains.at[net.z], sem.at[1]),
         pltpu.make_async_copy(slot_ref, slots.at[net.t], sem.at[2]),
     ]
-    own_pack = pltpu.make_async_copy(pack_ref, pack_out.at[net.z], sem.at[4])
-    for copy in mine + [own_pack]:
+    col_rows = col_ref.shape[0]
+    below = mlp_out.at[pl.ds(col_rows, rows_ref.shape[0])]
+    here = [
+        pltpu.make_async_copy(pack_ref, pack_out.at[net.z], sem.at[4]),
+        pltpu.make_async_copy(col_ref, mlp_out.at[pl.ds(0, col_rows)], sem.at[5]),
+    ]
+    for copy in mine + here:
         copy.start()
-    net.enter(line.others + [net.device(1, 1), net.device(2, 1), net.device(3, 0), net.device(3, 1)])
+    held, owned = TP * net.z + net.t, seq * net.t + net.z
+    owner, giver = (held // seq, lax.rem(held, seq)), (lax.rem(owned, TP), owned // TP)
+    away = held != owned
+    barrier = pltpu.get_barrier_semaphore()
+
+    @pl.when(away)
+    def _():
+        for t, z in (owner, giver):
+            pl.semaphore_signal(barrier, inc=1, device_id=(net.base + t, z), device_id_type=MESH)
+    net.enter(
+        line.others + [net.device(1, 1), net.device(2, 1), net.device(3, 0), net.device(3, 1)],
+        jnp.where(away, 2, 0),
+    )
     for copy in mine:
         copy.wait()
 
@@ -1140,13 +1157,69 @@
         push(slots, net.t, net.slot(m, s), to)
     for copy in sends:
         copy.start()
-    small_sends, small_arrivals = list(sends), list(arrivals)
-    for d, to in enumerate(line.others):
-        n = len(sends)
-        source = lax.rem(net.z + seq - 1 - d, seq)
-        sends.append(remote(pack_ref, pack_out.at[net.z], ps.at[n], pr.at[n], to))
-        arrivals.append(remote(pack_ref, pack_out.at[source], ps.at[n], pr.at[n], to))
-        sends[-1].start()
+    first = len(sends)
+
+    def hop(way, e):
+        n = first + 2 * e + (0 if way > 0 else 1)
+        to = (net.base + net.t, net.z + way)
+        at = pack_ref if e == 0 else pack_out.at[net.z - way * e]
+        lands = pack_out.at[net.z - way * e]
+        return remote(at, lands, ps.at[n], pr.at[n], to)
+
+    def forward(way, e):
+        place = net.z if way > 0 else seq - 1 - net.z
+
+        @pl.when((place >= e) & (place < seq - 1))
+        def _():
+            if e > 0:
+                landed(way, e - 1)
+            hop(way, e).start()
+
+        if e > 0:
+            @pl.when((place >= e) & (place == seq - 1))
+            def _():
+                landed(way, e - 1)
+
+    def landed(way, e):
+        n = first + 2 * e + (0 if way > 0 else 1)
+        from_at = pack_out.at[net.z - way * (e + 1)]
+        remote(from_at, from_at, ps.at[n], pr.at[n], (net.base + net.t, net.z)).wait_recv()
+
+    def last(way):
+        place = net.z if way > 0 else seq - 1 - net.z
+
+        @pl.when(place == seq - 1)
+        def _():
+            landed(way, seq - 2)
+
+        for e in range(seq - 1):
+            @pl.when((place >= e) & (place < seq - 1))
+            def _():
+                hop(way, e).wait_send()
+
+    forward(1, 0)
+    forward(-1, 0)
+    n = first + 2 * (seq - 1)
+    owner_id = (net.base + owner[0], owner[1])
+    moved = [
+        remote(rows_ref, below, ps.at[n], pr.at[n], owner_id),
+        remote(later_ref, later_out, ps.at[n + 1], pr.at[n + 1], owner_id),
+    ]
+    kept = [
+        pltpu.make_async_copy(rows_ref, below, sem.at[6]),
+        pltpu.make_async_copy(later_ref, later_out, sem.at[7]),
+    ]
+
+    @pl.when(away)
+    def _():
+        for copy in moved:
+            copy.start()
+
+    @pl.when(held == owned)
+    def _():
+        for copy in kept:
+            copy.start()
+
     for copy in arrivals[: seq - 1]:
         copy.wait_recv()
     rows, width = x_ref.shape
@@ -1165,7 +1238,7 @@
 
     lax.fori_loop(0, rows // chunk, norm, 0)
     gather.begin()
-    for copy in small_arrivals[seq - 1 :]:
+    for copy in arrivals[seq - 1 :]:
         copy.wait_recv()
     saves = [
         pltpu.make_async_copy(a, b, sem.at[n])
@@ -1175,40 +1248,60 @@
         save.start()
     for n in range(1, TP):
         gather.before(n)
+        if n == 2:
+            forward(1, 1)
+            forward(-1, 1)
     gather.finish()
     saves.append(pltpu.make_async_copy(full, full_out, sem.at[3]))
     saves[-1].start()
-    for copy in arrivals[len(small_arrivals) :]:
-        copy.wait_recv()
+    for e in range(2, seq - 1):
+        forward(1, e)
+        forward(-1, e)
+    last(1)
+    last(-1)
+
+    @pl.when(away)
+    def _():
+        for copy in moved:
+            copy.wait()
+
+    @pl.when(held == owned)
+    def _():
+        for copy in kept:
+            copy.wait()
+
     for copy in sends:
         copy.wait_send()
-    own_pack.wait()
+    for copy in here:
+        copy.wait()
     for save in saves:
         save.wait()
 
 
-def opening(seq, x, small, gain, slot, pack):
+def opening(seq, x, small, gain, slot, pack, col, below, later):
     rows, width = x.shape
     shape = jax.ShapeDtypeStruct
     dma = pltpu.SemaphoreType.DMA
-    pushes = 3 * (seq - 1) + TP - 1
+    pushes = 4 * (seq - 1) + TP - 1 + 2
     return pl.pallas_call(
         open_kernel,
-        in_specs=[VM, ANY, ANY, ANY, ANY],
-        out_specs=[ANY] * 5,
+        in_specs=[VM] + [ANY] * 7,
+        out_specs=[ANY] * 7,
         out_shape=[
             shape((seq,) + small.shape, F32),
             shape((seq,) + gain.shape, F32),
             shape((TP,) + slot.shape, jnp.int32),
             shape((TP, rows, width), BF),
             shape((seq,) + pack.shape, BF),
+            shape((col.shape[0] + below.shape[0], col.shape[1]), BF),
+            shape(later.shape, BF),
         ],
         scratch_shapes=[
             pltpu.VMEM((TP, rows, width), BF),
             pltpu.VMEM((seq,) + small.shape, F32),
             pltpu.VMEM((seq,) + gain.shape, F32),
             pltpu.VMEM((TP,) + slot.shape, jnp.int32),
-            dma((10,)), dma((10,)), dma((pushes,)), dma((pushes,)), dma((5,)),
+            dma((10,)), dma((10,)), dma((pushes,)), dma((pushes,)), dma((8,)),
         ],
         compiler_params=pltpu.CompilerParams(
             collective_id=6, has_side_effects=True, vmem_limit_bytes=40 << 20
@@ -1217,7 +1310,7 @@
             flops=40 * 10**9, bytes_accessed=10 << 20, transcendentals=0
         ),
         name="opening",
-    )(x, small, gain, slot, pack)
+    )(x, small, gain, slot, pack, col, below, later)
 
 
 def close_kernel(
@@ -1375,12 +1468,13 @@
     small = jnp.concatenate([conv_kernel, conv_bias[:, None], gate_bias, decay_logit[:, None]], 1)
     small = small.reshape(LAYERS * 8, channels).astype(F32)
     slot = jnp.pad(jnp.stack([lengths, offsets], 1), ((0, 7), (0, 126)))
-    def col(weight, layer, width):
-        return lax.dynamic_slice_in_dim(weight[layer], t * width, width, 1)
-
-    def chunk(weight, layer):
+    def col(weight, layer, width, t):
+        size = (1, weight.shape[1], width)
+        return lax.dynamic_slice(weight, (layer, 0, t * width), size)[0]
+
+    def chunk(weight, layer, t):
         size = weight.shape[1] // tp
-        return lax.dynamic_slice_in_dim(weight[layer], t * size, size, 0)
+        return lax.dynamic_slice(weight, (layer, t * size, 0), (1, size, weight.shape[2]))[0]
 
     def below(rows, twice):
         rest, blocks = mlp_split(rows.shape[1], twice)
@@ -1388,23 +1482,28 @@
         side = [rows[i * low : (i + 1) * low, twice:] for i in range(blocks)]
         return jnp.concatenate([rows[:, :twice], jnp.concatenate(side, 1)], 0)
 
-    def rec_pack(l, ready):
-        out = chunk(out_proj, l)
-        gates = jnp.concatenate([chunk(rate_proj, l), chunk(admit_proj, l)], 1)
+    def rec_rows(l, t):
+        out = chunk(out_proj, l, t)
+        gates = jnp.concatenate([chunk(rate_proj, l, t), chunk(admit_proj, l, t)], 1)
         out = [out[:, i * 2 * head : (i + 1) * 2 * head] for i in range(3)] + [gates]
-        out, ready = lax.optimization_barrier((jnp.concatenate(out, 0), ready))
-        rec = jnp.concatenate([col(branch_proj, l, head), col(stream_proj, l, head)], 1)
-        return jnp.concatenate([rec, owner_chunks(plan, out)], 0), ready
-
-    def mlp_pack(l, ready):
-        down, ready = lax.optimization_barrier((below(chunk(mlp_down, l), 2 * units), ready))
-        mlp = jnp.concatenate([col(mlp_gate, l, units), col(mlp_up, l, units)], 1)
-        return jnp.concatenate([mlp, owner_chunks(plan, down)], 0), ready
-
-    pack, _ = rec_pack(0, ())
-    smalls, gains, layout, normed, rec = opening(
-        seq, block_input, small, norm_gains.reshape(2 * LAYERS, -1).astype(F32), slot, pack
+        return jnp.concatenate(out, 0)
+
+    def rec_pack(l, rows_of, t):
+        rec = jnp.concatenate([col(branch_proj, l, head, t), col(stream_proj, l, head, t)], 1)
+        return jnp.concatenate([rec, rows_of], 0)
+
+    def mlp_rows(l, t):
+        return below(chunk(mlp_down, l, t), 2 * units)
+
+    def mlp_cols(l, t):
+        return jnp.concatenate([col(mlp_gate, l, units, t), col(mlp_up, l, units, t)], 1)
+
+    pack = rec_pack(0, owner_chunks(plan, rec_rows(0, t)), t)
+    smalls, gains, layout, normed, rec, mlp, rec_owned = opening(
+        seq, block_input, small, norm_gains.reshape(2 * LAYERS, -1).astype(F32), slot, pack,
+        mlp_cols(0, t), mlp_rows(0, t), rec_rows(1, t),
     )
+    mlp, rec = lax.optimization_barrier((mlp, rec))
     layout = layout[:, 0, :2]
     gains = jnp.moveaxis(gains, 0, 1).reshape(LAYERS, 2, -1)
     smalls = jnp.moveaxis(smalls, 0, 1).reshape(LAYERS, 8, -1)
@@ -1414,23 +1513,23 @@
     residual = block_input.astype(F32)
     saved_all, weights = [], []
     for l in range(LAYERS):
-        if l == 0:
-            pack, rec = mlp_pack(l, rec)
-        else:
-            pack, normed = mlp_pack(l, normed)
+        if l > 0:
+            mlp_owned, t, normed = lax.optimization_barrier((mlp_owned, t, normed))
+            mlp = jnp.concatenate([mlp_cols(l, t), mlp_owned], 0)
         w = dict(
             gain=gains[l],
             small=jnp.concatenate([smalls[l, :7], -8.0 * jax.nn.softplus(-smalls[l, 7:])], 0),
             decay=smalls[l, 7:],
             rec=rec,
-            mlp=lax.all_gather(pack, "seq"),
+            mlp=lax.all_gather(mlp, "seq"),
         )
         weights.append(w)
         kept = rec_forward(normed, residual, w["gain"][1], w["rec"], w["small"], layout)
         middle, normed_two, *kept = kept
         if l + 1 < LAYERS:
-            pack, normed_two = rec_pack(l + 1, normed_two)
-            rec = lax.all_gather(pack, "seq")
+            rows_of, t, normed_two = lax.optimization_barrier((rec_owned, t, normed_two))
+            rec = lax.all_gather(rec_pack(l + 1, rows_of, t), "seq")
+            mlp_owned = owner_chunks(plan, mlp_rows(l + 1, t))
         output, normed, *kept_two = mlp_forward(
             normed_two, middle, gains[(l + 1) % LAYERS, 0], w["mlp"]
         )

time: 939 us -> 894 us (0.952)
  local copies, waits for them, and re-layouts: 61.7 us -> 34.2 us
  Pallas kernels: 737 us -> 721 us
    pallas_call x2, Pallas kernels: 197 us -> 142 us  [rec_forward(): pl.pallas_call(partial(rec_forward_kernel, gathered), in_specs=[ANY, VM,...]
    pallas_call x1, Pallas kernels: 54 us -> 92.1 us  [opening(): pl.pallas_call(open_kernel, in_specs=[VM] + [ANY] * 7, out_specs=[ANY] *...]
    slice x10 -> x1, local copies, waits for them, and re-layouts: 21.4 us -> 0.03 us  [rec_rows(): out = [out[:, i * 2 * head:(i + 1) * 2 * head] for i in range(3)] + [gates]]
    dynamic_slice x8 -> x0, local copies, waits for them, and re-layouts: 13.2 us -> none  [the longest x4 7.82 us: col(): return lax.dynamic_slice_in_dim(weight[layer], t * width, width, 1)]
    squeeze x0 -> x10, local copies, waits for them, and re-layouts: none -> 11.3 us  [the longest x6 7.24 us: col(): return lax.dynamic_slice(weight, (layer, 0, t * width), size)[0]]
  transfers between devices with their start and end apart: 12 -> 10, of which waited for: 5 -> 5; matrix products, arithmetic and copies ran while one was open for 6% -> 4% of each run, Pallas kernels for 59% -> 55%
where the time goes in v4:
time: 894 us; the launch traced here: 885 us
  Pallas kernels  721 us (81%)
  waiting for transfers between devices  89.2 us (10%)
  local copies, waits for them, and re-layouts  34.2 us (4%)
  other arithmetic  19.2 us (2%)
  between operations  16.8 us (2%)
    pallas_call x2, Pallas kernels, rec_backward(): pl.pallas_call(rec_backward_kernel, in_specs=[ANY, VM, VM, VM, ANY, VM, p...  182 us
    pallas_call x2, Pallas kernels, rec_forward(): pl.pallas_call(partial(rec_forward_kernel, gathered), in_specs=[ANY, VM,...  142 us
    pallas_call x2, Pallas kernels, mlp_backward(): pl.pallas_call(mlp_backward_kernel, in_specs=[ANY, VM, VM, VM, ANY, ANY,...  142 us
    pallas_call x2, Pallas kernels, mlp_forward(): pl.pallas_call(mlp_forward_kernel, in_specs=[ANY, VM, VM, ANY], out_specs...  133 us
    pallas_call x1, Pallas kernels, opening(): pl.pallas_call(open_kernel, in_specs=[VM] + [ANY] * 7, out_specs=[ANY] *...  92.1 us
    all_gather x2, waiting for transfers between devices, local(): lax.all_gather(mlp, 'seq')  67.2 us
    pallas_call x1, Pallas kernels, closing(): pl.pallas_call(close_kernel, in_specs=[VM, VM] + [ANY] * len(blocks), out...  30 us
  transfers between devices with their start and end apart: 10, of which 5 were waited for; matrix products, arithmetic and copies ran while one was open for 4% of the time, Pallas kernels for 55%

profile of v4, /device:TPU:0, one launch (start us, length us, event | category | flops | bytes accessed | tf_op | source)
XLA Modules:
  0.0 885.5 jit_solution(11274407407915960141)
XLA Ops:
  12.6 1.3 convert_element_type.181.residual_ref.values_ref
  13.9 1.1 dynamic-slice_bitcast_fusion.10
  15.0 1.7 dynamic-slice_bitcast_fusion.2
  17.2 92.1 %opening.1 = (f32[4,16,512]{2,1,0:T(8,128)S(1)}, f32[4,4,384]{2,1,0:T(4,128)S(1)}, s32[8,8,128]{2,1,0:T(8,128)S(1)}, bf16[8,256,1536]{2,1,0:T(8,128)(2,1)S(1)}, ...) custom-call(bf16[256,1536]{1,0:T(8,128)(2,1)S(1)} %copy-done, ...), custom_call_target="tpu_custom_call" | custom-call | flops 40000000000 | bytes 10485760 | tf_op jit(solution)/shard_map/opening/pallas_call | solution.py:1286
  109.3 2.6 copy-done.1
  111.9 1.5 copy-done.2
  115.7 62.3 %rec_forward_first.1 = (f32[256,1536]{1,0:T(8,128)}, bf16[256,1536]{1,0:T(8,128)(2,1)}, bf16[8,128]{1,0:T(8,128)(2,1)}, f32[8,256,256]{2,1,0:T(8,128)}, f32[8,26...) custom-call(bf16[8,256,1536]{2,1,0:T(8,128)(2,1)} %copy-done.1, ...), custom_call_target="tpu_custom_call" | custom-call | flops 70000001024 | bytes 31457280 | tf_op jit(solution)/shard_map/rec_forward_first/pallas_call | solution.py:804
  183.3 50.5 %all-gather.7.cloned.1.call-done = bf16[2304,1152]{1,0:T(8,128)(2,1)} async-done(((bf16[576,1152]{1,0:T(8,128)(2,1)}), bf16[2304,1152]{1,0:T(8,128)(2,1)}) %all-gather.7.cloned.1.call-update) | async-done | bytes 5308432 | tf_op jit(solution)/shard_map/all_gather | solution.py:1524
  233.8 66.1 %mlp_forward.2 = (f32[256,1536]{1,0:T(8,128)}, bf16[256,1536]{1,0:T(8,128)(2,1)}, bf16[8,256,1536]{2,1,0:T(8,128)(2,1)}, bf16[8,256,1152]{2,1,0:T(8,128)(2,1)}) custom-call(bf16[256,1536]{1,0:T(8,128)(2,1)} %get-tuple-element.90.x_ref, f32[256,1536]{1,0:T(8,128)} %get-tuple-element.91.residual_ref.values_ref, f32[1,1536]{1,0:T(1,128)} %get-tuple-element.201.gain_ref, ...), custom_call_target="tpu_custom_call" | custom-call | flops 60000002048 | bytes 31457280 | tf_op jit(solution)/shard_map/mlp_forward/pallas_call | solution.py:419
  299.9 1.3 dynamic-slice_bitcast_fusion
  301.2 1.3 dynamic-slice_bitcast_fusion.1
  302.5 1.4 fusion
  304.0 1.6 convert_multiply_fusion
  306.2 79.9 %rec_forward.1 = (f32[256,1536]{1,0:T(8,128)}, bf16[256,1536]{1,0:T(8,128)(2,1)}, bf16[8,256,1536]{2,1,0:T(8,128)(2,1)}, f32[8,256,256]{2,1,0:T(8,128)}, f32[8,2...) custom-call(bf16[256,1536]{1,0:T(8,128)(2,1)} %get-tuple-element.94.x_ref, ...), custom_call_target="tpu_custom_call" | custom-call | flops 70000001024 | bytes 31457280 | tf_op jit(solution)/shard_map/rec_forward/pallas_call | solution.py:804
  386.2 16.8 %all-gather.11.cloned.1.call-done = bf16[2304,1152]{1,0:T(8,128)(2,1)} async-done(((bf16[576,1152]{1,0:T(8,128)(2,1)}), bf16[2304,1152]{1,0:T(8,128)(2,1)}) %all-gather.11.cloned.1.call-update) | async-done | bytes 5308432 | tf_op jit(solution)/shard_map/all_gather | solution.py:1524
  403.0 66.4 %mlp_forward.3 = (f32[256,1536]{1,0:T(8,128)}, bf16[256,1536]{1,0:T(8,128)(2,1)}, bf16[8,256,1536]{2,1,0:T(8,128)(2,1)}, bf16[8,256,1152]{2,1,0:T(8,128)(2,1)}) custom-call(bf16[256,1536]{1,0:T(8,128)(2,1)} %get-tuple-element.97.x_ref, f32[256,1536]{1,0:T(8,128)} %get-tuple-element.98.residual_ref.values_ref, f32[1,1536]{1,0:T(1,128)} %get-tuple-element.200.gain_ref, ...), custom_call_target="tpu_custom_call" | custom-call | flops 60000002048 | bytes 31457280 | tf_op jit(solution)/shard_map/mlp_forward/pallas_call | solution.py:419
  469.4 70.6 %mlp_backward.2 = (f32[256,1536]{1,0:T(8,128)}, bf16[256,1536]{1,0:T(8,128)(2,1)}, f32[1,1536]{1,0:T(1,128)}, bf16[4,576,1152]{2,1,0:T(8,128)(2,1)}) custom-call(bf16[256,1536]{1,0:T(8,128)(2,1)} %get-tuple-element.158.g_ref, f32[256,1536]{1,0:T(8,128)} %get-tuple-element.157.upstream_ref, f32[256,1536]{1,0:T(8,128)} %get-tuple-element.98.residual_ref.values_ref, ...), custom_call_target="tpu_custom_call" | custom-call | flops 70000001024 | bytes 31457280 | tf_op jit(solution)/shard_map/mlp_backward/pallas_call | solution.py:531
  540.1 89.3 %rec_backward.2 = (f32[256,1536]{1,0:T(8,128)}, bf16[256,1536]{1,0:T(8,128)(2,1)}, f32[1,1536]{1,0:T(1,128)}, bf16[4,640,512]{2,1,0:T(8,128)(2,1)}, f32[8,256]{1,0:T(8,128)}) custom-call(bf16[256,1536]{1,0:T(8,128)(2,1)} %get-tuple-element.104.g_ref, f32[256,1536]{1,0:T(8,128)} %get-tuple-element.105.upstream_ref, ...), custom_call_target="tpu_custom_call" | custom-call | flops 80000000000 | bytes 31457280 | tf_op jit(solution)/shard_map/rec_backward/pallas_call | solution.py:1061
  629.3 6.5 reduce-scatter.5.cloned.1.call-done
  636.2 71.4 %mlp_backward.3 = (f32[256,1536]{1,0:T(8,128)}, bf16[256,1536]{1,0:T(8,128)(2,1)}, f32[1,1536]{1,0:T(1,128)}, bf16[4,576,1152]{2,1,0:T(8,128)(2,1)}) custom-call(bf16[256,1536]{1,0:T(8,128)(2,1)} %get-tuple-element.115.g_ref, f32[256,1536]{1,0:T(8,128)} %get-tuple-element.116.upstream_ref, f32[256,1536]{1,0:T(8,128)} %get-tuple-element.91.residual_ref.values_ref, ...), custom_call_target="tpu_custom_call" | custom-call | flops 70000001024 | bytes 31457280 | tf_op jit(solution)/shard_map/mlp_backward/pallas_call | solution.py:531
  707.7 1.3 copy-done.4
  711.5 92.4 %rec_backward.3 = (f32[256,1536]{1,0:T(8,128)}, bf16[256,1536]{1,0:T(8,128)(2,1)}, f32[1,1536]{1,0:T(1,128)}, bf16[4,640,512]{2,1,0:T(8,128)(2,1)}, f32[8,256]{1,0:T(8,128)}) custom-call(bf16[256,1536]{1,0:T(8,128)(2,1)} %get-tuple-element.121.g_ref, f32[256,1536]{1,0:T(8,128)} %get-tuple-element.122.upstream_ref, ...), custom_call_target="tpu_custom_call" | custom-call | flops 80000000000 | bytes 31457280 | tf_op jit(solution)/shard_map/rec_backward/pallas_call | solution.py:1061
  807.5 1.3 copy-done.5
  808.9 30.0 %closing.1 = (f32[4,1536]{1,0:T(4,128)S(1)}, f32[16,256]{1,0:T(8,128)S(1)}, bf16[8,48,1152]{2,1,0:T(8,128)(2,1)S(1)}, bf16[8,48,1152]{2,1,0:T(8,128)(2,1)S(1)}, bf16[8,48,512]{2,1,0:T(8,128)(2,1)S(1)}) custom-call(f32[4,1536]{1,0:T(4,128)S(1)} %pad_maximum_fusion.4.gain_ref, f32[16,256]{1,0:T(8,128)S(1)} %pad_maximum_fusion.5.channel_ref, ...), custom_call_target="tpu_custom_call" | custom-call | flops 40000000000 | bytes 10485760 | tf_op jit(solution)/shard_map/closing/pallas_call | solution.py:1384
  846.6 1.4 maximum_convert_fusion.2
  848.0 1.3 maximum_convert_fusion
  849.3 1.3 maximum_convert_fusion.1
  850.7 10.2 %reduce-scatter.11.cloned.1.call-done = bf16[1,640,512]{2,1,0:T(8,128)(2,1)} async-done(((bf16[4,640,512]{2,1,0:T(8,128)(2,1)}), bf16[1,640,512]{2,1,0:T(8,128)(2,1)}) %reduce-scatter.11.cloned.1.call-update) | async-done | bytes 655376 | tf_op jit(solution)/shard_map/reduce_scatter | solution.py:1427
  860.9 1.8 slice.315
  862.7 3.7 all-to-all-start
  869.7 5.0 all-to-all-done
  877.0 1.1 copy.63
  (154 shorter events, 32.1 us)
Async XLA Ops:
  7.2 226.6 %all-gather.7.cloned.1.call-start = ((), (), s32[]{:S(2)}) async-start(), calls=%async_computation.9 | async-start | bytes 6635520 | tf_op jit(solution)/shard_map/all_gather | solution.py:1524
  8.3 4.2 copy-start.25
  8.3 4.2 copy-start.26
  8.3 4.2 copy-start.24
  8.3 4.2 copy-start
  9.3 7.8 collective-permute-start
  13.9 2.8 copy-start.19
  13.9 2.8 copy-start.23
  109.3 2.6 copy-start.1
  114.1 192.1 %all-gather.9.cloned.1.call-start = ((), (), s32[]{:S(2)}) async-start(), calls=%async_computation.10 | async-start | bytes 3276800 | tf_op jit(solution)/shard_map/all_gather | solution.py:1531
  114.9 63.0 %copy-start.15 = (f32[2,8,2048]{2,1,0:T(8,128)}, f32[2,8,2048]{2,1,0:T(8,128)S(1)}, u32[]{:S(2)}) copy-start(f32[2,8,2048]{2,1,0:T(8,128)S(1)} %reshape.500) | copy-start | bytes 393220
  179.1 120.8 %collective-permute-start.1 = (bf16[192,1152]{1,0:T(8,128)(2,1)S(1)}, bf16[192,1152]{1,0:T(8,128)(2,1)S(1)}, u32[]{:S(2)}, u32[]{:S(2)}) collective-permute-start(bf16[192,1152]{1,0:T(8,128)(2,1)S(1)} %maximum_maximum_fusion.1), channel_id=1, source_target_pairs={{0,0},{1,8},{2,16},{3,24},{4,1},{5,9},{6,17},{7,25},{8,2},{9,10},{... | collective-permute-start | bytes 1327112 | tf_op jit(solution)/shard_map/ppermute | solution.py:52
  183.3 219.7 %all-gather.11.cloned.1.call-start = ((), (), s32[]{:S(2)}) async-start(), calls=%async_computation.11 | async-start | bytes 6635520 | tf_op jit(solution)/shard_map/all_gather | solution.py:1524
  303.9 331.9 %reduce-scatter.5.cloned.1.call-start = ((), (), s32[]{:S(2)}) async-start(), calls=%async_computation.5 | async-start | bytes 6635520 | tf_op jit(solution)/shard_map/reduce_scatter | solution.py:1427
  540.0 171.4 %reduce-scatter.7.cloned.1.call-start = ((), (), s32[]{:S(2)}) async-start(), calls=%async_computation.6 | async-start | bytes 3276800 | tf_op jit(solution)/shard_map/reduce_scatter | solution.py:1427
  635.9 171.6 %reduce-scatter.9.cloned.1.call-start = ((), (), s32[]{:S(2)}) async-start(), calls=%async_computation.7 | async-start | bytes 6635520 | tf_op jit(solution)/shard_map/reduce_scatter | solution.py:1427
  707.6 2.3 copy-start.6
  707.6 153.3 %reduce-scatter.11.cloned.1.call-start = ((), (), s32[]{:S(2)}) async-start(), calls=%async_computation.8 | async-start | bytes 3276800 | tf_op jit(solution)/shard_map/reduce_scatter | solution.py:1427
  711.5 92.4 %copy-start.10 = (bf16[1,640,512]{2,1,0:T(8,128)(2,1)S(1)}, bf16[1,640,512]{2,1,0:T(8,128)(2,1)}, u32[]{:S(2)}) copy-start(bf16[1,640,512]{2,1,0:T(8,128)(2,1)} %reduce-scatter.7.cloned.1.call-done) | copy-start | bytes 1966084
  711.5 92.5 %copy-start.18 = (f32[8,256]{1,0:T(8,128)S(1)}, f32[8,256]{1,0:T(8,128)}, u32[]{:S(2)}) copy-start(f32[8,256]{1,0:T(8,128)} %get-tuple-element.133) | copy-start | bytes 24580
  711.5 94.0 %copy-start.20 = (f32[1,1536]{1,0:T(1,128)S(1)}, f32[1,1536]{1,0:T(1,128)}, u32[]{:S(2)}) copy-start(f32[1,1536]{1,0:T(1,128)} %get-tuple-element.131) | copy-start | bytes 18436
  711.5 94.0 %copy-start.21 = (f32[1,1536]{1,0:T(1,128)S(1)}, f32[1,1536]{1,0:T(1,128)}, u32[]{:S(2)}) copy-start(f32[1,1536]{1,0:T(1,128)} %get-tuple-element.130) | copy-start | bytes 18436
  711.5 94.0 %copy-start.22 = (f32[1,1536]{1,0:T(1,128)S(1)}, f32[1,1536]{1,0:T(1,128)}, u32[]{:S(2)}) copy-start(f32[1,1536]{1,0:T(1,128)} %get-tuple-element.129) | copy-start | bytes 18436
  842.7 3.9 copy-start.7
  842.7 3.9 copy-start.11
  850.6 16.7 %copy-start.17 = (bf16[1,64,256]{2,1,0:T(8,128)(2,1)S(1)}, bf16[1,64,256]{2,1,0:T(8,128)(2,1)}, u32[]{:S(2)}) copy-start(bf16[1,64,256]{2,1,0:T(8,128)(2,1)} %get-tuple-element.166) | copy-start | bytes 98308
  850.6 17.4 %copy-start.16 = (bf16[1,64,256]{2,1,0:T(8,128)(2,1)S(1)}, bf16[1,64,256]{2,1,0:T(8,128)(2,1)}, u32[]{:S(2)}) copy-start(bf16[1,64,256]{2,1,0:T(8,128)(2,1)} %get-tuple-element.167) | copy-start | bytes 98308
  850.6 18.0 %copy-start.12 = (bf16[1,64,512]{2,1,0:T(8,128)(2,1)S(1)}, bf16[1,64,512]{2,1,0:T(8,128)(2,1)}, u32[]{:S(2)}) copy-start(bf16[1,64,512]{2,1,0:T(8,128)(2,1)} %get-tuple-element.163) | copy-start | bytes 196612
  850.6 18.0 %copy-start.13 = (bf16[1,64,512]{2,1,0:T(8,128)(2,1)S(1)}, bf16[1,64,512]{2,1,0:T(8,128)(2,1)}, u32[]{:S(2)}) copy-start(bf16[1,64,512]{2,1,0:T(8,128)(2,1)} %get-tuple-element.164) | copy-start | bytes 196612
  850.7 18.0 %copy-start.14 = (bf16[1,64,512]{2,1,0:T(8,128)(2,1)S(1)}, bf16[1,64,512]{2,1,0:T(8,128)(2,1)}, u32[]{:S(2)}) copy-start(bf16[1,64,512]{2,1,0:T(8,128)(2,1)} %get-tuple-element.165) | copy-start | bytes 196612
  862.7 12.1 %all-to-all-start = ((bf16[8,48,512]{2,1,0:T(8,128)(2,1)}), bf16[8,48,512]{2,1,0:T(8,128)(2,1)S(1)}, u32[]{:S(2)}, u32[]{:S(2)}) async-start(bf16[8,48,512]{2,1,0:T(8,128)(2,1)} %bitcast.54), calls=%async_computation.4 | async-start | bytes 786432 | tf_op jit(solution)/shard_map/all_to_all | solution.py:1563
  868.7 6.4 copy-start.8
  (5 other events, 7.9 us)
Sparse Core Ops, SparseCore 0:
  114.2 119.5 all-gather.6
  235.9 53.6 all-gather.8
  304.0 98.8 all-gather.10
  540.1 95.6 reduce-scatter.4
  638.1 52.5 reduce-scatter.6
  707.7 96.7 reduce-scatter.8
  807.7 53.1 reduce-scatter.10

commit v5 on v4

--- a/solution.py
+++ b/solution.py
@@ -94,12 +94,12 @@
     def device(self, m, s):
         return (self.base + self.slot(m, s), self.z)
 
-    def enter(self, extra=(), more=0):
+    def enter(self, extra=()):
         barrier = pltpu.get_barrier_semaphore()
         devices = [self.device(1, 0), self.device(2, 0), self.device(0, 1)] + list(extra)
         for device in devices:
             pl.semaphore_signal(barrier, inc=1, device_id=device, device_id_type=MESH)
-        pl.semaphore_wait(barrier, len(devices) + more)
+        pl.semaphore_wait(barrier, len(devices))
 
 
 def remote(src, dst, send, recv, device):
@@ -512,10 +512,11 @@
         beside = min(2 * units - first, width // 2)
         for z in range(seq):
             own = product[z * part_units : (z + 1) * part_units]
-            gcol_ref[z, base : base + part_units, first : first + beside] = own[:, :beside]
+            to = lax.rem(net.t + z, seq)
+            gcol_ref[to, base : base + part_units, first : first + beside] = own[:, :beside]
             if beside < width // 2:
                 for n in range(blocks):
-                    gcol_ref[z, base + part_units :, n * rest : (n + 1) * rest] = own[
+                    gcol_ref[to, base + part_units :, n * rest : (n + 1) * rest] = own[
                         n * low : (n + 1) * low, beside:
                     ]
     scatter.finish()
@@ -1103,8 +1104,8 @@
 
 
 def open_kernel(
-    x_ref, small_ref, gain_ref, slot_ref, pack_ref, col_ref, rows_ref, later_ref,
-    small_out, gain_out, slot_out, full_out, pack_out, mlp_out, later_out,
+    x_ref, small_ref, gain_ref, slot_ref, pack_ref,
+    small_out, gain_out, slot_out, full_out, pack_out,
     full, smalls, gains, slots, gs, gr, ps, pr, sem,
 ):
     net = Net()
@@ -1117,27 +1118,10 @@
         pltpu.make_async_copy(gain_ref, gains.at[net.z], sem.at[1]),
         pltpu.make_async_copy(slot_ref, slots.at[net.t], sem.at[2]),
     ]
-    col_rows = col_ref.shape[0]
-    below = mlp_out.at[pl.ds(col_rows, rows_ref.shape[0])]
-    here = [
-        pltpu.make_async_copy(pack_ref, pack_out.at[net.z], sem.at[4]),
-        pltpu.make_async_copy(col_ref, mlp_out.at[pl.ds(0, col_rows)], sem.at[5]),
-    ]
-    for copy in mine + here:
+    own_pack = pltpu.make_async_copy(pack_ref, pack_out.at[net.z], sem.at[4])
+    for copy in mine + [own_pack]:
         copy.start()
-    held, owned = TP * net.z + net.t, seq * net.t + net.z
-    owner, giver = (held // seq, lax.rem(held, seq)), (lax.rem(owned, TP), owned // TP)
-    away = held != owned
-    barrier = pltpu.get_barrier_semaphore()
-
-    @pl.when(away)
-    def _():
-        for t, z in (owner, giver):
-            pl.semaphore_signal(barrier, inc=1, device_id=(net.base + t, z), device_id_type=MESH)
-    net.enter(
-        line.others + [net.device(1, 1), net.device(2, 1), net.device(3, 0), net.device(3, 1)],
-        jnp.where(away, 2, 0),
-    )
+    net.enter(line.others + [net.device(1, 1), net.device(2, 1), net.device(3, 0), net.device(3, 1)])
     for copy in mine:
         copy.wait()
 
@@ -1199,27 +1183,6 @@
 
     forward(1, 0)
     forward(-1, 0)
-    n = first + 2 * (seq - 1)
-    owner_id = (net.base + owner[0], owner[1])
-    moved = [
-        remote(rows_ref, below, ps.at[n], pr.at[n], owner_id),
-        remote(later_ref, later_out, ps.at[n + 1], pr.at[n + 1], owner_id),
-    ]
-    kept = [
-        pltpu.make_async_copy(rows_ref, below, sem.at[6]),
-        pltpu.make_async_copy(later_ref, later_out, sem.at[7]),
-    ]
-
-    @pl.when(away)
-    def _():
-        for copy in moved:
-            copy.start()
-
-    @pl.when(held == owned)
-    def _():
-        for copy in kept:
-            copy.start()
-
     for copy in arrivals[: seq - 1]:
         copy.wait_recv()
     rows, width = x_ref.shape
@@ -1260,48 +1223,35 @@
     last(1)
     last(-1)
 
-    @pl.when(away)
-    def _():
-        for copy in moved:
-            copy.wait()
-
-    @pl.when(held == owned)
-    def _():
-        for copy in kept:
-            copy.wait()
-
     for copy in sends:
         copy.wait_send()
-    for copy in here:
-        copy.wait()
+    own_pack.wait()
     for save in saves:
         save.wait()
 
 
-def opening(seq, x, small, gain, slot, pack, col, below, later):
+def opening(seq, x, small, gain, slot, pack):
     rows, width = x.shape
     shape = jax.ShapeDtypeStruct
     dma = pltpu.SemaphoreType.DMA
-    pushes = 4 * (seq - 1) + TP - 1 + 2
+    pushes = 4 * (seq - 1) + TP - 1
     return pl.pallas_call(
         open_kernel,
-        in_specs=[VM] + [ANY] * 7,
-        out_specs=[ANY] * 7,
+        in_specs=[VM] + [ANY] * 4,
+        out_specs=[ANY] * 5,
         out_shape=[
             shape((seq,) + small.shape, F32),
             shape((seq,) + gain.shape, F32),
             shape((TP,) + slot.shape, jnp.int32),
             shape((TP, rows, width), BF),
             shape((seq,) + pack.shape, BF),
-            shape((col.shape[0] + below.shape[0], col.shape[1]), BF),
-            shape(later.shape, BF),
         ],
         scratch_shapes=[
             pltpu.VMEM((TP, rows, width), BF),
             pltpu.VMEM((seq,) + small.shape, F32),
             pltpu.VMEM((seq,) + gain.shape, F32),
             pltpu.VMEM((TP,) + slot.shape, jnp.int32),
-            dma((10,)), dma((10,)), dma((pushes,)), dma((pushes,)), dma((8,)),
+            dma((10,)), dma((10,)), dma((pushes,)), dma((pushes,)), dma((5,)),
         ],
         compiler_params=pltpu.CompilerParams(
             collective_id=6, has_side_effects=True, vmem_limit_bytes=40 << 20
@@ -1310,17 +1260,16 @@
             flops=40 * 10**9, bytes_accessed=10 << 20, transcendentals=0
         ),
         name="opening",
-    )(x, small, gain, slot, pack, col, below, later)
-
-
-def close_kernel(
-    gain_ref, channel_ref, *refs
-):
-    count = (len(refs) - 8) // 2
-    blocks, (gain_out, channel_out), moved = refs[:count], refs[count : count + 2], refs[
-        count + 2 : 2 * count + 2
-    ]
-    plane_gain, line_gain, line_channel, ps, pr, sem = refs[2 * count + 2 :]
+    )(x, small, gain, slot, pack)
+
+
+def close_kernel(layers, gain_ref, channel_ref, *refs):
+    rows_in, refs = refs[:layers], refs[layers:]
+    count = (len(refs) - 8 - layers) // 2
+    blocks, (gain_out, channel_out) = refs[:count], refs[count : count + 2]
+    moved, refs = refs[count + 2 : 2 * count + 2], refs[2 * count + 2 :]
+    rows_out = refs[:layers]
+    plane_gain, line_gain, line_channel, ps, pr, sem = refs[layers:]
     net = Net()
     seq = line_gain.shape[0]
     line = Line(net, seq)
@@ -1355,6 +1304,29 @@
     for block, out in zip(blocks, moved):
         for slot, to in zip(slots, plane):
             rest.append(push(block.at[slot], out.at[net.t], out.at[slot], to))
+    each = TP // seq
+    owner = lax.rem(net.z + TP - net.t, seq) * each + net.t // seq
+    giver = lax.rem(net.t, each) * seq + lax.rem(net.z + TP - net.t // each, seq)
+    first = ps.shape[0] - layers
+    rows = [
+        remote(src, dst, ps.at[first + l], pr.at[first + l], (net.base + owner, net.z))
+        for l, (src, dst) in enumerate(zip(rows_in, rows_out))
+    ]
+    rows_here = [
+        pltpu.make_async_copy(src, dst, sem.at[count + l])
+        for l, (src, dst) in enumerate(zip(rows_in, rows_out))
+    ]
+
+    @pl.when(owner != net.t)
+    def _():
+        for copy in rows:
+            copy.start()
+
+    @pl.when(owner == net.t)
+    def _():
+        for copy in rows_here:
+            copy.start()
+
     for copy in gains:
         copy.wait_recv()
     total = plane_gain[0]
@@ -1376,22 +1348,37 @@
     for copy in own:
         copy.wait()
 
-
-def closing(seq, gains, channels, blocks):
+    @pl.when(owner != net.t)
+    def _():
+        for copy in rows:
+            copy.wait_send()
+
+    @pl.when(owner == net.t)
+    def _():
+        for copy in rows_here:
+            copy.wait()
+
+    @pl.when(giver != net.t)
+    def _():
+        for copy in rows:
+            copy.wait_recv()
+
+
+def closing(seq, gains, channels, rows, blocks):
     shape = jax.ShapeDtypeStruct
     dma = pltpu.SemaphoreType.DMA
-    pushes = (TP - 1) * (1 + len(blocks)) + 2 * (seq - 1)
+    pushes = (TP - 1) * (1 + len(blocks)) + 2 * (seq - 1) + len(rows)
     return pl.pallas_call(
-        close_kernel,
-        in_specs=[VM, VM] + [ANY] * len(blocks),
-        out_specs=[VM, VM] + [ANY] * len(blocks),
+        partial(close_kernel, len(rows)),
+        in_specs=[VM, VM] + [ANY] * (len(rows) + len(blocks)),
+        out_specs=[VM, VM] + [ANY] * (len(rows) + len(blocks)),
         out_shape=[shape(gains.shape, F32), shape(channels.shape, F32)]
-        + [shape(block.shape, block.dtype) for block in blocks],
+        + [shape(block.shape, block.dtype) for block in blocks + rows],
         scratch_shapes=[
             pltpu.VMEM((TP,) + gains.shape, F32),
             pltpu.VMEM((seq,) + gains.shape, F32),
             pltpu.VMEM((seq,) + channels.shape, F32),
-            dma((pushes,)), dma((pushes,)), dma((len(blocks),)),
+            dma((pushes,)), dma((pushes,)), dma((len(blocks) + len(rows),)),
         ],
         compiler_params=pltpu.CompilerParams(
             collective_id=7, has_side_effects=True, vmem_limit_bytes=40 << 20
@@ -1400,7 +1387,7 @@
             flops=40 * 10**9, bytes_accessed=10 << 20, transcendentals=0
         ),
         name="closing",
-    )(gains, channels, *blocks)
+    )(gains, channels, *rows, *blocks)
 
 
 def layer_backward(upstream, upstream_low, w, saved, slots, pending):
@@ -1431,22 +1418,33 @@
     return jnp.moveaxis(parts, 0, 1).reshape(parts.shape[1], -1)
 
 
-def owned_grads(plan, mlp_share, rec_share, mlp, rec, width, head, units):
+def unit_columns(parts, seq):
+    tp, n, units = parts.shape
+    part = units // seq
+    places = {}
+    for t in range(tp):
+        for p in range(seq):
+            places[p * tp + t // seq * seq + (t + p) % seq] = (t, p)
+    chunks = [places[q] for q in range(tp * seq)]
+    return jnp.concatenate([parts[t, :, p * part : (p + 1) * part] for t, p in chunks], 1)
+
+
+def owned_grads(plan, down_rows, rec_share, mlp, rec, width, head, units):
     base = width // plan.seq
     h, u = head // plan.seq, units // plan.seq
     out = [rec_share[base + i * h : base + (i + 1) * h] for i in range(3)]
     gates = rec_share[base + 3 * h :]
     rest, blocks = mlp_split(width, 2 * units)
-    down = [mlp_share[base + u :, i * rest : (i + 1) * rest] for i in range(blocks)]
+    down = [down_rows[u:, i * rest : (i + 1) * rest] for i in range(blocks)]
     grads = [
         columns(rec[:, :, :head]),
         columns(rec[:, :, head:]),
         gates[:, :head],
         gates[:, head:],
         jnp.concatenate(out, 1),
-        columns(mlp[:, :, :units]),
-        columns(mlp[:, :, units:]),
-        jnp.concatenate([mlp_share[base : base + u], jnp.concatenate(down, 0)], 1),
+        unit_columns(mlp[:, :, :units], plan.seq),
+        unit_columns(mlp[:, :, units:], plan.seq),
+        jnp.concatenate([down_rows[:u], jnp.concatenate(down, 0)], 1),
     ]
     return [to_owners(plan, g.astype(F32), 0) for g in grads]
 
@@ -1492,18 +1490,29 @@
         rec = jnp.concatenate([col(branch_proj, l, head, t), col(stream_proj, l, head, t)], 1)
         return jnp.concatenate([rec, rows_of], 0)
 
+    def unit_chunk(t, plane):
+        return t // seq * seq + (t + plane) % seq
+
     def mlp_rows(l, t):
-        return below(chunk(mlp_down, l, t), 2 * units)
-
-    def mlp_cols(l, t):
-        return jnp.concatenate([col(mlp_gate, l, units, t), col(mlp_up, l, units, t)], 1)
+        return below(chunk(mlp_down, l, unit_chunk(t, z)), 2 * units)
+
+    def mlp_pack(l, t):
+        rows_of, part = mlp_gate.shape[1], units // seq
+        cols = [
+            lax.dynamic_slice(
+                weight, (l, 0, (p * tp + unit_chunk(t, p)) * part), (1, rows_of, part)
+            )[0]
+            for weight in (mlp_gate, mlp_up)
+            for p in range(seq)
+        ]
+        return jnp.concatenate([jnp.concatenate(cols, 1), mlp_rows(l, t)], 0)
 
     pack = rec_pack(0, owner_chunks(plan, rec_rows(0, t)), t)
-    smalls, gains, layout, normed, rec, mlp, rec_owned = opening(
-        seq, block_input, small, norm_gains.reshape(2 * LAYERS, -1).astype(F32), slot, pack,
-        mlp_cols(0, t), mlp_rows(0, t), rec_rows(1, t),
+    mlp = mlp_pack(0, t)
+    smalls, gains, layout, normed, rec = opening(
+        seq, block_input, small, norm_gains.reshape(2 * LAYERS, -1).astype(F32), slot, pack
     )
-    mlp, rec = lax.optimization_barrier((mlp, rec))
+    t, mlp, rec = lax.optimization_barrier((t, mlp, rec))
     layout = layout[:, 0, :2]
     gains = jnp.moveaxis(gains, 0, 1).reshape(LAYERS, 2, -1)
     smalls = jnp.moveaxis(smalls, 0, 1).reshape(LAYERS, 8, -1)
@@ -1514,8 +1523,7 @@
     saved_all, weights = [], []
     for l in range(LAYERS):
         if l > 0:
-            mlp_owned, t, normed = lax.optimization_barrier((mlp_owned, t, normed))
-            mlp = jnp.concatenate([mlp_cols(l, t), mlp_owned], 0)
+            mlp, normed = lax.optimization_barrier((mlp, normed))
         w = dict(
             gain=gains[l],
             small=jnp.concatenate([smalls[l, :7], -8.0 * jax.nn.softplus(-smalls[l, 7:])], 0),
@@ -1527,9 +1535,10 @@
         kept = rec_forward(normed, residual, w["gain"][1], w["rec"], w["small"], layout)
         middle, normed_two, *kept = kept
         if l + 1 < LAYERS:
-            rows_of, t, normed_two = lax.optimization_barrier((rec_owned, t, normed_two))
-            rec = lax.all_gather(rec_pack(l + 1, rows_of, t), "seq")
-            mlp_owned = owner_chunks(plan, mlp_rows(l + 1, t))
+            t, normed_two = lax.optimization_barrier((t, normed_two))
+            pack = rec_pack(l + 1, owner_chunks(plan, rec_rows(l + 1, t)), t)
+            mlp, pack, normed_two = lax.optimization_barrier((mlp_pack(l + 1, t), pack, normed_two))
+            rec = lax.all_gather(pack, "seq")
         output, normed, *kept_two = mlp_forward(
             normed_two, middle, gains[(l + 1) % LAYERS, 0], w["mlp"]
         )
@@ -1558,14 +1567,17 @@
     blocks = [by_slot(shares[l][0]) for l in range(LAYERS)]
     blocks += [by_slot(shares[l][1]) for l in range(1, LAYERS)]
     gains, channel, *blocks = closing(
-        seq, jnp.concatenate(gain_all, 0), jnp.concatenate(channel_all, 0), blocks
+        seq, jnp.concatenate(gain_all, 0), jnp.concatenate(channel_all, 0),
+        [shares[l][0][base:] for l in range(LAYERS)], blocks,
     )
+    blocks, downs = blocks[:-LAYERS], blocks[-LAYERS:]
     last = lax.all_to_all(
         by_slot(shares[0][1]), "rep", split_axis=0, concat_axis=0, axis_index_groups=plan.tp_groups
     )
     mlps, recs = blocks[:LAYERS], [last] + blocks[LAYERS:]
     outs = [
-        owned_grads(plan, *shares[l], mlps[l], recs[l], width, head, units) for l in range(LAYERS)
+        owned_grads(plan, downs[l], shares[l][1], mlps[l], recs[l], width, head, units)
+        for l in range(LAYERS)
     ]
     big = [jnp.stack([outs[l][i] for l in range(LAYERS)]) for i in range(8)]
 

time: 894 us -> 885 us (0.990)
  Pallas kernels: 721 us -> 687 us
  local copies, waits for them, and re-layouts: 34.2 us -> 67.1 us
  waiting for transfers between devices: 89.2 us -> 59.9 us
  starting transfers between devices: 5.61 us -> 18.1 us
    pallas_call x2, Pallas kernels: 122 us -> 88.4 us  [the longest x1 58.2 us: opening(): pl.pallas_call(open_kernel, in_specs=[VM] + [ANY] * 4, out_specs=[ANY] *...]
    all_gather x2, waiting for transfers between devices: 67.2 us -> 48.2 us  [local(): lax.all_gather(mlp, 'seq')]
    reduce_scatter x4, waiting for transfers between devices: 16.7 us -> 6.53 us  [over_seq(): return lax.psum_scatter(value, 'seq', scatter_dimension=0, tiled=False)]
  transfers between devices with their start and end apart: 10 -> 10, of which waited for: 5 -> 4; matrix products, arithmetic and copies ran while one was open for 4% -> 7% of each run, Pallas kernels for 55% -> 56%
where the time goes in v5:
time: 885 us; the launch traced here: 875 us
  Pallas kernels  687 us (78%)
  local copies, waits for them, and re-layouts  67.1 us (8%)
  waiting for transfers between devices  59.9 us (7%)
  other arithmetic  26.5 us (3%)
  starting transfers between devices  18.1 us (2%)
  between operations  16.4 us (2%)
    pallas_call x2, Pallas kernels, rec_backward(): pl.pallas_call(rec_backward_kernel, in_specs=[ANY, VM, VM, VM, ANY, VM, p...  181 us
    pallas_call x2, Pallas kernels, rec_forward(): pl.pallas_call(partial(rec_forward_kernel, gathered), in_specs=[ANY, VM,...  143 us
    pallas_call x2, Pallas kernels, mlp_backward(): pl.pallas_call(mlp_backward_kernel, in_specs=[ANY, VM, VM, VM, ANY, ANY,...  142 us
    pallas_call x2, Pallas kernels, mlp_forward(): pl.pallas_call(mlp_forward_kernel, in_specs=[ANY, VM, VM, ANY], out_specs...  133 us
    pallas_call x1, Pallas kernels, opening(): pl.pallas_call(open_kernel, in_specs=[VM] + [ANY] * 4, out_specs=[ANY] *...  58.2 us
    all_gather x2, waiting for transfers between devices, local(): lax.all_gather(mlp, 'seq')  48.2 us
    pallas_call x1, Pallas kernels, closing(): pl.pallas_call(partial(close_kernel, len(rows)), in_specs=[VM, VM] + [ANY...  30.3 us
  transfers between devices with their start and end apart: 10, of which 4 were waited for; matrix products, arithmetic and copies ran while one was open for 7% of the time, Pallas kernels for 56%

profile of v5, /device:TPU:0, one launch (start us, length us, event | category | flops | bytes accessed | tf_op | source)
XLA Modules:
  0.0 875.1 jit_solution(11943010815658774254)
XLA Ops:
  7.3 1.8 copy-done
  10.6 3.6 collective-permute-start
  17.5 2.5 convert_element_type.157.residual_ref.values_ref
  20.0 1.7 dynamic-slice_bitcast_fusion.14
  21.7 3.5 dynamic-slice_bitcast_fusion.16
  25.2 3.5 concatenate.157
  28.7 2.4 maximum_maximum_fusion
  33.3 58.2 %opening.1 = (f32[4,16,512]{2,1,0:T(8,128)S(1)}, f32[4,4,384]{2,1,0:T(4,128)S(1)}, s32[8,8,128]{2,1,0:T(8,128)S(1)}, bf16[8,256,1536]{2,1,0:T(8,128)(2,1)S(1)}, bf16[4,640,512]{2,1,0:T(8,128)(2,1)S(1)}) custom-call(bf16[256,1536]{1,0:T(8,128)(2,1)S(1)} %copy-done.2, f32[16,512]{1,0:T(8,128)S(1)} %fusion.small_ref, f32[4,384]{1,0:T(4,128)S(1)} %reshape.1883.gain_ref, ...), custom_call_target="tpu_custom_call" | custom-call | flops 40000000000 | bytes 10485760 | tf_op jit(solution)/shard_map/opening/pallas_call | solution.py:1238
  91.5 2.6 copy-done.12
  97.9 62.7 %rec_forward_first.1 = (f32[256,1536]{1,0:T(8,128)}, bf16[256,1536]{1,0:T(8,128)(2,1)}, bf16[8,128]{1,0:T(8,128)(2,1)}, f32[8,256,256]{2,1,0:T(8,128)}, f32[8,26...) custom-call(bf16[8,256,1536]{2,1,0:T(8,128)(2,1)} %copy-done.12, ...), custom_call_target="tpu_custom_call" | custom-call | flops 70000001024 | bytes 31457280 | tf_op jit(solution)/shard_map/rec_forward_first/pallas_call | solution.py:805
  163.1 1.6 collective-permute-start.1
  174.5 31.4 %all-gather.7.cloned.1.call-done = bf16[2304,1152]{1,0:T(8,128)(2,1)} async-done(((bf16[576,1152]{1,0:T(8,128)(2,1)}), bf16[2304,1152]{1,0:T(8,128)(2,1)}) %all-gather.7.cloned.1.call-update) | async-done | bytes 5308432 | tf_op jit(solution)/shard_map/all_gather | solution.py:1532
  206.0 66.1 %mlp_forward.2 = (f32[256,1536]{1,0:T(8,128)}, bf16[256,1536]{1,0:T(8,128)(2,1)}, bf16[8,256,1536]{2,1,0:T(8,128)(2,1)}, bf16[8,256,1152]{2,1,0:T(8,128)(2,1)}) custom-call(bf16[256,1536]{1,0:T(8,128)(2,1)} %get-tuple-element.93.x_ref, f32[256,1536]{1,0:T(8,128)} %get-tuple-element.94.residual_ref.values_ref, f32[1,1536]{1,0:T(1,128)} %get-tuple-element.339.gain_ref, ...), custom_call_target="tpu_custom_call" | custom-call | flops 60000002048 | bytes 31457280 | tf_op jit(solution)/shard_map/mlp_forward/pallas_call | solution.py:419
  272.2 1.6 convert_multiply_fusion
  274.4 79.9 %rec_forward.1 = (f32[256,1536]{1,0:T(8,128)}, bf16[256,1536]{1,0:T(8,128)(2,1)}, bf16[8,256,1536]{2,1,0:T(8,128)(2,1)}, f32[8,256,256]{2,1,0:T(8,128)}, f32[8,2...) custom-call(bf16[256,1536]{1,0:T(8,128)(2,1)} %get-tuple-element.97.x_ref, ...), custom_call_target="tpu_custom_call" | custom-call | flops 70000001024 | bytes 31457280 | tf_op jit(solution)/shard_map/rec_forward/pallas_call | solution.py:805
  354.3 16.7 %all-gather.11.cloned.1.call-done = bf16[2304,1152]{1,0:T(8,128)(2,1)} async-done(((bf16[576,1152]{1,0:T(8,128)(2,1)}), bf16[2304,1152]{1,0:T(8,128)(2,1)}) %all-gather.11.cloned.1.call-update) | async-done | bytes 5308432 | tf_op jit(solution)/shard_map/all_gather | solution.py:1532
  371.1 66.6 %mlp_forward.3 = (f32[256,1536]{1,0:T(8,128)}, bf16[256,1536]{1,0:T(8,128)(2,1)}, bf16[8,256,1536]{2,1,0:T(8,128)(2,1)}, bf16[8,256,1152]{2,1,0:T(8,128)(2,1)}) custom-call(bf16[256,1536]{1,0:T(8,128)(2,1)} %get-tuple-element.100.x_ref, f32[256,1536]{1,0:T(8,128)} %get-tuple-element.101.residual_ref.values_ref, f32[1,1536]{1,0:T(1,128)} %get-tuple-element.338.gain_ref, ...), custom_call_target="tpu_custom_call" | custom-call | flops 60000002048 | bytes 31457280 | tf_op jit(solution)/shard_map/mlp_forward/pallas_call | solution.py:419
  437.6 70.6 %mlp_backward.2 = (f32[256,1536]{1,0:T(8,128)}, bf16[256,1536]{1,0:T(8,128)(2,1)}, f32[1,1536]{1,0:T(1,128)}, bf16[4,576,1152]{2,1,0:T(8,128)(2,1)}) custom-call(bf16[256,1536]{1,0:T(8,128)(2,1)} %get-tuple-element.294.g_ref, f32[256,1536]{1,0:T(8,128)} %get-tuple-element.293.upstream_ref, f32[256,1536]{1,0:T(8,128)} %get-tuple-element.101.residual_ref.values_ref, ...), custom_call_target="tpu_custom_call" | custom-call | flops 70000001024 | bytes 31457280 | tf_op jit(solution)/shard_map/mlp_backward/pallas_call | solution.py:532
  508.3 89.3 %rec_backward.2 = (f32[256,1536]{1,0:T(8,128)}, bf16[256,1536]{1,0:T(8,128)(2,1)}, f32[1,1536]{1,0:T(1,128)}, bf16[4,640,512]{2,1,0:T(8,128)(2,1)}, f32[8,256]{1,0:T(8,128)}) custom-call(bf16[256,1536]{1,0:T(8,128)(2,1)} %get-tuple-element.106.g_ref, f32[256,1536]{1,0:T(8,128)} %get-tuple-element.107.upstream_ref, ...), custom_call_target="tpu_custom_call" | custom-call | flops 80000000000 | bytes 31457280 | tf_op jit(solution)/shard_map/rec_backward/pallas_call | solution.py:1062
  597.6 6.5 reduce-scatter.5.cloned.1.call-done
  604.2 71.4 %mlp_backward.3 = (f32[256,1536]{1,0:T(8,128)}, bf16[256,1536]{1,0:T(8,128)(2,1)}, f32[1,1536]{1,0:T(1,128)}, bf16[4,576,1152]{2,1,0:T(8,128)(2,1)}) custom-call(bf16[256,1536]{1,0:T(8,128)(2,1)} %get-tuple-element.117.g_ref, f32[256,1536]{1,0:T(8,128)} %get-tuple-element.118.upstream_ref, f32[256,1536]{1,0:T(8,128)} %get-tuple-element.94.residual_ref.values_ref, ...), custom_call_target="tpu_custom_call" | custom-call | flops 70000001024 | bytes 31457280 | tf_op jit(solution)/shard_map/mlp_backward/pallas_call | solution.py:532
  677.9 1.8 slice.770.refs_1_
  681.0 92.1 %rec_backward.3 = (f32[256,1536]{1,0:T(8,128)}, bf16[256,1536]{1,0:T(8,128)(2,1)}, f32[1,1536]{1,0:T(1,128)}, bf16[4,640,512]{2,1,0:T(8,128)(2,1)}, f32[8,256]{1,0:T(8,128)}) custom-call(bf16[256,1536]{1,0:T(8,128)(2,1)} %get-tuple-element.123.g_ref, f32[256,1536]{1,0:T(8,128)} %get-tuple-element.124.upstream_ref, ...), custom_call_target="tpu_custom_call" | custom-call | flops 80000000000 | bytes 31457280 | tf_op jit(solution)/shard_map/rec_backward/pallas_call | solution.py:1062
  778.1 1.8 slice.769.refs_0_
  785.0 30.3 %closing.1 = (f32[4,1536]{1,0:T(4,128)S(1)}, f32[16,256]{1,0:T(8,128)S(1)}, bf16[8,48,1152]{2,1,0:T(8,128)(2,1)S(1)}, bf16[8,48,1152]{2,1,0:T(8,128)(2,1)S(1)}, ...) custom-call(f32[4,1536]{1,0:T(4,128)S(1)} %copy-done.10, ...), custom_call_target="tpu_custom_call" | custom-call | flops 40000000000 | bytes 10485760 | tf_op jit(solution)/shard_map/closing/pallas_call | solution.py:1371
  826.8 1.6 concatenate.182
  837.1 1.8 slice.951
  838.9 12.6 %all-to-all-start = ((bf16[8,48,512]{2,1,0:T(8,128)(2,1)}), bf16[8,48,512]{2,1,0:T(8,128)(2,1)S(1)}, u32[]{:S(2)}, u32[]{:S(2)}) async-start(bf16[8,48,512]{2,1,0:T(8,128)(2,1)} %bitcast.66), calls=%async_computation.4 | async-start | bytes 786432 | tf_op jit(solution)/shard_map/all_to_all | solution.py:1574
  854.8 5.1 all-to-all-done
  861.6 2.0 maximum_convert_fusion.3
  863.6 1.9 maximum_convert_fusion.4
  865.4 2.7 copy.59
  (172 shorter events, 60.9 us)
Async XLA Ops:
  7.2 1.9 copy-start
  7.2 10.2 %copy-start.30 = (bf16[2,512]{1,0:T(2,128)(2,1)S(1)}, bf16[2,512]{1,0:T(2,128)(2,1)}, u32[]{:S(2)}) copy-start(bf16[2,512]{1,0:T(2,128)(2,1)} %param.25) | copy-start | bytes 6148
  7.2 10.2 %copy-start.31 = (bf16[2,512]{1,0:T(2,128)(2,1)S(1)}, bf16[2,512]{1,0:T(2,128)(2,1)}, u32[]{:S(2)}) copy-start(bf16[2,512]{1,0:T(2,128)(2,1)} %param.29) | copy-start | bytes 6148
  7.2 10.3 %copy-start.29 = (bf16[2,2,384]{2,1,0:T(2,128)(2,1)S(1)}, bf16[2,2,384]{2,1,0:T(2,128)(2,1)}, u32[]{:S(2)}) copy-start(bf16[2,2,384]{2,1,0:T(2,128)(2,1)} %param.21) | copy-start | bytes 9220
  7.2 198.8 %all-gather.7.cloned.1.call-start = ((), (), s32[]{:S(2)}) async-start(), calls=%async_computation.9 | async-start | bytes 6635520 | tf_op jit(solution)/shard_map/all_gather | solution.py:1532
  10.6 20.5 %collective-permute-start = (bf16[256,512]{1,0:T(8,128)(2,1)}, bf16[256,512]{1,0:T(8,128)(2,1)}, u32[]{:S(2)}, u32[]{:S(2)}) collective-permute-start(bf16[256,512]{1,0:T(8,128)(2,1)} %maximum_maximum_fusion.2), channel_id=1, source_target_pairs={{0,0},{1,8},{2,16},{3,24},{4,1},{5,9},{6,17},{7,25},{8,2},{9,10},{... | collective-permute-start | bytes 786440 | tf_op jit(solution)/shard_map/ppermute | solution.py:52
  15.3 6.4 copy-start.24
  15.3 6.4 copy-start.28
  91.5 2.6 copy-start.12
  96.3 178.1 %all-gather.9.cloned.1.call-start = ((), (), s32[]{:S(2)}) async-start(), calls=%async_computation.10 | async-start | bytes 3276800 | tf_op jit(solution)/shard_map/all_gather | solution.py:1541
  97.2 63.4 %copy-start.20 = (f32[2,8,2048]{2,1,0:T(8,128)}, f32[2,8,2048]{2,1,0:T(8,128)S(1)}, u32[]{:S(2)}) copy-start(f32[2,8,2048]{2,1,0:T(8,128)S(1)} %reshape.1868) | copy-start | bytes 393220
  163.1 10.5 %collective-permute-start.1 = (bf16[256,512]{1,0:T(8,128)(2,1)}, bf16[256,512]{1,0:T(8,128)(2,1)S(1)}, u32[]{:S(2)}, u32[]{:S(2)}) collective-permute-start(bf16[256,512]{1,0:T(8,128)(2,1)} %maximum_maximum_fusion.3), channel_id=1, source_target_pairs={{0,0},{1,8},{2,16},{3,24},{4,1},{5,9},{6,17},{7,25},{8,2},{9,10},{... | collective-permute-start | bytes 786440 | tf_op jit(solution)/shard_map/ppermute | solution.py:52
  174.5 196.6 %all-gather.11.cloned.1.call-start = ((), (), s32[]{:S(2)}) async-start(), calls=%async_computation.11 | async-start | bytes 6635520 | tf_op jit(solution)/shard_map/all_gather | solution.py:1532
  206.0 66.2 %copy-start.15 = (bf16[256,1536]{1,0:T(8,128)(2,1)S(1)}, bf16[256,1536]{1,0:T(8,128)(2,1)}, u32[]{:S(2)}) copy-start(bf16[256,1536]{1,0:T(8,128)(2,1)} %param.18) | copy-start | bytes 2359300
  272.1 332.0 %reduce-scatter.5.cloned.1.call-start = ((), (), s32[]{:S(2)}) async-start(), calls=%async_computation.5 | async-start | bytes 6635520 | tf_op jit(solution)/shard_map/reduce_scatter | solution.py:1414
  508.2 172.7 %reduce-scatter.7.cloned.1.call-start = ((), (), s32[]{:S(2)}) async-start(), calls=%async_computation.6 | async-start | bytes 3276800 | tf_op jit(solution)/shard_map/reduce_scatter | solution.py:1414
  604.1 174.0 %reduce-scatter.9.cloned.1.call-start = ((), (), s32[]{:S(2)}) async-start(), calls=%async_computation.7 | async-start | bytes 6635520 | tf_op jit(solution)/shard_map/reduce_scatter | solution.py:1414
  675.6 161.6 %reduce-scatter.11.cloned.1.call-start = ((), (), s32[]{:S(2)}) async-start(), calls=%async_computation.8 | async-start | bytes 3276800 | tf_op jit(solution)/shard_map/reduce_scatter | solution.py:1414
  681.0 92.2 %copy-start.16 = (bf16[1,640,512]{2,1,0:T(8,128)(2,1)S(1)}, bf16[1,640,512]{2,1,0:T(8,128)(2,1)}, u32[]{:S(2)}) copy-start(bf16[1,640,512]{2,1,0:T(8,128)(2,1)} %reduce-scatter.7.cloned.1.call-done) | copy-start | bytes 1966084
  681.0 92.9 %copy-start.23 = (f32[8,256]{1,0:T(8,128)S(1)}, f32[8,256]{1,0:T(8,128)}, u32[]{:S(2)}) copy-start(f32[8,256]{1,0:T(8,128)} %get-tuple-element.135) | copy-start | bytes 24580
  681.0 94.5 %copy-start.25 = (f32[1,1536]{1,0:T(1,128)S(1)}, f32[1,1536]{1,0:T(1,128)}, u32[]{:S(2)}) copy-start(f32[1,1536]{1,0:T(1,128)} %get-tuple-element.133) | copy-start | bytes 18436
  681.0 94.5 %copy-start.26 = (f32[1,1536]{1,0:T(1,128)S(1)}, f32[1,1536]{1,0:T(1,128)}, u32[]{:S(2)}) copy-start(f32[1,1536]{1,0:T(1,128)} %get-tuple-element.132) | copy-start | bytes 18436
  681.0 94.5 %copy-start.27 = (f32[1,1536]{1,0:T(1,128)S(1)}, f32[1,1536]{1,0:T(1,128)}, u32[]{:S(2)}) copy-start(f32[1,1536]{1,0:T(1,128)} %get-tuple-element.131) | copy-start | bytes 18436
  825.8 6.5 copy-start.8
  826.8 5.5 copy-start.6
  835.8 16.7 %copy-start.22 = (bf16[1,64,256]{2,1,0:T(8,128)(2,1)S(1)}, bf16[1,64,256]{2,1,0:T(8,128)(2,1)}, u32[]{:S(2)}) copy-start(bf16[1,64,256]{2,1,0:T(8,128)(2,1)} %get-tuple-element.302) | copy-start | bytes 98308
  835.8 17.4 %copy-start.21 = (bf16[1,64,256]{2,1,0:T(8,128)(2,1)S(1)}, bf16[1,64,256]{2,1,0:T(8,128)(2,1)}, u32[]{:S(2)}) copy-start(bf16[1,64,256]{2,1,0:T(8,128)(2,1)} %get-tuple-element.303) | copy-start | bytes 98308
  835.8 18.0 %copy-start.17 = (bf16[1,64,512]{2,1,0:T(8,128)(2,1)S(1)}, bf16[1,64,512]{2,1,0:T(8,128)(2,1)}, u32[]{:S(2)}) copy-start(bf16[1,64,512]{2,1,0:T(8,128)(2,1)} %get-tuple-element.299) | copy-start | bytes 196612
  835.8 18.0 %copy-start.18 = (bf16[1,64,512]{2,1,0:T(8,128)(2,1)S(1)}, bf16[1,64,512]{2,1,0:T(8,128)(2,1)}, u32[]{:S(2)}) copy-start(bf16[1,64,512]{2,1,0:T(8,128)(2,1)} %get-tuple-element.300) | copy-start | bytes 196612
  835.8 18.0 %copy-start.19 = (bf16[1,64,512]{2,1,0:T(8,128)(2,1)S(1)}, bf16[1,64,512]{2,1,0:T(8,128)(2,1)}, u32[]{:S(2)}) copy-start(bf16[1,64,512]{2,1,0:T(8,128)(2,1)} %get-tuple-element.301) | copy-start | bytes 196612
  838.9 20.9 %all-to-all-start = ((bf16[8,48,512]{2,1,0:T(8,128)(2,1)}), bf16[8,48,512]{2,1,0:T(8,128)(2,1)S(1)}, u32[]{:S(2)}, u32[]{:S(2)}) async-start(bf16[8,48,512]{2,1,0:T(8,128)(2,1)} %bitcast.66), calls=%async_computation.4 | async-start | bytes 786432 | tf_op jit(solution)/shard_map/all_to_all | solution.py:1574
  861.6 6.5 copy-start.1
  (10 other events, 10.0 us)
Sparse Core Ops, SparseCore 0:
  96.4 109.5 all-gather.6
  208.1 53.4 all-gather.8
  272.3 98.7 all-gather.10
  508.4 95.6 reduce-scatter.4
  606.4 52.5 reduce-scatter.6
  675.7 96.7 reduce-scatter.8
  781.3 53.5 reduce-scatter.10

commit v6 on v5

--- a/solution.py
+++ b/solution.py
@@ -240,6 +240,94 @@
     def total(self, at):
         own = self.part[0, 0, at].astype(F32) + self.near[0, at].astype(F32)
         return own + self.far[0, at].astype(F32) + self.far[1, at].astype(F32)
+
+
+class Exchange:
+    def __init__(self, net, seq, blocks, moved, rows_in, rows_out, send, recv, own):
+        self.net = net
+        self.blocks, self.moved, self.rows_in, self.rows_out = blocks, moved, rows_in, rows_out
+        self.send, self.recv, self.own = send, recv, own
+        self.others = [(m, s) for m in range(4) for s in range(2)][1:]
+        each = TP // seq
+        self.owner = lax.rem(net.z + TP - net.t, seq) * each + net.t // seq
+        self.giver = lax.rem(net.t, each) * seq + lax.rem(net.z + TP - net.t // each, seq)
+
+    def pushes(self, arriving=False):
+        copies = []
+        for block, out in zip(self.blocks, self.moved):
+            for m, s in self.others:
+                n, slot = len(copies), self.net.slot(m, s)
+                copies.append(
+                    remote(
+                        block.at[slot], out.at[slot if arriving else self.net.t],
+                        self.send.at[n], self.recv.at[n], self.net.device(m, s),
+                    )
+                )
+        return copies
+
+    def rows(self):
+        first = len(self.blocks) * len(self.others)
+        to = (self.net.base + self.owner, self.net.z)
+        return [
+            remote(src, dst, self.send.at[first + n], self.recv.at[first + n], to)
+            for n, (src, dst) in enumerate(zip(self.rows_in, self.rows_out))
+        ]
+
+    def kept(self):
+        copies = []
+        for block, out in zip(self.blocks, self.moved):
+            at = self.own.at[len(copies)]
+            copies.append(pltpu.make_async_copy(block.at[self.net.t], out.at[self.net.t], at))
+        return copies
+
+    def rows_kept(self):
+        first = len(self.blocks)
+        return [
+            pltpu.make_async_copy(src, dst, self.own.at[first + n])
+            for n, (src, dst) in enumerate(zip(self.rows_in, self.rows_out))
+        ]
+
+    def begin(self):
+        for copy in self.kept() + self.pushes():
+            copy.start()
+
+        @pl.when(self.owner != self.net.t)
+        def _():
+            for copy in self.rows():
+                copy.start()
+
+        @pl.when(self.owner == self.net.t)
+        def _():
+            for copy in self.rows_kept():
+                copy.start()
+
+    def finish(self):
+        for copy in self.pushes(arriving=True):
+            copy.wait_recv()
+        for copy in self.pushes():
+            copy.wait_send()
+        for copy in self.kept():
+            copy.wait()
+
+        @pl.when(self.owner != self.net.t)
+        def _():
+            for copy in self.rows():
+                copy.wait_send()
+
+        @pl.when(self.owner == self.net.t)
+        def _():
+            for copy in self.rows_kept():
+                copy.wait()
+
+        @pl.when(self.giver != self.net.t)
+        def _():
+            for copy in self.rows():
+                copy.wait_recv()
+
+
+def exchange_scratch(blocks, rows):
+    dma, count = pltpu.SemaphoreType.DMA, (TP - 1) * len(blocks) + len(rows)
+    return [dma((count,)), dma((count,)), dma((len(blocks) + len(rows),))]
 
 
 def plane_scratch(rows, width):
@@ -842,13 +930,17 @@
 
 
 def rec_backward_kernel(
-    g_ref, upstream_ref, values_ref, gain_ref, pack_ref, small_ref, slots_ref,
-    x_ref, branch_ref, stream_ref, conv_ref, state_ref,
-    grad_ref, low_ref, gain_out, gcol_ref, channel_ref,
-    full, part, near, wide, far, gs, gr, ss, sr,
+    count, g_ref, upstream_ref, values_ref, gain_ref, pack_ref, small_ref, slots_ref,
+    x_ref, branch_ref, stream_ref, conv_ref, state_ref, *refs
+):
+    given, refs = refs[:count], refs[count:]
+    grad_ref, low_ref, gain_out, gcol_ref, channel_ref, *refs = refs
+    taken, refs = refs[:count], refs[count:]
+    (
+        full, part, near, wide, far, gs, gr, ss, sr,
     col, gates, wout, xs, branch, stream, conv, state,
-    retain, direct, suffix, joined, both, gpre, mixed, ends, carry, hs, hr, es, er, sem,
-):
+    retain, direct, suffix, joined, both, gpre, mixed, ends, carry, hs, hr, es, er, sem, *sems,
+    ) = refs
     net = Net()
     seq = ends.shape[0]
     line = Line(net, seq)
@@ -869,7 +961,15 @@
     loads = unpack_rec(pack_ref, col, wout, gates, sem, 9) + loads
     for load in [own] + loads:
         load.start()
-    net.enter(line.others)
+    if count:
+        exchange = Exchange(
+            net, seq, given[:-1], taken[:-1], given[-1:], taken[-1:], *sems
+        )
+        net.enter(
+            line.others + [net.device(1, 1), net.device(2, 1), net.device(3, 0), net.device(3, 1)]
+        )
+    else:
+        net.enter(line.others)
     own.wait()
     gather.begin()
 
@@ -905,6 +1005,8 @@
         write_halves(retain, at, jnp.where(restart, 0.0, jnp.exp(log_retain)))
 
     steps(gather, None, open_block)
+    if count:
+        exchange.begin()
     lanes = [pl.ds(i, 128) for i in range(0, head, 128)]
 
     def step(i, carried):
@@ -1047,11 +1149,13 @@
         lax.fori_loop(0, TP, lambda i, _: (halo(i).wait_send(), 0)[1], 0)
 
     scatter.finish()
+    if count:
+        exchange.finish()
     end_backward(scatter, upstream_ref, values_ref, gain_ref, grad_ref, low_ref, gain_out)
     gather.finish()
 
 
-def rec_backward(g, upstream, values, gain, pack, small, slots, saved):
+def rec_backward(g, upstream, values, gain, pack, small, slots, saved, given):
     rows, width = g.shape
     seq, _, head = pack.shape
     head = head // 2
@@ -1060,17 +1164,18 @@
     dma = pltpu.SemaphoreType.DMA
     x, branch, stream, conv, state = saved
     return pl.pallas_call(
-        rec_backward_kernel,
+        partial(rec_backward_kernel, len(given)),
         in_specs=[ANY, VM, VM, VM, ANY, VM, pl.BlockSpec(memory_space=pltpu.SMEM)]
-        + [ANY] * 5,
-        out_specs=[VM] * 5,
+        + [ANY] * (5 + len(given)),
+        out_specs=[VM] * 5 + [ANY] * len(given),
         out_shape=[
             shape((rows, width), F32),
             shape((rows, width), BF),
             shape((1, width), F32),
             shape(pack.shape, BF),
             shape((8, head), F32),
-        ],
+        ]
+        + [shape(array.shape, array.dtype) for array in given],
         scratch_shapes=plane_scratch(rows, width)
         + rec_scratch(pack, width)
         + [
@@ -1089,17 +1194,18 @@
             pltpu.VMEM((seq, 2 * TP, head), F32),
             pltpu.VMEM((TP, head), F32),
             dma((TP,)), dma((TP,)), dma((seq - 1,)), dma((seq - 1,)), dma((9 + 5 * seq,)),
-        ],
+        ]
+        + (exchange_scratch(given[:-1], given[-1:]) if given else []),
         compiler_params=pltpu.CompilerParams(
-            collective_id=4, has_side_effects=True, vmem_limit_bytes=60 << 20
+            collective_id=8 if given else 4, has_side_effects=True, vmem_limit_bytes=60 << 20
         ),
         cost_estimate=pl.CostEstimate(
             flops=80 * 10**9, bytes_accessed=30 << 20, transcendentals=0
         ),
-        name="rec_backward",
+        name="rec_backward_exchange" if given else "rec_backward",
     )(
         g, upstream, values, gain.reshape(1, -1), pack, small, slots,
-        x.reshape(tokens, width), branch, stream, conv, state,
+        x.reshape(tokens, width), branch, stream, conv, state, *given,
     )
 
 
@@ -1265,24 +1371,17 @@
 
 def close_kernel(layers, gain_ref, channel_ref, *refs):
     rows_in, refs = refs[:layers], refs[layers:]
-    count = (len(refs) - 8 - layers) // 2
+    count = (len(refs) - 10 - layers) // 2
     blocks, (gain_out, channel_out) = refs[:count], refs[count : count + 2]
     moved, refs = refs[count + 2 : 2 * count + 2], refs[2 * count + 2 :]
     rows_out = refs[:layers]
-    plane_gain, line_gain, line_channel, ps, pr, sem = refs[layers:]
+    plane_gain, line_gain, line_channel, ps, pr, *sems = refs[layers:]
     net = Net()
     seq = line_gain.shape[0]
     line = Line(net, seq)
-    plane = [net.device(m, s) for m in range(4) for s in range(2)][1:]
-    slots = [net.slot(m, s) for m in range(4) for s in range(2)][1:]
-    own = [
-        pltpu.make_async_copy(block.at[net.t], out.at[net.t], sem.at[n])
-        for n, (block, out) in enumerate(zip(blocks, moved))
-    ]
+    plane = [(m, s) for m in range(4) for s in range(2)][1:]
     plane_gain[net.t] = gain_ref[...]
     line_channel[net.z] = channel_ref[...]
-    for copy in own:
-        copy.start()
     net.enter(line.others + [net.device(1, 1), net.device(2, 1), net.device(3, 0), net.device(3, 1)])
     used = []
 
@@ -1293,40 +1392,19 @@
         return remote(src, landed, ps.at[n], pr.at[n], to)
 
     gains = [
-        push(plane_gain.at[net.t], plane_gain.at[net.t], plane_gain.at[slot], to)
-        for slot, to in zip(slots, plane)
+        push(
+            plane_gain.at[net.t], plane_gain.at[net.t], plane_gain.at[net.slot(m, s)],
+            net.device(m, s),
+        )
+        for m, s in plane
     ]
     sources = [lax.rem(net.z + seq - 1 - d, seq) for d in range(seq - 1)]
     rest = [
         push(line_channel.at[net.z], line_channel.at[net.z], line_channel.at[source], to)
         for source, to in zip(sources, line.others)
     ]
-    for block, out in zip(blocks, moved):
-        for slot, to in zip(slots, plane):
-            rest.append(push(block.at[slot], out.at[net.t], out.at[slot], to))
-    each = TP // seq
-    owner = lax.rem(net.z + TP - net.t, seq) * each + net.t // seq
-    giver = lax.rem(net.t, each) * seq + lax.rem(net.z + TP - net.t // each, seq)
-    first = ps.shape[0] - layers
-    rows = [
-        remote(src, dst, ps.at[first + l], pr.at[first + l], (net.base + owner, net.z))
-        for l, (src, dst) in enumerate(zip(rows_in, rows_out))
-    ]
-    rows_here = [
-        pltpu.make_async_copy(src, dst, sem.at[count + l])
-        for l, (src, dst) in enumerate(zip(rows_in, rows_out))
-    ]
-
-    @pl.when(owner != net.t)
-    def _():
-        for copy in rows:
-            copy.start()
-
-    @pl.when(owner == net.t)
-    def _():
-        for copy in rows_here:
-            copy.start()
-
+    exchange = Exchange(net, seq, blocks, moved, rows_in, rows_out, *sems)
+    exchange.begin()
     for copy in gains:
         copy.wait_recv()
     total = plane_gain[0]
@@ -1345,29 +1423,13 @@
     channel_out[...] = channel
     for copy in used:
         copy.wait_send()
-    for copy in own:
-        copy.wait()
-
-    @pl.when(owner != net.t)
-    def _():
-        for copy in rows:
-            copy.wait_send()
-
-    @pl.when(owner == net.t)
-    def _():
-        for copy in rows_here:
-            copy.wait()
-
-    @pl.when(giver != net.t)
-    def _():
-        for copy in rows:
-            copy.wait_recv()
+    exchange.finish()
 
 
 def closing(seq, gains, channels, rows, blocks):
     shape = jax.ShapeDtypeStruct
     dma = pltpu.SemaphoreType.DMA
-    pushes = (TP - 1) * (1 + len(blocks)) + 2 * (seq - 1) + len(rows)
+    pushes = TP - 1 + 2 * (seq - 1)
     return pl.pallas_call(
         partial(close_kernel, len(rows)),
         in_specs=[VM, VM] + [ANY] * (len(rows) + len(blocks)),
@@ -1378,8 +1440,9 @@
             pltpu.VMEM((TP,) + gains.shape, F32),
             pltpu.VMEM((seq,) + gains.shape, F32),
             pltpu.VMEM((seq,) + channels.shape, F32),
-            dma((pushes,)), dma((pushes,)), dma((len(blocks) + len(rows),)),
-        ],
+            dma((pushes,)), dma((pushes,)),
+        ]
+        + exchange_scratch(blocks, rows),
         compiler_params=pltpu.CompilerParams(
             collective_id=7, has_side_effects=True, vmem_limit_bytes=40 << 20
         ),
@@ -1390,7 +1453,7 @@
     )(gains, channels, *rows, *blocks)
 
 
-def layer_backward(upstream, upstream_low, w, saved, slots, pending):
+def layer_backward(split, upstream, upstream_low, w, saved, slots, pending):
     residual, kept, middle, kept_two = saved
     pending_mlp, pending_rec = pending
     upstream_low, pending_mlp = lax.optimization_barrier((upstream_low, pending_mlp))
@@ -1399,15 +1462,19 @@
     )
     mlp_share = over_seq(g_mlp)
     mid_low, pending_rec = lax.optimization_barrier((mid_low, pending_rec))
-    grad, grad_low, grad_gain_one, g_rec, channel = rec_backward(
-        mid_low, grad_middle, residual, w["gain"][0], w["rec"], w["small"], slots, kept
+    given = []
+    if not isinstance(pending_mlp, tuple):
+        (mlp_block, rows), (rec_block, _) = split(pending_mlp), split(pending_rec)
+        given = [mlp_block, rec_block, rows]
+    grad, grad_low, grad_gain_one, g_rec, channel, *taken = rec_backward(
+        mid_low, grad_middle, residual, w["gain"][0], w["rec"], w["small"], slots, kept, given
     )
     g_rec, mlp_share = lax.optimization_barrier((g_rec, mlp_share))
     rec_share = over_seq(g_rec)
     slope = 8.0 * jax.nn.sigmoid(-w["decay"])
     channel = jnp.concatenate([channel[:7], channel[7:] * slope], 0)
     gains = jnp.concatenate([grad_gain_one, grad_gain_two], 0)
-    return grad, grad_low, (mlp_share, rec_share), channel, gains, (pending_mlp, pending_rec)
+    return grad, grad_low, (mlp_share, rec_share), channel, gains, (pending_mlp, pending_rec), taken
 
 
 def over_seq(value):
@@ -1549,32 +1616,29 @@
     gradient = cotangent.astype(F32) * inside.astype(F32)[:, None]
 
     gradient_low = gradient.astype(BF)
-    shares = [None] * LAYERS
+    width = block_input.shape[1]
+    base = width // seq
+
+    def split(share):
+        return share[:base].reshape(tp, -1, share.shape[1]), share[base:]
+
+    shares, mlps, recs, downs = ([None] * LAYERS for _ in range(4))
     channel_all, gain_all = [None] * LAYERS, [None] * LAYERS
     for l in reversed(range(LAYERS)):
-        gradient, gradient_low, shares[l], channel_all[l], gain_all[l], pending = layer_backward(
-            gradient, gradient_low, weights[l], saved_all[l], layout,
+        gradient, gradient_low, shares[l], channel_all[l], gain_all[l], pending, taken = layer_backward(
+            split, gradient, gradient_low, weights[l], saved_all[l], layout,
             ((), ()) if l + 1 == LAYERS else shares[l + 1],
         )
         if l + 1 < LAYERS:
-            shares[l + 1] = pending
-    width = block_input.shape[1]
-    base = width // seq
-
-    def by_slot(share):
-        return share[:base].reshape(tp, -1, share.shape[1])
-
-    blocks = [by_slot(shares[l][0]) for l in range(LAYERS)]
-    blocks += [by_slot(shares[l][1]) for l in range(1, LAYERS)]
-    gains, channel, *blocks = closing(
-        seq, jnp.concatenate(gain_all, 0), jnp.concatenate(channel_all, 0),
-        [shares[l][0][base:] for l in range(LAYERS)], blocks,
+            shares[l + 1], mlps[l + 1], recs[l + 1], downs[l + 1] = pending, *taken
+    mlp_block, rows = split(shares[0][0])
+    gains, channel, mlps[0], downs[0] = closing(
+        seq, jnp.concatenate(gain_all, 0), jnp.concatenate(channel_all, 0), [rows], [mlp_block]
     )
-    blocks, downs = blocks[:-LAYERS], blocks[-LAYERS:]
-    last = lax.all_to_all(
-        by_slot(shares[0][1]), "rep", split_axis=0, concat_axis=0, axis_index_groups=plan.tp_groups
+    recs[0] = lax.all_to_all(
+        split(shares[0][1])[0], "rep", split_axis=0, concat_axis=0,
+        axis_index_groups=plan.tp_groups,
     )
-    mlps, recs = blocks[:LAYERS], [last] + blocks[LAYERS:]
     outs = [
         owned_grads(plan, downs[l], shares[l][1], mlps[l], recs[l], width, head, units)
         for l in range(LAYERS)

time: 885 us -> 878 us (level)
  waiting for transfers between devices: 59.9 us -> 85.6 us
  Pallas kernels: 687 us -> 673 us
  local copies, waits for them, and re-layouts: 67.1 us -> 56.9 us
    reduce_scatter x4, waiting for transfers between devices: 6.53 us -> 35.2 us  [over_seq(): return lax.psum_scatter(value, 'seq', scatter_dimension=0, tiled=False)]
    pallas_call x1, Pallas kernels: 30.3 us -> 16.3 us  [closing(): pl.pallas_call(partial(close_kernel, len(rows)), in_specs=[VM, VM] + [ANY...]
    all_to_all x1, starting transfers between devices: 12.6 us -> 3.45 us  [local(): lax.all_to_all(split(shares[0][1])[0], 'rep', split_axis=0, concat_axis=0...]
  transfers between devices with their start and end apart: 10 -> 10, of which waited for: 4 -> 5; matrix products, arithmetic and copies ran while one was open for 7% -> 7% of each run, Pallas kernels for 56% -> 55%
where the time goes in v6:
time: 878 us; the launch traced here: 869 us
  Pallas kernels  673 us (77%)
  waiting for transfers between devices  85.6 us (10%)
  local copies, waits for them, and re-layouts  56.9 us (6%)
  other arithmetic  26.1 us (3%)
  between operations  16.8 us (2%)
  starting transfers between devices  10.9 us (1%)
    pallas_call x2, Pallas kernels, rec_backward(): pl.pallas_call(partial(rec_backward_kernel, len(given)), in_specs=[ANY, V...  181 us
    pallas_call x2, Pallas kernels, rec_forward(): pl.pallas_call(partial(rec_forward_kernel, gathered), in_specs=[ANY, VM,...  143 us
    pallas_call x2, Pallas kernels, mlp_backward(): pl.pallas_call(mlp_backward_kernel, in_specs=[ANY, VM, VM, VM, ANY, ANY,...  142 us
    pallas_call x2, Pallas kernels, mlp_forward(): pl.pallas_call(mlp_forward_kernel, in_specs=[ANY, VM, VM, ANY], out_specs...  133 us
    pallas_call x1, Pallas kernels, opening(): pl.pallas_call(open_kernel, in_specs=[VM] + [ANY] * 4, out_specs=[ANY] *...  58.2 us
    all_gather x2, waiting for transfers between devices, local(): lax.all_gather(mlp, 'seq')  45.3 us
    reduce_scatter x4, waiting for transfers between devices, over_seq(): return lax.psum_scatter(value, 'seq', scatter_dimension=0, tiled=False)  35.2 us
  transfers between devices with their start and end apart: 10, of which 5 were waited for; matrix products, arithmetic and copies ran while one was open for 7% of the time, Pallas kernels for 55%

profile of v6, /device:TPU:0, one launch (start us, length us, event | category | flops | bytes accessed | tf_op | source)
XLA Modules:
  0.0 869.1 jit_solution(6080338533717107460)
XLA Ops:
  7.3 1.8 copy-done
  10.6 3.6 collective-permute-start
  17.5 2.5 convert_element_type.157.residual_ref.values_ref
  20.0 1.7 dynamic-slice_bitcast_fusion.14
  21.7 3.5 dynamic-slice_bitcast_fusion.16
  25.2 3.5 concatenate.157
  28.7 2.4 maximum_maximum_fusion
  33.3 58.2 %opening.1 = (f32[4,16,512]{2,1,0:T(8,128)S(1)}, f32[4,4,384]{2,1,0:T(4,128)S(1)}, s32[8,8,128]{2,1,0:T(8,128)S(1)}, bf16[8,256,1536]{2,1,0:T(8,128)(2,1)S(1)}, bf16[4,640,512]{2,1,0:T(8,128)(2,1)S(1)}) custom-call(bf16[256,1536]{1,0:T(8,128)(2,1)S(1)} %copy-done.2, f32[16,512]{1,0:T(8,128)S(1)} %fusion.small_ref, f32[4,384]{1,0:T(4,128)S(1)} %reshape.1883.gain_ref, ...), custom_call_target="tpu_custom_call" | custom-call | flops 40000000000 | bytes 10485760 | tf_op jit(solution)/shard_map/opening/pallas_call | solution.py:1344
  91.5 2.6 copy-done.3
  97.9 62.7 %rec_forward_first.1 = (f32[256,1536]{1,0:T(8,128)}, bf16[256,1536]{1,0:T(8,128)(2,1)}, bf16[8,128]{1,0:T(8,128)(2,1)}, f32[8,256,256]{2,1,0:T(8,128)}, f32[8,26...) custom-call(bf16[8,256,1536]{2,1,0:T(8,128)(2,1)} %copy-done.3, ...), custom_call_target="tpu_custom_call" | custom-call | flops 70000001024 | bytes 31457280 | tf_op jit(solution)/shard_map/rec_forward_first/pallas_call | solution.py:893
  163.0 3.6 collective-permute-start.1
  175.5 1.8 pad_maximum_fusion.1
  177.4 28.5 %all-gather.7.cloned.1.call-done = bf16[2304,1152]{1,0:T(8,128)(2,1)} async-done(((bf16[576,1152]{1,0:T(8,128)(2,1)}), bf16[2304,1152]{1,0:T(8,128)(2,1)}) %all-gather.7.cloned.1.call-update) | async-done | bytes 5308432 | tf_op jit(solution)/shard_map/all_gather | solution.py:1599
  206.0 66.1 %mlp_forward.2 = (f32[256,1536]{1,0:T(8,128)}, bf16[256,1536]{1,0:T(8,128)(2,1)}, bf16[8,256,1536]{2,1,0:T(8,128)(2,1)}, bf16[8,256,1152]{2,1,0:T(8,128)(2,1)}) custom-call(bf16[256,1536]{1,0:T(8,128)(2,1)} %get-tuple-element.93.x_ref, f32[256,1536]{1,0:T(8,128)} %get-tuple-element.94.residual_ref.values_ref, f32[1,1536]{1,0:T(1,128)} %get-tuple-element.339.gain_ref, ...), custom_call_target="tpu_custom_call" | custom-call | flops 60000002048 | bytes 31457280 | tf_op jit(solution)/shard_map/mlp_forward/pallas_call | solution.py:507
  272.2 1.6 convert_multiply_fusion
  274.5 79.8 %rec_forward.1 = (f32[256,1536]{1,0:T(8,128)}, bf16[256,1536]{1,0:T(8,128)(2,1)}, bf16[8,256,1536]{2,1,0:T(8,128)(2,1)}, f32[8,256,256]{2,1,0:T(8,128)}, f32[8,2...) custom-call(bf16[256,1536]{1,0:T(8,128)(2,1)} %get-tuple-element.97.x_ref, ...), custom_call_target="tpu_custom_call" | custom-call | flops 70000001024 | bytes 31457280 | tf_op jit(solution)/shard_map/rec_forward/pallas_call | solution.py:893
  354.3 16.8 %all-gather.11.cloned.1.call-done = bf16[2304,1152]{1,0:T(8,128)(2,1)} async-done(((bf16[576,1152]{1,0:T(8,128)(2,1)}), bf16[2304,1152]{1,0:T(8,128)(2,1)}) %all-gather.11.cloned.1.call-update) | async-done | bytes 5308432 | tf_op jit(solution)/shard_map/all_gather | solution.py:1599
  371.1 66.6 %mlp_forward.3 = (f32[256,1536]{1,0:T(8,128)}, bf16[256,1536]{1,0:T(8,128)(2,1)}, bf16[8,256,1536]{2,1,0:T(8,128)(2,1)}, bf16[8,256,1152]{2,1,0:T(8,128)(2,1)}) custom-call(bf16[256,1536]{1,0:T(8,128)(2,1)} %get-tuple-element.100.x_ref, f32[256,1536]{1,0:T(8,128)} %get-tuple-element.101.residual_ref.values_ref, f32[1,1536]{1,0:T(1,128)} %get-tuple-element.338.gain_ref, ...), custom_call_target="tpu_custom_call" | custom-call | flops 60000002048 | bytes 31457280 | tf_op jit(solution)/shard_map/mlp_forward/pallas_call | solution.py:507
  437.6 70.6 %mlp_backward.2 = (f32[256,1536]{1,0:T(8,128)}, bf16[256,1536]{1,0:T(8,128)(2,1)}, f32[1,1536]{1,0:T(1,128)}, bf16[4,576,1152]{2,1,0:T(8,128)(2,1)}) custom-call(bf16[256,1536]{1,0:T(8,128)(2,1)} %get-tuple-element.294.g_ref, f32[256,1536]{1,0:T(8,128)} %get-tuple-element.293.upstream_ref, f32[256,1536]{1,0:T(8,128)} %get-tuple-element.101.residual_ref.values_ref, ...), custom_call_target="tpu_custom_call" | custom-call | flops 70000001024 | bytes 31457280 | tf_op jit(solution)/shard_map/mlp_backward/pallas_call | solution.py:620
  508.3 89.3 %rec_backward.1 = (f32[256,1536]{1,0:T(8,128)}, bf16[256,1536]{1,0:T(8,128)(2,1)}, f32[1,1536]{1,0:T(1,128)}, bf16[4,640,512]{2,1,0:T(8,128)(2,1)}, f32[8,256]{1,0:T(8,128)}) custom-call(bf16[256,1536]{1,0:T(8,128)(2,1)} %get-tuple-element.106.g_ref, f32[256,1536]{1,0:T(8,128)} %get-tuple-element.107.upstream_ref, ...), custom_call_target="tpu_custom_call" | custom-call | flops 80000000000 | bytes 31457280 | tf_op jit(solution)/shard_map/rec_backward/pallas_call | solution.py:1166
  597.6 6.5 reduce-scatter.5.cloned.1.call-done
  604.2 71.4 %mlp_backward.3 = (f32[256,1536]{1,0:T(8,128)}, bf16[256,1536]{1,0:T(8,128)(2,1)}, f32[1,1536]{1,0:T(1,128)}, bf16[4,576,1152]{2,1,0:T(8,128)(2,1)}) custom-call(bf16[256,1536]{1,0:T(8,128)(2,1)} %get-tuple-element.117.g_ref, f32[256,1536]{1,0:T(8,128)} %get-tuple-element.118.upstream_ref, f32[256,1536]{1,0:T(8,128)} %get-tuple-element.94.residual_ref.values_ref, ...), custom_call_target="tpu_custom_call" | custom-call | flops 70000001024 | bytes 31457280 | tf_op jit(solution)/shard_map/mlp_backward/pallas_call | solution.py:620
  679.7 1.8 slice.766
  681.5 92.1 %rec_backward_exchange.1 = (f32[256,1536]{1,0:T(8,128)}, bf16[256,1536]{1,0:T(8,128)(2,1)}, f32[1,1536]{1,0:T(1,128)}, bf16[4,640,512]{2,1,0:T(8,128)(2,1)}, f32...) custom-call(bf16[256,1536]{1,0:T(8,128)(2,1)} %get-tuple-element.123.g_re, ...), custom_call_target="tpu_custom_call" | custom-call | flops 80000000000 | bytes 31457280 | tf_op jit(solution)/shard_map/rec_backward_exchange/pallas_call | solution.py:1166
  786.5 16.3 %closing.1 = (f32[4,1536]{1,0:T(4,128)S(1)}, f32[16,256]{1,0:T(8,128)S(1)}, bf16[8,48,1152]{2,1,0:T(8,128)(2,1)S(1)}, bf16[192,1152]{1,0:T(8,128)(2,1)S(1)}) custom-call(f32[4,1536]{1,0:T(4,128)S(1)} %pad_maximum_fusion.2.gain_ref, f32[16,256]{1,0:T(8,128)S(1)} %pad_maximum_fusion.3.channel_ref, bf16[192,1152]{1,0:T(8,128)(2,1)S(1)} %slice.772.refs_0_, ...), custom_call_target="tpu_custom_call" | custom-call | flops 40000000000 | bytes 10485760 | tf_op jit(solution)/shard_map/closing/pallas_call | solution.py:1433
  811.4 28.7 %reduce-scatter.11.cloned.1.call-done = bf16[1,640,512]{2,1,0:T(8,128)(2,1)} async-done(((bf16[4,640,512]{2,1,0:T(8,128)(2,1)}), bf16[1,640,512]{2,1,0:T(8,128)(2,1)}) %reduce-scatter.11.cloned.1.call-update) | async-done | bytes 655376 | tf_op jit(solution)/shard_map/reduce_scatter | solution.py:1481
  840.1 1.8 slice.951
  841.9 3.5 all-to-all-start
  848.7 5.0 all-to-all-done
  855.3 2.0 maximum_convert_fusion.3
  857.3 1.9 maximum_convert_fusion.4
  859.2 2.7 copy.59
  (172 shorter events, 51.9 us)
Async XLA Ops:
  7.2 10.2 %copy-start.30 = (bf16[2,512]{1,0:T(2,128)(2,1)S(1)}, bf16[2,512]{1,0:T(2,128)(2,1)}, u32[]{:S(2)}) copy-start(bf16[2,512]{1,0:T(2,128)(2,1)} %param.25) | copy-start | bytes 6148
  7.2 10.2 %copy-start.31 = (bf16[2,512]{1,0:T(2,128)(2,1)S(1)}, bf16[2,512]{1,0:T(2,128)(2,1)}, u32[]{:S(2)}) copy-start(bf16[2,512]{1,0:T(2,128)(2,1)} %param.29) | copy-start | bytes 6148
  7.2 10.3 %copy-start.29 = (bf16[2,2,384]{2,1,0:T(2,128)(2,1)S(1)}, bf16[2,2,384]{2,1,0:T(2,128)(2,1)}, u32[]{:S(2)}) copy-start(bf16[2,2,384]{2,1,0:T(2,128)(2,1)} %param.21) | copy-start | bytes 9220
  7.2 198.8 %all-gather.7.cloned.1.call-start = ((), (), s32[]{:S(2)}) async-start(), calls=%async_computation.9 | async-start | bytes 6635520 | tf_op jit(solution)/shard_map/all_gather | solution.py:1599
  10.6 20.5 %collective-permute-start = (bf16[256,512]{1,0:T(8,128)(2,1)}, bf16[256,512]{1,0:T(8,128)(2,1)}, u32[]{:S(2)}, u32[]{:S(2)}) collective-permute-start(bf16[256,512]{1,0:T(8,128)(2,1)} %maximum_maximum_fusion.2), channel_id=1, source_target_pairs={{0,0},{1,8},{2,16},{3,24},{4,1},{5,9},{6,17},{7,25},{8,2},{9,10},{... | collective-permute-start | bytes 786440 | tf_op jit(solution)/shard_map/ppermute | solution.py:52
  15.3 6.4 copy-start.23
  15.3 6.4 copy-start.28
  96.3 178.1 %all-gather.9.cloned.1.call-start = ((), (), s32[]{:S(2)}) async-start(), calls=%async_computation.10 | async-start | bytes 3276800 | tf_op jit(solution)/shard_map/all_gather | solution.py:1608
  97.2 63.4 %copy-start.18 = (f32[2,8,2048]{2,1,0:T(8,128)}, f32[2,8,2048]{2,1,0:T(8,128)S(1)}, u32[]{:S(2)}) copy-start(f32[2,8,2048]{2,1,0:T(8,128)S(1)} %reshape.1868) | copy-start | bytes 393220
  163.0 12.5 %collective-permute-start.1 = (bf16[256,512]{1,0:T(8,128)(2,1)}, bf16[256,512]{1,0:T(8,128)(2,1)}, u32[]{:S(2)}, u32[]{:S(2)}) collective-permute-start(bf16[256,512]{1,0:T(8,128)(2,1)} %maximum_maximum_fusion.3), channel_id=1, source_target_pairs={{0,0},{1,8},{2,16},{3,24},{4,1},{5,9},{6,17},{7,25},{8,2},{9,10},{... | collective-permute-start | bytes 786440 | tf_op jit(solution)/shard_map/ppermute | solution.py:52
  177.4 193.7 %all-gather.11.cloned.1.call-start = ((), (), s32[]{:S(2)}) async-start(), calls=%async_computation.11 | async-start | bytes 6635520 | tf_op jit(solution)/shard_map/all_gather | solution.py:1599
  206.0 66.2 %copy-start.12 = (bf16[256,1536]{1,0:T(8,128)(2,1)S(1)}, bf16[256,1536]{1,0:T(8,128)(2,1)}, u32[]{:S(2)}) copy-start(bf16[256,1536]{1,0:T(8,128)(2,1)} %param.18) | copy-start | bytes 2359300
  272.1 332.0 %reduce-scatter.5.cloned.1.call-start = ((), (), s32[]{:S(2)}) async-start(), calls=%async_computation.5 | async-start | bytes 6635520 | tf_op jit(solution)/shard_map/reduce_scatter | solution.py:1481
  508.2 171.4 %reduce-scatter.7.cloned.1.call-start = ((), (), s32[]{:S(2)}) async-start(), calls=%async_computation.6 | async-start | bytes 3276800 | tf_op jit(solution)/shard_map/reduce_scatter | solution.py:1481
  604.1 180.1 %reduce-scatter.9.cloned.1.call-start = ((), (), s32[]{:S(2)}) async-start(), calls=%async_computation.7 | async-start | bytes 6635520 | tf_op jit(solution)/shard_map/reduce_scatter | solution.py:1481
  675.6 164.5 %reduce-scatter.11.cloned.1.call-start = ((), (), s32[]{:S(2)}) async-start(), calls=%async_computation.8 | async-start | bytes 3276800 | tf_op jit(solution)/shard_map/reduce_scatter | solution.py:1481
  776.6 3.1 copy-start.21
  776.6 3.0 copy-start.22
  776.6 3.9 copy-start.13
  776.8 4.3 copy-start.24
  776.8 4.3 copy-start.25
  776.8 4.3 copy-start.26
  776.8 4.3 copy-start.27
  810.1 36.2 %copy-start.20 = (bf16[1,64,256]{2,1,0:T(8,128)(2,1)S(1)}, bf16[1,64,256]{2,1,0:T(8,128)(2,1)}, u32[]{:S(2)}) copy-start(bf16[1,64,256]{2,1,0:T(8,128)(2,1)} %get-tuple-element.302) | copy-start | bytes 98308
  810.1 36.9 %copy-start.19 = (bf16[1,64,256]{2,1,0:T(8,128)(2,1)S(1)}, bf16[1,64,256]{2,1,0:T(8,128)(2,1)}, u32[]{:S(2)}) copy-start(bf16[1,64,256]{2,1,0:T(8,128)(2,1)} %get-tuple-element.303) | copy-start | bytes 98308
  810.1 37.6 %copy-start.15 = (bf16[1,64,512]{2,1,0:T(8,128)(2,1)S(1)}, bf16[1,64,512]{2,1,0:T(8,128)(2,1)}, u32[]{:S(2)}) copy-start(bf16[1,64,512]{2,1,0:T(8,128)(2,1)} %get-tuple-element.299) | copy-start | bytes 196612
  810.1 37.6 %copy-start.16 = (bf16[1,64,512]{2,1,0:T(8,128)(2,1)S(1)}, bf16[1,64,512]{2,1,0:T(8,128)(2,1)}, u32[]{:S(2)}) copy-start(bf16[1,64,512]{2,1,0:T(8,128)(2,1)} %get-tuple-element.300) | copy-start | bytes 196612
  810.1 37.6 %copy-start.17 = (bf16[1,64,512]{2,1,0:T(8,128)(2,1)S(1)}, bf16[1,64,512]{2,1,0:T(8,128)(2,1)}, u32[]{:S(2)}) copy-start(bf16[1,64,512]{2,1,0:T(8,128)(2,1)} %get-tuple-element.301) | copy-start | bytes 196612
  841.9 11.7 %all-to-all-start = ((bf16[8,48,512]{2,1,0:T(8,128)(2,1)}), bf16[8,48,512]{2,1,0:T(8,128)(2,1)S(1)}, u32[]{:S(2)}, u32[]{:S(2)}) async-start(bf16[8,48,512]{2,1,0:T(8,128)(2,1)} %bitcast.66), calls=%async_computation.4 | async-start | bytes 786432 | tf_op jit(solution)/shard_map/all_to_all | solution.py:1638
  846.3 9.0 %copy-start.11 = (bf16[1,48,2048]{2,1,0:T(8,128)(2,1)S(1)}, bf16[1,48,2048]{2,1,0:T(8,128)(2,1)}, u32[]{:S(2)}) copy-start(bf16[1,48,2048]{2,1,0:T(8,128)(2,1)} %convert_element_type.165) | copy-start | bytes 589828
  847.7 9.7 %copy-start.10 = (bf16[1,48,2048]{2,1,0:T(8,128)(2,1)S(1)}, bf16[1,48,2048]{2,1,0:T(8,128)(2,1)}, u32[]{:S(2)}) copy-start(bf16[1,48,2048]{2,1,0:T(8,128)(2,1)} %convert_element_type.169) | copy-start | bytes 589828
  855.3 6.5 copy-start.1
  (10 other events, 22.1 us)
Sparse Core Ops, SparseCore 0:
  96.4 109.5 all-gather.6
  208.1 53.4 all-gather.8
  272.3 98.7 all-gather.10
  508.4 95.6 reduce-scatter.4
  606.4 52.5 reduce-scatter.6
  675.7 96.7 reduce-scatter.8
  786.7 53.4 reduce-scatter.10

commit v7 on v6

--- a/solution.py
+++ b/solution.py
@@ -1589,8 +1589,6 @@
     residual = block_input.astype(F32)
     saved_all, weights = [], []
     for l in range(LAYERS):
-        if l > 0:
-            mlp, normed = lax.optimization_barrier((mlp, normed))
         w = dict(
             gain=gains[l],
             small=jnp.concatenate([smalls[l, :7], -8.0 * jax.nn.softplus(-smalls[l, 7:])], 0),

time: 878 us -> 870 us (level)
  no operation moved by 1% of the time
where the time goes in v7:
time: 870 us; the launch traced here: 861 us
  Pallas kernels  672 us (77%)
  waiting for transfers between devices  77.7 us (9%)
  local copies, waits for them, and re-layouts  56.8 us (7%)
  other arithmetic  26.2 us (3%)
  between operations  16.8 us (2%)
  starting transfers between devices  10.9 us (1%)
    pallas_call x2, Pallas kernels, rec_backward(): pl.pallas_call(partial(rec_backward_kernel, len(given)), in_specs=[ANY, V...  182 us
    pallas_call x2, Pallas kernels, rec_forward(): pl.pallas_call(partial(rec_forward_kernel, gathered), in_specs=[ANY, VM,...  142 us
    pallas_call x2, Pallas kernels, mlp_backward(): pl.pallas_call(mlp_backward_kernel, in_specs=[ANY, VM, VM, VM, ANY, ANY,...  142 us
    pallas_call x2, Pallas kernels, mlp_forward(): pl.pallas_call(mlp_forward_kernel, in_specs=[ANY, VM, VM, ANY], out_specs...  133 us
    pallas_call x1, Pallas kernels, opening(): pl.pallas_call(open_kernel, in_specs=[VM] + [ANY] * 4, out_specs=[ANY] *...  58.2 us
    all_gather x2, waiting for transfers between devices, local(): lax.all_gather(mlp, 'seq')  37.3 us
    reduce_scatter x4, waiting for transfers between devices, over_seq(): return lax.psum_scatter(value, 'seq', scatter_dimension=0, tiled=False)  35.3 us
  transfers between devices with their start and end apart: 10, of which 5 were waited for; matrix products, arithmetic and copies ran while one was open for 7% of the time, Pallas kernels for 55%

profile of v7, /device:TPU:0, one launch (start us, length us, event | category | flops | bytes accessed | tf_op | source)
XLA Modules:
  0.0 860.9 jit_solution(1288335367421295494)
XLA Ops:
  7.3 1.8 copy-done
  10.6 3.6 collective-permute-start
  17.4 2.5 convert_element_type.157.residual_ref.values_ref
  19.9 1.8 dynamic-slice_bitcast_fusion.14
  21.7 3.5 dynamic-slice_bitcast_fusion.16
  25.1 3.5 concatenate.157
  28.7 2.4 maximum_maximum_fusion
  33.4 58.2 %opening.1 = (f32[4,16,512]{2,1,0:T(8,128)S(1)}, f32[4,4,384]{2,1,0:T(4,128)S(1)}, s32[8,8,128]{2,1,0:T(8,128)S(1)}, bf16[8,256,1536]{2,1,0:T(8,128)(2,1)S(1)}, bf16[4,640,512]{2,1,0:T(8,128)(2,1)S(1)}) custom-call(bf16[256,1536]{1,0:T(8,128)(2,1)S(1)} %copy-done.2, f32[16,512]{1,0:T(8,128)S(1)} %fusion.small_ref, f32[4,384]{1,0:T(4,128)S(1)} %reshape.1883.gain_ref, ...), custom_call_target="tpu_custom_call" | custom-call | flops 40000000000 | bytes 10485760 | tf_op jit(solution)/shard_map/opening/pallas_call | solution.py:1344
  91.5 2.6 copy-done.3
  97.9 62.4 %rec_forward_first.1 = (f32[256,1536]{1,0:T(8,128)}, bf16[256,1536]{1,0:T(8,128)(2,1)}, bf16[8,128]{1,0:T(8,128)(2,1)}, f32[8,256,256]{2,1,0:T(8,128)}, f32[8,26...) custom-call(bf16[8,256,1536]{2,1,0:T(8,128)(2,1)} %copy-done.3, ...), custom_call_target="tpu_custom_call" | custom-call | flops 70000001024 | bytes 31457280 | tf_op jit(solution)/shard_map/rec_forward_first/pallas_call | solution.py:893
  162.7 3.6 collective-permute-start.1
  174.6 1.8 pad_maximum_fusion.1
  176.6 1.6 convert_multiply_fusion
  179.5 25.8 %all-gather.7.cloned.1.call-done = bf16[2304,1152]{1,0:T(8,128)(2,1)} async-done(((bf16[576,1152]{1,0:T(8,128)(2,1)}), bf16[2304,1152]{1,0:T(8,128)(2,1)}) %all-gather.7.cloned.1.call-update) | async-done | bytes 5308432 | tf_op jit(solution)/shard_map/all_gather | solution.py:1597
  205.3 66.1 %mlp_forward.2 = (f32[256,1536]{1,0:T(8,128)}, bf16[256,1536]{1,0:T(8,128)(2,1)}, bf16[8,256,1536]{2,1,0:T(8,128)(2,1)}, bf16[8,256,1152]{2,1,0:T(8,128)(2,1)}) custom-call(bf16[256,1536]{1,0:T(8,128)(2,1)} %get-tuple-element.90.x_ref, f32[256,1536]{1,0:T(8,128)} %get-tuple-element.91.residual_ref.values_ref, f32[1,1536]{1,0:T(1,128)} %get-tuple-element.335.gain_ref, ...), custom_call_target="tpu_custom_call" | custom-call | flops 60000002048 | bytes 31457280 | tf_op jit(solution)/shard_map/mlp_forward/pallas_call | solution.py:507
  271.5 79.6 %rec_forward.1 = (f32[256,1536]{1,0:T(8,128)}, bf16[256,1536]{1,0:T(8,128)(2,1)}, bf16[8,256,1536]{2,1,0:T(8,128)(2,1)}, f32[8,256,256]{2,1,0:T(8,128)}, f32[8,2...) custom-call(bf16[256,1536]{1,0:T(8,128)(2,1)} %get-tuple-element.93.x_ref, ...), custom_call_target="tpu_custom_call" | custom-call | flops 70000001024 | bytes 31457280 | tf_op jit(solution)/shard_map/rec_forward/pallas_call | solution.py:893
  351.1 11.5 %all-gather.11.cloned.1.call-done = bf16[2304,1152]{1,0:T(8,128)(2,1)} async-done(((bf16[576,1152]{1,0:T(8,128)(2,1)}), bf16[2304,1152]{1,0:T(8,128)(2,1)}) %all-gather.11.cloned.1.call-update) | async-done | bytes 5308432 | tf_op jit(solution)/shard_map/all_gather | solution.py:1597
  362.7 66.5 %mlp_forward.3 = (f32[256,1536]{1,0:T(8,128)}, bf16[256,1536]{1,0:T(8,128)(2,1)}, bf16[8,256,1536]{2,1,0:T(8,128)(2,1)}, bf16[8,256,1152]{2,1,0:T(8,128)(2,1)}) custom-call(bf16[256,1536]{1,0:T(8,128)(2,1)} %get-tuple-element.96.x_ref, f32[256,1536]{1,0:T(8,128)} %get-tuple-element.97.residual_ref.values_ref, f32[1,1536]{1,0:T(1,128)} %get-tuple-element.334.gain_ref, ...), custom_call_target="tpu_custom_call" | custom-call | flops 60000002048 | bytes 31457280 | tf_op jit(solution)/shard_map/mlp_forward/pallas_call | solution.py:507
  429.1 70.5 %mlp_backward.2 = (f32[256,1536]{1,0:T(8,128)}, bf16[256,1536]{1,0:T(8,128)(2,1)}, f32[1,1536]{1,0:T(1,128)}, bf16[4,576,1152]{2,1,0:T(8,128)(2,1)}) custom-call(bf16[256,1536]{1,0:T(8,128)(2,1)} %get-tuple-element.290.g_ref, f32[256,1536]{1,0:T(8,128)} %get-tuple-element.289.upstream_ref, f32[256,1536]{1,0:T(8,128)} %get-tuple-element.97.residual_ref.values_ref, ...), custom_call_target="tpu_custom_call" | custom-call | flops 70000001024 | bytes 31457280 | tf_op jit(solution)/shard_map/mlp_backward/pallas_call | solution.py:620
  499.8 89.5 %rec_backward.1 = (f32[256,1536]{1,0:T(8,128)}, bf16[256,1536]{1,0:T(8,128)(2,1)}, f32[1,1536]{1,0:T(1,128)}, bf16[4,640,512]{2,1,0:T(8,128)(2,1)}, f32[8,256]{1,0:T(8,128)}) custom-call(bf16[256,1536]{1,0:T(8,128)(2,1)} %get-tuple-element.102.g_ref, f32[256,1536]{1,0:T(8,128)} %get-tuple-element.103.upstream_ref, ...), custom_call_target="tpu_custom_call" | custom-call | flops 80000000000 | bytes 31457280 | tf_op jit(solution)/shard_map/rec_backward/pallas_call | solution.py:1166
  589.3 6.6 reduce-scatter.5.cloned.1.call-done
  595.9 71.3 %mlp_backward.3 = (f32[256,1536]{1,0:T(8,128)}, bf16[256,1536]{1,0:T(8,128)(2,1)}, f32[1,1536]{1,0:T(1,128)}, bf16[4,576,1152]{2,1,0:T(8,128)(2,1)}) custom-call(bf16[256,1536]{1,0:T(8,128)(2,1)} %get-tuple-element.113.g_ref, f32[256,1536]{1,0:T(8,128)} %get-tuple-element.114.upstream_ref, f32[256,1536]{1,0:T(8,128)} %get-tuple-element.91.residual_ref.values_ref, ...), custom_call_target="tpu_custom_call" | custom-call | flops 70000001024 | bytes 31457280 | tf_op jit(solution)/shard_map/mlp_backward/pallas_call | solution.py:620
  671.4 1.8 slice.766
  673.2 92.1 %rec_backward_exchange.1 = (f32[256,1536]{1,0:T(8,128)}, bf16[256,1536]{1,0:T(8,128)(2,1)}, f32[1,1536]{1,0:T(1,128)}, bf16[4,640,512]{2,1,0:T(8,128)(2,1)}, f32...) custom-call(bf16[256,1536]{1,0:T(8,128)(2,1)} %get-tuple-element.119.g_re, ...), custom_call_target="tpu_custom_call" | custom-call | flops 80000000000 | bytes 31457280 | tf_op jit(solution)/shard_map/rec_backward_exchange/pallas_call | solution.py:1166
  778.3 16.3 %closing.1 = (f32[4,1536]{1,0:T(4,128)S(1)}, f32[16,256]{1,0:T(8,128)S(1)}, bf16[8,48,1152]{2,1,0:T(8,128)(2,1)S(1)}, bf16[192,1152]{1,0:T(8,128)(2,1)S(1)}) custom-call(f32[4,1536]{1,0:T(4,128)S(1)} %pad_maximum_fusion.2.gain_ref, f32[16,256]{1,0:T(8,128)S(1)} %pad_maximum_fusion.3.channel_ref, bf16[192,1152]{1,0:T(8,128)(2,1)S(1)} %slice.772.refs_0_, ...), custom_call_target="tpu_custom_call" | custom-call | flops 40000000000 | bytes 10485760 | tf_op jit(solution)/shard_map/closing/pallas_call | solution.py:1433
  803.2 28.7 %reduce-scatter.11.cloned.1.call-done = bf16[1,640,512]{2,1,0:T(8,128)(2,1)} async-done(((bf16[4,640,512]{2,1,0:T(8,128)(2,1)}), bf16[1,640,512]{2,1,0:T(8,128)(2,1)}) %reduce-scatter.11.cloned.1.call-update) | async-done | bytes 655376 | tf_op jit(solution)/shard_map/reduce_scatter | solution.py:1481
  831.8 1.8 slice.951
  833.6 3.5 all-to-all-start
  840.4 5.0 all-to-all-done
  847.1 2.0 maximum_convert_fusion.3
  849.1 1.9 maximum_convert_fusion.4
  850.9 2.7 copy.59
  (172 shorter events, 51.9 us)
Async XLA Ops:
  7.2 10.1 %copy-start.30 = (bf16[2,512]{1,0:T(2,128)(2,1)S(1)}, bf16[2,512]{1,0:T(2,128)(2,1)}, u32[]{:S(2)}) copy-start(bf16[2,512]{1,0:T(2,128)(2,1)} %param.25) | copy-start | bytes 6148
  7.2 10.1 %copy-start.31 = (bf16[2,512]{1,0:T(2,128)(2,1)S(1)}, bf16[2,512]{1,0:T(2,128)(2,1)}, u32[]{:S(2)}) copy-start(bf16[2,512]{1,0:T(2,128)(2,1)} %param.29) | copy-start | bytes 6148
  7.2 10.1 %copy-start.29 = (bf16[2,2,384]{2,1,0:T(2,128)(2,1)S(1)}, bf16[2,2,384]{2,1,0:T(2,128)(2,1)}, u32[]{:S(2)}) copy-start(bf16[2,2,384]{2,1,0:T(2,128)(2,1)} %param.21) | copy-start | bytes 9220
  7.2 198.1 %all-gather.7.cloned.1.call-start = ((), (), s32[]{:S(2)}) async-start(), calls=%async_computation.9 | async-start | bytes 6635520 | tf_op jit(solution)/shard_map/all_gather | solution.py:1597
  10.6 20.4 %collective-permute-start = (bf16[256,512]{1,0:T(8,128)(2,1)}, bf16[256,512]{1,0:T(8,128)(2,1)}, u32[]{:S(2)}, u32[]{:S(2)}) collective-permute-start(bf16[256,512]{1,0:T(8,128)(2,1)} %maximum_maximum_fusion.2), channel_id=1, source_target_pairs={{0,0},{1,8},{2,16},{3,24},{4,1},{5,9},{6,17},{7,25},{8,2},{9,10},{... | collective-permute-start | bytes 786440 | tf_op jit(solution)/shard_map/ppermute | solution.py:52
  15.3 6.4 copy-start.23
  15.3 6.4 copy-start.28
  95.7 175.8 %all-gather.9.cloned.1.call-start = ((), (), s32[]{:S(2)}) async-start(), calls=%async_computation.10 | async-start | bytes 3276800 | tf_op jit(solution)/shard_map/all_gather | solution.py:1606
  97.2 63.1 %copy-start.18 = (f32[2,8,2048]{2,1,0:T(8,128)}, f32[2,8,2048]{2,1,0:T(8,128)S(1)}, u32[]{:S(2)}) copy-start(f32[2,8,2048]{2,1,0:T(8,128)S(1)} %reshape.1868) | copy-start | bytes 393220
  162.7 11.9 %collective-permute-start.1 = (bf16[256,512]{1,0:T(8,128)(2,1)}, bf16[256,512]{1,0:T(8,128)(2,1)}, u32[]{:S(2)}, u32[]{:S(2)}) collective-permute-start(bf16[256,512]{1,0:T(8,128)(2,1)} %maximum_maximum_fusion.3), channel_id=1, source_target_pairs={{0,0},{1,8},{2,16},{3,24},{4,1},{5,9},{6,17},{7,25},{8,2},{9,10},{... | collective-permute-start | bytes 786440 | tf_op jit(solution)/shard_map/ppermute | solution.py:52
  173.4 3.1 copy-start.12
  176.5 186.2 %all-gather.11.cloned.1.call-start = ((), (), s32[]{:S(2)}) async-start(), calls=%async_computation.11 | async-start | bytes 6635520 | tf_op jit(solution)/shard_map/all_gather | solution.py:1597
  179.5 416.4 %reduce-scatter.5.cloned.1.call-start = ((), (), s32[]{:S(2)}) async-start(), calls=%async_computation.5 | async-start | bytes 6635520 | tf_op jit(solution)/shard_map/reduce_scatter | solution.py:1481
  499.7 171.7 %reduce-scatter.7.cloned.1.call-start = ((), (), s32[]{:S(2)}) async-start(), calls=%async_computation.6 | async-start | bytes 3276800 | tf_op jit(solution)/shard_map/reduce_scatter | solution.py:1481
  595.9 180.1 %reduce-scatter.9.cloned.1.call-start = ((), (), s32[]{:S(2)}) async-start(), calls=%async_computation.7 | async-start | bytes 6635520 | tf_op jit(solution)/shard_map/reduce_scatter | solution.py:1481
  667.3 164.5 %reduce-scatter.11.cloned.1.call-start = ((), (), s32[]{:S(2)}) async-start(), calls=%async_computation.8 | async-start | bytes 3276800 | tf_op jit(solution)/shard_map/reduce_scatter | solution.py:1481
  768.3 3.1 copy-start.21
  768.3 3.0 copy-start.22
  768.3 3.9 copy-start.13
  768.5 4.3 copy-start.24
  768.5 4.3 copy-start.25
  768.5 4.3 copy-start.26
  768.6 4.3 copy-start.27
  801.8 36.2 %copy-start.20 = (bf16[1,64,256]{2,1,0:T(8,128)(2,1)S(1)}, bf16[1,64,256]{2,1,0:T(8,128)(2,1)}, u32[]{:S(2)}) copy-start(bf16[1,64,256]{2,1,0:T(8,128)(2,1)} %get-tuple-element.298) | copy-start | bytes 98308
  801.8 36.9 %copy-start.19 = (bf16[1,64,256]{2,1,0:T(8,128)(2,1)S(1)}, bf16[1,64,256]{2,1,0:T(8,128)(2,1)}, u32[]{:S(2)}) copy-start(bf16[1,64,256]{2,1,0:T(8,128)(2,1)} %get-tuple-element.299) | copy-start | bytes 98308
  801.8 37.6 %copy-start.15 = (bf16[1,64,512]{2,1,0:T(8,128)(2,1)S(1)}, bf16[1,64,512]{2,1,0:T(8,128)(2,1)}, u32[]{:S(2)}) copy-start(bf16[1,64,512]{2,1,0:T(8,128)(2,1)} %get-tuple-element.295) | copy-start | bytes 196612
  801.8 37.6 %copy-start.16 = (bf16[1,64,512]{2,1,0:T(8,128)(2,1)S(1)}, bf16[1,64,512]{2,1,0:T(8,128)(2,1)}, u32[]{:S(2)}) copy-start(bf16[1,64,512]{2,1,0:T(8,128)(2,1)} %get-tuple-element.296) | copy-start | bytes 196612
  801.8 37.6 %copy-start.17 = (bf16[1,64,512]{2,1,0:T(8,128)(2,1)S(1)}, bf16[1,64,512]{2,1,0:T(8,128)(2,1)}, u32[]{:S(2)}) copy-start(bf16[1,64,512]{2,1,0:T(8,128)(2,1)} %get-tuple-element.297) | copy-start | bytes 196612
  833.6 11.7 %all-to-all-start = ((bf16[8,48,512]{2,1,0:T(8,128)(2,1)}), bf16[8,48,512]{2,1,0:T(8,128)(2,1)S(1)}, u32[]{:S(2)}, u32[]{:S(2)}) async-start(bf16[8,48,512]{2,1,0:T(8,128)(2,1)} %bitcast.66), calls=%async_computation.4 | async-start | bytes 786432 | tf_op jit(solution)/shard_map/all_to_all | solution.py:1636
  838.0 9.0 %copy-start.11 = (bf16[1,48,2048]{2,1,0:T(8,128)(2,1)S(1)}, bf16[1,48,2048]{2,1,0:T(8,128)(2,1)}, u32[]{:S(2)}) copy-start(bf16[1,48,2048]{2,1,0:T(8,128)(2,1)} %convert_element_type.165) | copy-start | bytes 589828
  839.4 9.7 %copy-start.10 = (bf16[1,48,2048]{2,1,0:T(8,128)(2,1)S(1)}, bf16[1,48,2048]{2,1,0:T(8,128)(2,1)}, u32[]{:S(2)}) copy-start(bf16[1,48,2048]{2,1,0:T(8,128)(2,1)} %convert_element_type.169) | copy-start | bytes 589828
  847.1 6.5 copy-start.1
  (10 other events, 22.1 us)
Sparse Core Ops, SparseCore 0:
  95.8 109.4 all-gather.6
  207.5 53.5 all-gather.8
  263.3 99.3 all-gather.10
  499.8 95.9 reduce-scatter.4
  598.1 52.5 reduce-scatter.6
  667.4 96.7 reduce-scatter.8
  778.4 53.4 reduce-scatter.10
